TPU v7x, 32 devices: a whole 2x2x4 slice. The times are simulated.
32 devices in a mesh: img: 8 (over z, core), mp: 4 (over y, x).
Axes of the slice: x: 2, y: 2, z: 4, core: 2. Of those that a mesh axis runs over, the one named last changes fastest.
Arguments:
- tokens: bfloat16 [6144, 2048], P('img'), may hold values from -6 to 6
- caption: bfloat16 [3072, 4096], P('img'), may hold values from -6 to 6
- masked: int32 [24, 256], P('img'), may hold values from 0 to 1, as said below
- out_grad: bfloat16 [6144, 2048], P('img'), may hold values from -6 to 6
- mask_embed: bfloat16 [2048], replicated, may hold values from -6 to 6
- norm_gains: float32 [3, 2048], replicated, may hold values from 0.25 to 1.75
- attention_in: bfloat16 [2048, 3, 2048], P(None, None, 'mp'), may hold values from -0.125 to 0.125
- attention_out: bfloat16 [2048, 2048], P('mp'), may hold values from -0.5 to 0.5
- cross_query: bfloat16 [2048, 2048], P(None, 'mp'), may hold values from -0.125 to 0.125
- cross_text: bfloat16 [4096, 2, 2048], P(None, None, 'mp'), may hold values from -0.09375 to 0.09375
- cross_out: bfloat16 [2048, 2048], P('mp'), may hold values from -0.375 to 0.375
- feed_expand: bfloat16 [2048, 8192], P(None, 'mp'), may hold values from -0.125 to 0.125
- feed_shrink: bfloat16 [8192, 2048], P('mp'), may hold values from -0.0625 to 0.0625
Outputs:
- mixed_out: bfloat16 [6144, 2048], P(('img', 'mp'))
- tokens_grad: float32 [6144, 2048], P(('img', 'mp'))
- caption_grad: float32 [3072, 4096], P('img', 'mp')
- embed_grad: float32 [2048], P(('img', 'mp'))
- gains_grad: float32 [3, 2048], P(None, ('img', 'mp'))
- grad_attention_in: float32 [2048, 3, 2048], P('img', None, 'mp')
- grad_attention_out: float32 [2048, 2048], P('mp', 'img')
- grad_cross_query: float32 [2048, 2048], P('img', 'mp')
- grad_cross_text: float32 [4096, 2, 2048], P('img', None, 'mp')
- grad_cross_out: float32 [2048, 2048], P('mp', 'img')
- grad_feed_expand: float32 [2048, 8192], P('img', 'mp')
- grad_feed_shrink: float32 [8192, 2048], P('mp', 'img')
Inputs may be any that keep to these rules, and one draw needn't show every extreme that they name: 1 marks a masked token. Each image masks 256 // k of its tokens for a whole k of 1 to 8, at positions drawn afresh; in every draw one image masks all 256 and one masks 256 // 8.
All inputs are finite; a program needn't handle non-finite values.
Results may differ from a plain program's by a relative error of at most 0.02.
Values may be sent and summed in bfloat16 or wider, within the bound.
A program may use at most 384 MiB of HBM per device.

v0:
```python
import math

import jax
import jax.numpy as jnp
from jax import lax
from jax.sharding import PartitionSpec as P

HDIM = 128


EPSILON = 1e-05


def times(left, right):
    return jnp.dot(left, right, preferred_element_type=jnp.float32)


def inner_rows(left, right):
    return lax.dot_general(
        left, right, (((0,), (0,)), ((), ())), preferred_element_type=jnp.float32
    )


def times_transposed(left, right):
    return lax.dot_general(
        left, right, (((1,), (1,)), ((), ())), preferred_element_type=jnp.float32
    )


def norm_parts(rows_in):
    centre = rows_in - jnp.mean(rows_in, axis=-1, keepdims=True)
    root_inverse = lax.rsqrt(jnp.mean(centre * centre, axis=-1, keepdims=True) + EPSILON)
    return (centre * root_inverse, root_inverse)


def norm_back(grad_rows, unit_rows, root_inverse, gain_row):
    weighted = grad_rows * gain_row
    middle = jnp.mean(weighted, axis=-1, keepdims=True)
    along = jnp.mean(weighted * unit_rows, axis=-1, keepdims=True)
    return root_inverse * (weighted - middle - unit_rows * along)


def score_block(queries, keys_in):
    raw_scores = jnp.einsum("bqhe,bkhe->bhqk", queries, keys_in, preferred_element_type=jnp.float32)
    return raw_scores * (1.0 / math.sqrt(queries.shape[-1]))


def attend_forward(queries, keys_in, values_in):
    scores = score_block(queries, keys_in)
    row_max = jnp.max(scores, axis=-1, keepdims=True)
    log_total = row_max + jnp.log(jnp.sum(jnp.exp(scores - row_max), axis=-1, keepdims=True))
    probs_low = jnp.exp(scores - log_total).astype(jnp.bfloat16)
    mixed_heads = jnp.einsum(
        "bhqk,bkhe->bqhe", probs_low, values_in, preferred_element_type=jnp.float32
    )
    return (mixed_heads.astype(jnp.bfloat16), log_total)


def attend_backward(queries, keys_in, values_in, log_total, grad_mixed):
    probs = jnp.exp(score_block(queries, keys_in) - log_total)
    grad_values = jnp.einsum(
        "bhqk,bqhe->bkhe",
        probs.astype(jnp.bfloat16),
        grad_mixed,
        preferred_element_type=jnp.float32,
    )
    grad_probs = jnp.einsum(
        "bqhe,bkhe->bhqk", grad_mixed, values_in, preferred_element_type=jnp.float32
    )
    centred = grad_probs - jnp.sum(probs * grad_probs, axis=-1, keepdims=True)
    grad_scores = (probs * centred * (1.0 / math.sqrt(queries.shape[-1]))).astype(jnp.bfloat16)
    grad_queries = jnp.einsum(
        "bhqk,bkhe->bqhe", grad_scores, keys_in, preferred_element_type=jnp.float32
    )
    grad_keys = jnp.einsum(
        "bhqk,bqhe->bkhe", grad_scores, queries, preferred_element_type=jnp.float32
    )
    return (grad_queries, grad_keys, grad_values)


def gelu_exact(values_in):
    return jax.nn.gelu(values_in, approximate=False)


def reduce_branch(partial_rows):
    return lax.psum(partial_rows, "mp")


def reduce_grad(partial_rows):
    return lax.psum(partial_rows, "mp")


def body(
    tokens,
    caption,
    masked,
    out_grad,
    mask_embed,
    norm_gains,
    attention_in,
    attention_out,
    cross_query,
    cross_text,
    cross_out,
    feed_expand,
    feed_shrink,
):
    axis_count = lax.axis_size("mp")
    axis_place = lax.axis_index("mp")
    images = masked.shape[0]
    length = masked.shape[1]
    rows_all = images * length
    share_rows = rows_all // axis_count
    model_width = tokens.shape[1]
    text_width = caption.shape[1]
    text_rows = caption.shape[0] // images
    heads_here = attention_in.shape[2] // HDIM

    def own_rows(rows_in):
        return lax.dynamic_slice_in_dim(rows_in, axis_place * share_rows, share_rows, 0)

    def share_of(rows_in):
        return own_rows(rows_in)

    mask_flat = masked.reshape(rows_all) > 0
    mask_float = mask_flat.astype(jnp.float32)
    entry_full = jnp.where(
        mask_flat[:, None], mask_embed.astype(jnp.float32)[None, :], tokens.astype(jnp.float32)
    )
    cotangent = out_grad.astype(jnp.float32) * mask_float[:, None]
    first_unit, first_root = norm_parts(entry_full)
    first_normed = (first_unit * norm_gains[0]).astype(jnp.bfloat16)
    projected = times(first_normed, attention_in.reshape(model_width, -1)).astype(jnp.bfloat16)
    projected = projected.reshape(images, length, 3, heads_here, HDIM)
    self_mixed, self_total = attend_forward(
        projected[:, :, 0], projected[:, :, 1], projected[:, :, 2]
    )
    self_mixed = self_mixed.reshape(rows_all, -1)
    after_self = entry_full + reduce_branch(times(self_mixed, attention_out))
    second_unit, second_root = norm_parts(after_self)
    second_normed = (second_unit * norm_gains[1]).astype(jnp.bfloat16)
    cross_queries = (
        times(second_normed, cross_query)
        .astype(jnp.bfloat16)
        .reshape(images, length, heads_here, HDIM)
    )
    text_pairs = times(caption, cross_text.reshape(text_width, -1)).astype(jnp.bfloat16)
    text_pairs = text_pairs.reshape(images, text_rows, 2, heads_here, HDIM)
    cross_mixed, cross_total = attend_forward(
        cross_queries, text_pairs[:, :, 0], text_pairs[:, :, 1]
    )
    cross_mixed = cross_mixed.reshape(rows_all, -1)
    after_cross = after_self + reduce_branch(times(cross_mixed, cross_out))
    third_unit, third_root = norm_parts(after_cross)
    third_normed = (third_unit * norm_gains[2]).astype(jnp.bfloat16)
    hidden = times(third_normed, feed_expand)
    active = gelu_exact(hidden).astype(jnp.bfloat16)
    final_rows = after_cross + reduce_branch(times(active, feed_shrink))
    mixed_out = share_of(final_rows).astype(jnp.bfloat16)
    feed_grad = cotangent.astype(jnp.bfloat16)
    shrink_sum = inner_rows(active, feed_grad)
    grad_active = times_transposed(feed_grad, feed_shrink)
    gelu_value, gelu_pull = jax.vjp(gelu_exact, hidden)
    grad_hidden = gelu_pull(grad_active)[0].astype(jnp.bfloat16)
    expand_sum = inner_rows(third_normed, grad_hidden)
    third_grad = reduce_grad(times_transposed(grad_hidden, feed_expand))
    before_feed = cotangent + norm_back(third_grad, third_unit, third_root, norm_gains[2])
    third_gain = jnp.sum(share_of(third_grad * third_unit), axis=0)
    cross_grad = before_feed.astype(jnp.bfloat16)
    cross_out_sum = inner_rows(cross_mixed, cross_grad)
    grad_cross_mixed = times_transposed(cross_grad, cross_out).astype(jnp.bfloat16)
    grad_cross_mixed = grad_cross_mixed.reshape(images, length, heads_here, HDIM)
    grad_cross_queries, grad_text_keys, grad_text_values = attend_backward(
        cross_queries, text_pairs[:, :, 0], text_pairs[:, :, 1], cross_total, grad_cross_mixed
    )
    grad_cross_queries = grad_cross_queries.astype(jnp.bfloat16).reshape(rows_all, -1)
    grad_text_pairs = jnp.stack([grad_text_keys, grad_text_values], axis=2).astype(jnp.bfloat16)
    grad_text_pairs = grad_text_pairs.reshape(images * text_rows, -1)
    cross_query_sum = inner_rows(second_normed, grad_cross_queries)
    cross_text_sum = inner_rows(caption, grad_text_pairs).reshape(text_width, 2, -1)
    caption_grad = lax.psum_scatter(
        times_transposed(grad_text_pairs, cross_text.reshape(text_width, -1)).astype(jnp.bfloat16),
        "mp",
        scatter_dimension=1,
        tiled=True,
    ).astype(jnp.float32)
    second_grad = reduce_grad(times_transposed(grad_cross_queries, cross_query))
    before_cross = before_feed + norm_back(second_grad, second_unit, second_root, norm_gains[1])
    second_gain = jnp.sum(share_of(second_grad * second_unit), axis=0)
    self_grad = before_cross.astype(jnp.bfloat16)
    self_out_sum = inner_rows(self_mixed, self_grad)
    grad_self_mixed = times_transposed(self_grad, attention_out).astype(jnp.bfloat16)
    grad_self_mixed = grad_self_mixed.reshape(images, length, heads_here, HDIM)
    grad_queries, grad_keys, grad_values = attend_backward(
        projected[:, :, 0], projected[:, :, 1], projected[:, :, 2], self_total, grad_self_mixed
    )
    grad_projected = jnp.stack([grad_queries, grad_keys, grad_values], axis=2).astype(jnp.bfloat16)
    grad_projected = grad_projected.reshape(rows_all, -1)
    self_in_sum = inner_rows(first_normed, grad_projected).reshape(model_width, 3, -1)
    first_grad = reduce_grad(
        times_transposed(grad_projected, attention_in.reshape(model_width, -1))
    )
    entry_grad = before_cross + norm_back(first_grad, first_unit, first_root, norm_gains[0])
    first_gain = jnp.sum(share_of(first_grad * first_unit), axis=0)
    entry_share = share_of(entry_grad)
    own_mask = own_rows(mask_float)[:, None]
    tokens_grad = entry_share * (1.0 - own_mask)
    embed_term = jnp.sum(entry_share * own_mask, axis=0)
    small_terms = jnp.stack([first_gain, second_gain, third_gain, embed_term], axis=0)
    small_sums = lax.psum_scatter(small_terms, ("img", "mp"), scatter_dimension=1, tiled=True)
    weight_sums = (
        lax.psum_scatter(
            self_in_sum.astype(jnp.bfloat16), "img", scatter_dimension=0, tiled=True
        ).astype(jnp.float32),
        lax.psum_scatter(
            self_out_sum.astype(jnp.bfloat16), "img", scatter_dimension=1, tiled=True
        ).astype(jnp.float32),
        lax.psum_scatter(
            cross_query_sum.astype(jnp.bfloat16), "img", scatter_dimension=0, tiled=True
        ).astype(jnp.float32),
        lax.psum_scatter(
            cross_text_sum.astype(jnp.bfloat16), "img", scatter_dimension=0, tiled=True
        ).astype(jnp.float32),
        lax.psum_scatter(
            cross_out_sum.astype(jnp.bfloat16), "img", scatter_dimension=1, tiled=True
        ).astype(jnp.float32),
        lax.psum_scatter(
            expand_sum.astype(jnp.bfloat16), "img", scatter_dimension=0, tiled=True
        ).astype(jnp.float32),
        lax.psum_scatter(
            shrink_sum.astype(jnp.bfloat16), "img", scatter_dimension=1, tiled=True
        ).astype(jnp.float32),
    )
    return (
        mixed_out,
        tokens_grad,
        caption_grad,
        small_sums[3],
        small_sums[0:3],
        weight_sums[0],
        weight_sums[1],
        weight_sums[2],
        weight_sums[3],
        weight_sums[4],
        weight_sums[5],
        weight_sums[6],
    )


def solution(mesh):
    return jax.shard_map(
        body,
        mesh=mesh,
        in_specs=(
            P("img", None),
            P("img", None),
            P("img", None),
            P("img", None),
            P(),
            P(),
            P(None, None, "mp"),
            P("mp", None),
            P(None, "mp"),
            P(None, None, "mp"),
            P("mp", None),
            P(None, "mp"),
            P("mp", None),
        ),
        out_specs=(
            P(("img", "mp"), None),
            P(("img", "mp"), None),
            P("img", "mp"),
            P(("img", "mp")),
            P(None, ("img", "mp")),
            P("img", None, "mp"),
            P("mp", "img"),
            P("img", "mp"),
            P("img", None, "mp"),
            P("mp", "img"),
            P("img", "mp"),
            P("mp", "img"),
        ),
        check_vma=False,
    )
```

profile of v0, /device:TPU:0, one launch (start us, length us, event | category | flops | bytes accessed | tf_op | source)
XLA Modules:
  0.0 1729.3 jit_solution(14395064071293846210)
XLA Ops:
  15.1 8.8 copy.84
  23.9 9.9 convolution_convert_fusion.5
  33.8 5.2 reshape.177
  52.9 6.3 fusion.84
  59.5 9.9 copy.142
  69.4 6.8 convolution_convert_fusion.11
  82.4 118.2 %all-reduce.9.cloned.1.call-done = f32[768,2048]{1,0:T(8,128)} async-done(((f32[768,2048]{1,0:T(8,128)}), f32[768,2048]{1,0:T(8,128)}) %all-reduce.9.cloned.1.call-update) | async-done | bytes 6291472 | tf_op jit(solution)/shard_map/psum | solution.py:86
  200.6 4.8 fusion.122
  227.1 6.3 fusion.81
  234.0 138.0 %all-reduce.11.cloned.1.call-done = f32[768,2048]{1,0:T(8,128)} async-done(((f32[768,2048]{1,0:T(8,128)}), f32[768,2048]{1,0:T(8,128)}) %all-reduce.11.cloned.1.call-update) | async-done | bytes 6291472 | tf_op jit(solution)/shard_map/psum | solution.py:86
  372.0 6.7 fusion.127
  386.7 21.8 %multiply_convert_fusion = (bf16[768,2048]{1,0:T(8,128)(2,1)}, f32[768,2048]{1,0:T(8,128)}, f32[768,2048]{1,0:T(8,128)}) fusion(bf16[2048,2048]{1,0:T(8,128)(2,1)S(1)} %bitcast.162, f32[768,2048]{1,0:T(8,128)S(1)} %subtract_multiply_fusion, f32[2048]{0:T(1024)S(1)} %bitcast.145), kind=kOutput, calls=%fused_computation.15 | convolution fusion | flops 6547832832 | bytes 30416896 | tf_op jit(solution)/shard_map/dot_general | solution.py:15
  408.6 15.1 add_convert_fusion
  423.7 11.9 fusion.134
  435.7 138.6 %all-reduce.13.cloned.1.call-done = f32[768,2048]{1,0:T(8,128)} async-done(((f32[768,2048]{1,0:T(8,128)}), f32[768,2048]{1,0:T(8,128)}) %all-reduce.13.cloned.1.call-update) | async-done | bytes 6291472 | tf_op jit(solution)/shard_map/psum | solution.py:90
  574.2 5.7 multiply_reduce_fusion.7
  581.6 5.1 multiply_add_fusion.1
  599.4 4.8 fusion.64
  606.4 6.3 fusion.78
  612.8 6.3 convolution_convert_fusion.6
  619.1 6.1 convolution_convert_fusion.7
  625.6 4.3 fusion.67
  637.7 7.9 convolution_convert_fusion.2
  645.6 21.3 %copy.116 = bf16[4096,2,512]{2,1,0:T(2,128)(2,1)} copy(bf16[4096,2,512]{0,2,1:T(8,128)(2,1)} %bitcast.132) | data formatting | bytes 16777216 | tf_op jit(solution)/shard_map/convert_element_type | solution.py:222
  668.0 10.4 convolution_convert_fusion.3
  678.5 12.0 convolution_convert_fusion.1
  691.0 60.3 %all-reduce.15.cloned.1.call-done = f32[768,2048]{1,0:T(8,128)} async-done(((f32[768,2048]{1,0:T(8,128)}), f32[768,2048]{1,0:T(8,128)}) %all-reduce.15.cloned.1.call-update) | async-done | bytes 6291472 | tf_op jit(solution)/shard_map/psum | solution.py:90
  751.3 5.9 multiply_reduce_fusion.6
  757.7 5.8 multiply_add_fusion
  769.4 11.1 convolution_convert_fusion
  780.8 11.9 fusion.133
  792.6 5.5 fusion.59
  806.6 5.6 fusion.46
  812.2 5.7 fusion.49
  824.8 4.0 convert_element_type.201
  828.8 10.5 fusion.135
  839.4 4.4 copy.114
  843.9 9.6 convolution_convert_fusion.4
  861.2 142.5 %all-reduce.17.cloned.1.call-done = bf16[4096,2,512]{2,1,0:T(2,128)(2,1)} async-done(((bf16[4096,2,512]{2,1,0:T(2,128)(2,1)}), bf16[4096,2,512]{2,1,0:T(2,128)(2,1)}) %all-reduce.17.cloned.1.call-update) | async-done | bytes 8388624
  1006.9 43.8 %reduce-scatter.11.cloned.1.call-done = bf16[384,1024]{1,0:T(8,128)(2,1)} async-done(((bf16[384,4096]{1,0:T(8,128)(2,1)}), bf16[384,1024]{1,0:T(8,128)(2,1)}) %reduce-scatter.11.cloned.1.call-update) | async-done | bytes 786448 | tf_op jit(solution)/shard_map/reduce_scatter | solution.py:181
  1055.2 87.4 %reduce-scatter.21.cloned.1.call-done = bf16[256,2048]{1,0:T(8,128)(2,1)} async-done(((bf16[2048,2048]{1,0:T(8,128)(2,1)}), bf16[256,2048]{1,0:T(8,128)(2,1)}) %reduce-scatter.21.cloned.1.call-update) | async-done | bytes 1048592 | tf_op jit(solution)/shard_map/reduce_scatter | solution.py:227
  1145.4 34.1 %reduce-scatter.15.cloned.1.call-done = bf16[512,256]{1,0:T(8,128)(2,1)} async-done(((bf16[512,2048]{1,0:T(8,128)(2,1)}), bf16[512,256]{1,0:T(8,128)(2,1)}) %reduce-scatter.15.cloned.1.call-update) | async-done | bytes 262160 | tf_op jit(solution)/shard_map/reduce_scatter | solution.py:215
  1181.4 88.7 %reduce-scatter.23.cloned.1.call-done = bf16[2048,256]{1,0:T(8,128)(2,1)} async-done(((bf16[2048,2048]{1,0:T(8,128)(2,1)}), bf16[2048,256]{1,0:T(8,128)(2,1)}) %reduce-scatter.23.cloned.1.call-update) | async-done | bytes 1048592 | tf_op jit(solution)/shard_map/reduce_scatter | solution.py:230
  1272.8 239.5 %all-reduce.19.cloned.1.call-done = (f32[768,2048]{1,0:T(8,128)}, f32[768,2048]{1,0:T(8,128)}) async-done(((f32[768,2048]{1,0:T(8,128)}, f32[768,2048]{1,0:T(8,128)}), (f32[768,2048]{1,0:T(8,128)}, f32[768,2048]{1,0:T(8,128)})) %all-reduce.19.cloned.1.call-update) | async-done | bytes 12582928 | tf_op jit(solution)/shard_map/psum | solution.py:86
  1512.3 4.4 fusion.125
  1516.8 3.9 multiply_reduce_fusion.10
  1527.8 56.6 %reduce-scatter.13.cloned.1.call-done = bf16[256,3,512]{2,0,1:T(8,128)(2,1)} async-done(((bf16[2048,3,512]{2,0,1:T(8,128)(2,1)}), bf16[256,3,512]{2,0,1:T(8,128)(2,1)}) %reduce-scatter.13.cloned.1.call-update) | async-done | bytes 786448 | tf_op jit(solution)/shard_map/reduce_scatter | solution.py:212
  1586.9 132.8 %reduce-scatter.25.cloned.1.call-done = f32[64,4]{1,0:T(8,128)} async-done(((f32[2048,4]{1,0:T(8,128)}), f32[64,4]{1,0:T(8,128)}) %reduce-scatter.25.cloned.1.call-update) | async-done | bytes 1040
  (215 shorter events, 141.5 us)
Async XLA Ops:
  7.2 62.2 %copy-start = (bf16[384,4096]{1,0:T(8,128)(2,1)S(1)}, bf16[384,4096]{1,0:T(8,128)(2,1)}, u32[]{:S(2)}) copy-start(bf16[384,4096]{1,0:T(8,128)(2,1)} %param.14) | copy-start | bytes 9437188
  7.2 7.2 copy-start.49
  7.2 193.3 %all-reduce.9.cloned.1.call-start = ((), (), s32[]{:S(2)}) async-start(), calls=%async_computation.8 | async-start | bytes 12582912 | tf_op jit(solution)/shard_map/psum | solution.py:86
  8.1 363.9 %copy-start.31 = (pred[768]{0:T(1024)(128)(4,1)}, pred[768]{0:T(1024)(128)(4,1)S(1)}, u32[]{:S(2)}) copy-start(pred[768]{0:T(1024)(128)(4,1)S(1)} %gt.18) | copy-start | bytes 2308
  8.9 363.1 %copy-start.25 = (f32[2048]{0:T(1024)}, f32[2048]{0:T(1024)S(1)}, u32[]{:S(2)}) copy-start(f32[2048]{0:T(1024)S(1)} %convert_element_type.172) | copy-start | bytes 24580
  11.5 12.4 copy-start.40
  14.4 9.4 copy-start.47
  15.1 8.8 copy-start.42
  59.3 312.7 %all-reduce.11.cloned.1.call-start = ((), (), s32[]{:S(2)}) async-start(), calls=%async_computation.9 | async-start | bytes 12582912 | tf_op jit(solution)/shard_map/psum | solution.py:86
  200.5 4.8 copy-start.3
  200.5 6.5 copy-start.5
  233.4 340.9 %all-reduce.13.cloned.1.call-start = ((), (), s32[]{:S(2)}) async-start(), calls=%async_computation.10 | async-start | bytes 12582912 | tf_op jit(solution)/shard_map/psum | solution.py:90
  378.7 5.3 slice-start
  379.5 7.2 slice-start.1
  381.9 26.7 %copy-start.14 = (f32[768,2048]{1,0:T(8,128)}, f32[768,2048]{1,0:T(8,128)S(1)}, u32[]{:S(2)}) copy-start(f32[768,2048]{1,0:T(8,128)S(1)} %subtract_multiply_fusion) | copy-start | bytes 18874372
  386.7 21.8 %copy-start.17 = (bf16[768,2048]{1,0:T(8,128)(2,1)S(1)}, bf16[768,2048]{1,0:T(8,128)(2,1)}, u32[]{:S(2)}) copy-start(bf16[768,2048]{1,0:T(8,128)(2,1)} %param.16) | copy-start | bytes 9437188
  386.7 21.8 %copy-start.44 = (f32[768]{0:T(1024)S(1)}, f32[768]{0:T(1024)}, u32[]{:S(2)}) copy-start(f32[768]{0:T(1024)} %convert_element_type.189) | copy-start | bytes 9220
  435.6 315.7 %all-reduce.15.cloned.1.call-start = ((), (), s32[]{:S(2)}) async-start(), calls=%async_computation.11 | async-start | bytes 12582912 | tf_op jit(solution)/shard_map/psum | solution.py:90
  574.2 6.4 copy-start.9
  574.2 7.3 copy-start.18
  574.2 7.4 copy-start.45
  581.6 7.8 copy-start.21
  589.4 10.0 copy-start.28
  612.7 6.4 copy-start.36
  612.7 244.9 %reduce-scatter.19.cloned.1.call-start = ((), (), s32[]{:S(2)}) async-start(), calls=%async_computation.16 | async-start | bytes 2359296 | tf_op jit(solution)/shard_map/reduce_scatter | solution.py:224
  619.1 240.3 %reduce-scatter.17.cloned.1.call-start = ((), (), s32[]{:S(2)}) async-start(), calls=%async_computation.15 | async-start | bytes 2359296 | tf_op jit(solution)/shard_map/reduce_scatter | solution.py:218
  625.3 378.4 %all-reduce.17.cloned.1.call-start = ((), (), s32[]{:S(2)}) async-start(), calls=%async_computation.20 | async-start | bytes 16777216
  666.9 11.6 copy-start.34
  666.9 383.8 %reduce-scatter.11.cloned.1.call-start = ((), (), s32[]{:S(2)}) async-start(), calls=%async_computation.12 | async-start | bytes 3932160 | tf_op jit(solution)/shard_map/reduce_scatter | solution.py:181
  678.5 464.2 %reduce-scatter.21.cloned.1.call-start = ((), (), s32[]{:S(2)}) async-start(), calls=%async_computation.17 | async-start | bytes 9437184 | tf_op jit(solution)/shard_map/reduce_scatter | solution.py:227
  690.5 60.8 %copy-start.37 = (f32[1,2048]{1,0:T(1,128)S(1)}, f32[1,2048]{1,0:T(1,128)}, u32[]{:S(2)}) copy-start(f32[1,2048]{1,0:T(1,128)} %get-tuple-element.38) | copy-start | bytes 24580
  690.6 66.6 %copy-start.39 = (f32[768]{0:T(1024)S(1)}, f32[768]{0:T(1024)}, u32[]{:S(2)}) copy-start(f32[768]{0:T(1024)} %copy-done.38) | copy-start | bytes 9220
  690.6 489.0 %reduce-scatter.15.cloned.1.call-start = ((), (), s32[]{:S(2)}) async-start(), calls=%async_computation.14 | async-start | bytes 2359296 | tf_op jit(solution)/shard_map/reduce_scatter | solution.py:215
  751.3 6.4 copy-start.10
  757.7 8.4 copy-start.20
  769.3 500.7 %reduce-scatter.23.cloned.1.call-start = ((), (), s32[]{:S(2)}) async-start(), calls=%async_computation.18 | async-start | bytes 9437184 | tf_op jit(solution)/shard_map/reduce_scatter | solution.py:230
  780.5 12.1 copy-start.23
  780.6 731.7 %all-reduce.19.cloned.1.call-start = ((), (), s32[]{:S(2)}) async-start(), calls=%async_computation.21 | async-start | bytes 25165824 | tf_op jit(solution)/shard_map/psum | solution.py:86
  798.1 8.4 copy-start.8
  798.1 8.4 copy-start.30
  828.8 10.5 copy-start.15
  839.3 4.6 copy-start.4
  839.3 4.6 copy-start.26
  839.3 4.6 copy-start.32
  839.3 4.6 copy-start.41
  839.4 745.0 %reduce-scatter.13.cloned.1.call-start = ((), (), s32[]{:S(2)}) async-start(), calls=%async_computation.13 | async-start | bytes 7077888 | tf_op jit(solution)/shard_map/reduce_scatter | solution.py:212
  853.5 866.2 %reduce-scatter.25.cloned.1.call-start = ((), (), s32[]{:S(2)}) async-start(), calls=%async_computation.19 | async-start | bytes 1081344
  1516.8 205.7 %copy-start.1 = (bf16[384,4096]{1,0:T(8,128)(2,1)S(1)}, bf16[384,4096]{1,0:T(8,128)(2,1)}, u32[]{:S(2)}) copy-start(bf16[384,4096]{1,0:T(8,128)(2,1)} %param.14) | copy-start | bytes 9437188
  (19 other events, 51.2 us)
Sparse Core Ops, SparseCore 0:
  59.4 141.1 all-reduce.8
  233.5 138.4 all-reduce.10
  435.7 138.4 all-reduce.12
  612.8 138.4 all-reduce.14
  754.0 35.7 reduce-scatter.18
  792.6 34.4 reduce-scatter.16
  829.4 174.1 all-reduce.16
  1006.6 44.0 reduce-scatter.10
  1053.0 89.5 reduce-scatter.20
  1145.4 34.1 reduce-scatter.14
  1181.9 88.1 reduce-scatter.22
  1273.6 238.5 all-reduce.18
  1514.6 69.7 reduce-scatter.12
  1586.5 133.1 reduce-scatter.24
where the time goes:
time: 1740 us; the launch traced here: 1730 us
  waiting for transfers between devices  1280 us (74%)
  matrix products  222 us (13%)
  local copies, waits for them, and re-layouts  123 us (7%)
  other arithmetic  87 us (5%)
    psum x3, waiting for transfers between devices, reduce_branch(): return lax.psum(partial_rows, 'mp')  496 us
    unnamed x16, waiting for transfers between devices  276 us
    psum x2, waiting for transfers between devices, reduce_grad(): return lax.psum(partial_rows, 'mp')  199 us
    reduce_scatter x1, waiting for transfers between devices, body(): lax.psum_scatter(shrink_sum.astype(jnp.bfloat16), 'img', scatter_dimensio...  88.7 us
    reduce_scatter x1, waiting for transfers between devices, body(): lax.psum_scatter(expand_sum.astype(jnp.bfloat16), 'img', scatter_dimensio...  87.4 us
    dot_general x7, matrix products, times(): return jnp.dot(left, right, preferred_element_type=jnp.float32)  65.7 us
    dot_general x7, matrix products, times_transposed(): lax.dot_general(left, right, (((1,), (1,)), ((), ())), preferred_element_...  62.4 us
    reduce_scatter x1, waiting for transfers between devices, body(): lax.psum_scatter(self_in_sum.astype(jnp.bfloat16), 'img', scatter_dimensi...  56.6 us
  transfers between devices with their start and end apart: 14, of which 12 were waited for; matrix products, arithmetic and copies ran while one was open for 14% of the time, Pallas kernels for 0%

commit v1 on v0

v1 whole, which is shorter than its diff:
```python
import functools
import math

import jax
import jax.numpy as jnp
from jax import lax
from jax.experimental import pallas as pl
from jax.experimental.pallas import tpu as pltpu
from jax.sharding import PartitionSpec as P

HDIM = 128
EPSILON = 1e-05
SCALE = 1.0 / math.sqrt(HDIM)
VMEM_BYTES = 52 * 1024 * 1024
MESH = pl.DeviceIdType.MESH
BF16 = jnp.bfloat16
F32 = jnp.float32

NN = (((1,), (0,)), ((), ()))
NT = (((1,), (1,)), ((), ()))
TN = (((0,), (0,)), ((), ()))


def product(left, right, dims=NN):
    return lax.dot_general(left, right, dims, preferred_element_type=F32)


def norm_parts(rows_in):
    centre = rows_in - jnp.mean(rows_in, axis=-1, keepdims=True)
    root_inverse = lax.rsqrt(jnp.mean(centre * centre, axis=-1, keepdims=True) + EPSILON)
    return (centre * root_inverse, root_inverse)


def norm_back(grad_rows, unit_rows, root_inverse, gain_row):
    weighted = grad_rows * gain_row
    middle = jnp.mean(weighted, axis=-1, keepdims=True)
    along = jnp.mean(weighted * unit_rows, axis=-1, keepdims=True)
    return root_inverse * (weighted - middle - unit_rows * along)


def post_forward(total, rows_in, gain):
    fresh = rows_in[0] + total
    unit, _ = norm_parts(fresh)
    return fresh, (unit * gain).astype(BF16), ()


def post_backward(total, rows_in, gain):
    before, source = rows_in
    unit, root = norm_parts(source)
    grad = before + norm_back(total, unit, root, gain)
    return grad, grad.astype(BF16), (jnp.sum(total * unit, axis=0, keepdims=True),)


def post_entry(total, rows_in, gain):
    before, source, mask = rows_in
    unit, root = norm_parts(source)
    grad = before + norm_back(total, unit, root, gain)
    sums = (
        jnp.sum(total * unit, axis=0, keepdims=True),
        jnp.sum(grad * mask, axis=0, keepdims=True),
    )
    return grad * (1.0 - mask), None, sums


def post_plain(total, rows_in, gain):
    return (rows_in[0] + total).astype(BF16), None, ()


def square_kernel(
    post, dims, row_count, sum_count, gather, tile, *refs
):
    lhs_ref, weight_ref, gain_ref = refs[:3]
    refs = refs[3:]
    row_refs, refs = refs[:row_count], refs[row_count:]
    wide_ref, refs = refs[0], refs[1:]
    if gather:
        full_ref, refs = refs[0], refs[1:]
    sum_refs, refs = refs[:sum_count], refs[sum_count:]
    first_out, first_in, second_out, second_in, mine, send_sem, recv_sem = refs
    place = lax.axis_index("mp")
    up, across = lax.div(place, 2), lax.rem(place, 2)
    beside = up * 2 + (1 - across)
    above = (1 - up) * 2 + across
    corner = (1 - up) * 2 + (1 - across)
    share = mine.shape[0]
    half = mine.shape[1] // 2
    columns = 256
    peers = (beside, above)

    barrier = pltpu.get_barrier_semaphore()
    for peer in peers:
        pl.semaphore_signal(barrier, inc=1, device_id={"mp": peer}, device_id_type=MESH)
    pl.semaphore_wait(barrier, 2)

    def rows_of(owner):
        return pl.ds(pl.multiple_of(owner * share, 16), share)

    def remote(source, target, slot, peer):
        return pltpu.make_async_remote_copy(
            src_ref=source,
            dst_ref=target,
            send_sem=send_sem.at[slot],
            recv_sem=recv_sem.at[slot],
            device_id={"mp": peer},
            device_id_type=MESH,
        )

    def partial_into(owner, side, put):
        block = rows_of(owner)

        def step(j, carry):
            at = pl.multiple_of(j * columns, columns)
            there = pl.ds(pl.multiple_of(side * half + j * columns, columns), columns)
            if dims == NT:
                part = product(lhs_ref[block, :], weight_ref[there, :], NT)
            else:
                part = product(lhs_ref[block, :], weight_ref[:, there])
            put(pl.ds(at, columns), there, part)
            return carry

        lax.fori_loop(0, half // columns, step, 0)

    copies = []
    for order, targets in ((0, (corner, corner)), (1, (beside, above))):
        for side in range(2):

            def put(at, there, part, side=side, order=order):
                first_out[side, order, :, at] = part.astype(BF16)

            partial_into(targets[side], side, put)
            copy = remote(
                first_out.at[side, order], first_in.at[side, order], side * 2 + order, peers[side]
            )
            copy.start()
            copies.append(copy)

    def put_mine(at, there, part):
        mine[:, there] = part

    for side, owner in ((0, above), (1, beside)):

        def put_on(at, there, part, side=side):
            second_out[side, :, at] = part.astype(BF16)

        partial_into(owner, side, put_on)
    for side in range(2):
        partial_into(place, side, put_mine)

    onward = []
    for side in range(2):
        copies[side].wait_recv()
        second_out[side] = (
            second_out[side].astype(F32) + first_in[side, 0].astype(F32)
        ).astype(BF16)
        copy = remote(second_out.at[side], second_in.at[side], 4 + side, peers[1 - side])
        copy.start()
        onward.append(copy)
    for side in range(2):
        copies[2 + side].wait_recv()
    for side in range(2):
        onward[side].wait_recv()

    for sum_ref in sum_refs:
        sum_ref[...] = jnp.zeros_like(sum_ref)

    def finish(t, carry):
        at = pl.ds(pl.multiple_of(t * tile, 16), tile)
        total = jnp.concatenate(
            [
                mine[at, side * half : (side + 1) * half]
                + first_in[side, 1, at, :].astype(F32)
                + second_in[side, at, :].astype(F32)
                for side in range(2)
            ],
            axis=1,
        )
        wide, narrow, sums = post(total, tuple(r[at, :] for r in row_refs), gain_ref[...])
        wide_ref[at, :] = wide
        if gather:
            full_ref[pl.ds(pl.multiple_of(place * share + t * tile, 16), tile), :] = narrow
        for sum_ref, term in zip(sum_refs, sums):
            sum_ref[...] += term
        return carry

    lax.fori_loop(0, share // tile, finish, 0)

    if gather:

        def spread(owner, side, slot, peer):
            where = full_ref.at[rows_of(owner), pl.ds(side * half, half)]
            copy = remote(where, where, slot, peer)
            copy.start()
            return copy

        first = [spread(place, 0, 6, above), spread(place, 1, 7, beside)]
        rest = [spread(place, 0, 8, beside), spread(place, 1, 9, above)]
        first[0].wait_recv()
        rest.append(spread(above, 0, 10, beside))
        first[1].wait_recv()
        rest.append(spread(beside, 1, 11, above))
        for copy in rest:
            copy.wait_recv()
        for copy in first + rest:
            copy.wait_send()
    for copy in copies + onward:
        copy.wait_send()


def square_step(lhs, weight, dims, post, gain, rows_in, wide_type, sum_count, gather, ident):
    rows = lhs.shape[0]
    width = gain.shape[1]
    share = rows // 4
    outs = [jax.ShapeDtypeStruct((share, width), wide_type)]
    if gather:
        outs.append(jax.ShapeDtypeStruct((rows, width), BF16))
    outs += [jax.ShapeDtypeStruct((1, width), F32)] * sum_count
    half = width // 2
    vmem = pl.BlockSpec(memory_space=pltpu.VMEM)
    slots = 12 if gather else 6
    return pl.pallas_call(
        functools.partial(
            square_kernel, post, dims, len(rows_in), sum_count, gather, 32
        ),
        out_shape=outs,
        in_specs=[vmem] * (3 + len(rows_in)),
        out_specs=[vmem] * len(outs),
        scratch_shapes=[
            pltpu.VMEM((2, 2, share, half), BF16),
            pltpu.VMEM((2, 2, share, half), BF16),
            pltpu.VMEM((2, share, half), BF16),
            pltpu.VMEM((2, share, half), BF16),
            pltpu.VMEM((share, width), F32),
            pltpu.SemaphoreType.DMA((slots,)),
            pltpu.SemaphoreType.DMA((slots,)),
        ],
        compiler_params=pltpu.CompilerParams(
            collective_id=ident, has_side_effects=True, vmem_limit_bytes=VMEM_BYTES
        ),
        cost_estimate=pl.CostEstimate(
            flops=2 * rows * width * lhs.shape[1],
            bytes_accessed=2 * (lhs.size + weight.size + 6 * share * width),
            transcendentals=0,
        ),
    )(lhs, weight, gain, *rows_in)


def plain_step(lhs, weight, dims, post, gain, rows_in, wide_type, sum_count, gather, ident):
    part = product(lhs, weight, dims).astype(BF16)
    total = lax.psum_scatter(part, "mp", scatter_dimension=0, tiled=True).astype(F32)
    wide, narrow, sums = post(total, rows_in, gain)
    outs = [wide.astype(wide_type)]
    if gather:
        outs.append(lax.all_gather(narrow, "mp", axis=0, tiled=True))
    return outs + list(sums)


def softmax_rows(queries, keys_in):
    scores = product(queries, keys_in, NT) * SCALE
    powers = jnp.exp(scores - jnp.max(scores, axis=-1, keepdims=True))
    return powers * (1.0 / jnp.sum(powers, axis=-1, keepdims=True))


def attend_forward_kernel(heads, separate, query_ref, pair_ref, out_ref):
    key_at = 0 if separate else heads
    for h in range(heads):
        queries = query_ref[:, h * HDIM : (h + 1) * HDIM]
        keys_in = pair_ref[:, (key_at + h) * HDIM : (key_at + h + 1) * HDIM]
        values_in = pair_ref[:, (key_at + heads + h) * HDIM : (key_at + heads + h + 1) * HDIM]
        probs = softmax_rows(queries, keys_in).astype(BF16)
        out_ref[:, h * HDIM : (h + 1) * HDIM] = product(probs, values_in).astype(BF16)


def attend_backward_kernel(heads, separate, query_ref, pair_ref, grad_ref, *outs):
    key_at = 0 if separate else heads
    query_out, pair_out = outs if separate else (outs[0], outs[0])
    for h in range(heads):
        own = slice(h * HDIM, (h + 1) * HDIM)
        key_slice = slice((key_at + h) * HDIM, (key_at + h + 1) * HDIM)
        value_slice = slice((key_at + heads + h) * HDIM, (key_at + heads + h + 1) * HDIM)
        queries, keys_in, values_in = query_ref[:, own], pair_ref[:, key_slice], pair_ref[:, value_slice]
        grad = grad_ref[:, own]
        probs = softmax_rows(queries, keys_in)
        pair_out[:, value_slice] = product(probs.astype(BF16), grad, TN).astype(BF16)
        grad_probs = product(grad, values_in, NT)
        centred = grad_probs - jnp.sum(probs * grad_probs, axis=-1, keepdims=True)
        grad_scores = (probs * centred * SCALE).astype(BF16)
        query_out[:, own] = product(grad_scores, keys_in).astype(BF16)
        pair_out[:, key_slice] = product(grad_scores, queries, TN).astype(BF16)


def image_blocks(images, *arrays):
    return [pl.BlockSpec((a.shape[0] // images, a.shape[1]), lambda i: (i, 0)) for a in arrays]


def attend_forward(images, heads, queries, pairs):
    separate = queries is not pairs
    out = jax.ShapeDtypeStruct((queries.shape[0], heads * HDIM), BF16)
    return pl.pallas_call(
        functools.partial(attend_forward_kernel, heads, separate),
        grid=(images,),
        out_shape=out,
        in_specs=image_blocks(images, queries, pairs),
        out_specs=image_blocks(images, out)[0],
        compiler_params=pltpu.CompilerParams(vmem_limit_bytes=VMEM_BYTES),
    )(queries, pairs)


def attend_backward(images, heads, queries, pairs, grad):
    separate = queries is not pairs
    outs = [jax.ShapeDtypeStruct(queries.shape, BF16)]
    if separate:
        outs.append(jax.ShapeDtypeStruct(pairs.shape, BF16))
    result = pl.pallas_call(
        functools.partial(attend_backward_kernel, heads, separate),
        grid=(images,),
        out_shape=outs,
        in_specs=image_blocks(images, queries, pairs, grad),
        out_specs=image_blocks(images, *outs),
        compiler_params=pltpu.CompilerParams(vmem_limit_bytes=VMEM_BYTES),
    )(queries, pairs, grad)
    return result if separate else result[0]


def gelu_exact(values_in):
    return jax.nn.gelu(values_in, approximate=False)


def body(
    step,
    tokens,
    caption,
    masked,
    out_grad,
    mask_embed,
    norm_gains,
    attention_in,
    attention_out,
    cross_query,
    cross_text,
    cross_out,
    feed_expand,
    feed_shrink,
):
    axis_count = lax.axis_size("mp")
    axis_place = lax.axis_index("mp")
    images, length = masked.shape
    rows_all = images * length
    share_rows = rows_all // axis_count
    model_width = tokens.shape[1]
    text_width = caption.shape[1]
    heads_here = attention_in.shape[2] // HDIM

    def own_rows(rows_in):
        return lax.dynamic_slice_in_dim(rows_in, axis_place * share_rows, share_rows, 0)

    def image_sum(part, dimension):
        return lax.psum_scatter(
            part.astype(BF16), "img", scatter_dimension=dimension, tiled=True
        ).astype(F32)

    gains = [norm_gains[k : k + 1] for k in range(3)]
    mask_column = (masked.reshape(rows_all, 1) > 0)

    def enter(rows_in, mask):
        return jnp.where(mask, mask_embed.astype(F32)[None, :], rows_in.astype(F32))

    own_mask = own_rows(mask_column)
    own_float = own_mask.astype(F32)
    own_entry = enter(own_rows(tokens), own_mask)
    first_unit, _ = norm_parts(enter(tokens, mask_column))
    first_normed = (first_unit * gains[0]).astype(BF16)
    weight_in = attention_in.reshape(model_width, -1)
    projected = product(first_normed, weight_in).astype(BF16)
    self_mixed = attend_forward(images, heads_here, projected, projected)
    own_self, second_normed = step(
        self_mixed, attention_out, NN, post_forward, gains[1], (own_entry,), F32, 0, True, 1
    )
    cross_queries = product(second_normed, cross_query).astype(BF16)
    weight_text = cross_text.reshape(text_width, -1)
    text_pairs = product(caption, weight_text).astype(BF16)
    cross_mixed = attend_forward(images, heads_here, cross_queries, text_pairs)
    own_cross, third_normed = step(
        cross_mixed, cross_out, NN, post_forward, gains[2], (own_self,), F32, 0, True, 2
    )

    feed_grad = jnp.where(mask_column, out_grad, jnp.zeros_like(out_grad))
    own_feed_grad = own_rows(feed_grad).astype(F32)
    hidden = product(third_normed, feed_expand)
    active = gelu_exact(hidden).astype(BF16)
    shrink_sum = image_sum(product(active, feed_grad, TN), 1)
    grad_active = product(feed_grad, feed_shrink, NT)
    _, gelu_pull = jax.vjp(gelu_exact, hidden)
    grad_hidden = gelu_pull(grad_active)[0].astype(BF16)
    expand_sum = image_sum(product(third_normed, grad_hidden, TN), 0)
    own_before_feed, cross_grad, third_gain = step(
        grad_hidden, feed_expand, NT, post_backward, gains[2], (own_feed_grad, own_cross), F32, 1, True, 3
    )

    cross_out_sum = image_sum(product(cross_mixed, cross_grad, TN), 1)
    grad_cross_mixed = product(cross_grad, cross_out, NT).astype(BF16)
    grad_cross_queries, grad_text_pairs = attend_backward(
        images, heads_here, cross_queries, text_pairs, grad_cross_mixed
    )
    cross_query_sum = image_sum(product(second_normed, grad_cross_queries, TN), 0)
    cross_text_sum = image_sum(product(caption, grad_text_pairs, TN), 0)
    caption_grad = lax.psum_scatter(
        product(grad_text_pairs, weight_text, NT).astype(BF16), "mp", scatter_dimension=1, tiled=True
    ).astype(F32)
    own_before_cross, self_grad, second_gain = step(
        grad_cross_queries, cross_query, NT, post_backward, gains[1], (own_before_feed, own_self), F32, 1, True, 4
    )

    self_out_sum = image_sum(product(self_mixed, self_grad, TN), 1)
    grad_self_mixed = product(self_grad, attention_out, NT).astype(BF16)
    grad_projected = attend_backward(images, heads_here, projected, projected, grad_self_mixed)
    self_in_sum = image_sum(product(first_normed, grad_projected, TN), 0)
    tokens_grad, first_gain, embed_term = step(
        grad_projected, weight_in, NT, post_entry, gains[0],
        (own_before_cross, own_entry, own_float), F32, 2, False, 5,
    )
    (mixed_out,) = step(
        active, feed_shrink, NN, post_plain, gains[0], (own_cross,), BF16, 0, False, 6
    )

    small_terms = jnp.concatenate([first_gain, second_gain, third_gain, embed_term], axis=0)
    small_sums = lax.psum_scatter(small_terms, ("img", "mp"), scatter_dimension=1, tiled=True)
    return (
        mixed_out,
        tokens_grad,
        caption_grad,
        small_sums[3],
        small_sums[0:3],
        self_in_sum.reshape(-1, 3, attention_in.shape[2]),
        self_out_sum,
        cross_query_sum,
        cross_text_sum.reshape(-1, 2, cross_text.shape[2]),
        cross_out_sum,
        expand_sum,
        shrink_sum,
    )


def solution(mesh):
    step = square_step if mesh.shape["mp"] == 4 else plain_step
    return jax.shard_map(
        functools.partial(body, step),
        mesh=mesh,
        in_specs=(
            P("img", None),
            P("img", None),
            P("img", None),
            P("img", None),
            P(),
            P(),
            P(None, None, "mp"),
            P("mp", None),
            P(None, "mp"),
            P(None, None, "mp"),
            P("mp", None),
            P(None, "mp"),
            P("mp", None),
        ),
        out_specs=(
            P(("img", "mp"), None),
            P(("img", "mp"), None),
            P("img", "mp"),
            P(("img", "mp")),
            P(None, ("img", "mp")),
            P("img", None, "mp"),
            P("mp", "img"),
            P("img", "mp"),
            P("img", None, "mp"),
            P("mp", "img"),
            P("img", "mp"),
            P("mp", "img"),
        ),
        check_vma=False,
    )
```

time: 1740 us -> 1080 us (0.62)
  waiting for transfers between devices: 1280 us -> 505 us
  Pallas kernels: 0 us -> 336 us
  matrix products: 222 us -> 128 us
  local copies, waits for them, and re-layouts: 123 us -> 52.1 us
  other arithmetic: 87 us -> 33.3 us
    psum x5 -> x0, waiting for transfers between devices: 695 us -> none  [the longest x3 496 us: reduce_branch(): return lax.psum(partial_rows, 'mp')]
    pallas_call x0 -> x10, Pallas kernels: none -> 336 us  [the longest x6 308 us: square_step(): pl.pallas_call(functools.partial(square_kernel, post, dims, len(rows_in),...]
    unnamed x16 -> x10, waiting for transfers between devices: 276 us -> 29.2 us
    reduce_scatter x7 -> x8, waiting for transfers between devices: 311 us -> 476 us  [the longest x7 432 us: image_sum(): lax.psum_scatter(part.astype(BF16), 'img', scatter_dimension=dimension, t...]
    dot_general x33 -> x15, matrix products: 222 us -> 128 us  [product(): return lax.dot_general(left, right, dims, preferred_element_type=F32)]
    convert_element_type x8 -> x0, local copies, waits for them, and re-layouts: 39.8 us -> none  [the longest x1 21.3 us: body(): cross_text_sum.astype(jnp.bfloat16)]
    reduce_sum x8 -> x0, other arithmetic: 24.7 us -> none  [the longest x3 15.9 us: norm_back(): middle = jnp.mean(weighted, axis=-1, keepdims=True)]
    unnamed x114 -> x61, local copies, waits for them, and re-layouts: 49.2 us -> 40.1 us
  transfers between devices with their start and end apart: 14 -> 9, of which waited for: 12 -> 9; matrix products, arithmetic and copies ran while one was open for 14% -> 9% of each run, Pallas kernels for 0% -> 3%
where the time goes in v1:
time: 1080 us; the launch traced here: 1070 us
  waiting for transfers between devices  505 us (47%)
  Pallas kernels  336 us (31%)
  matrix products  128 us (12%)
  local copies, waits for them, and re-layouts  52.1 us (5%)
  other arithmetic  33.3 us (3%)
  between operations  14.7 us (1%)
    reduce_scatter x7, waiting for transfers between devices, image_sum(): lax.psum_scatter(part.astype(BF16), 'img', scatter_dimension=dimension, t...  432 us
    pallas_call x6, Pallas kernels, square_step(): pl.pallas_call(functools.partial(square_kernel, post, dims, len(rows_in),...  308 us
    dot_general x15, matrix products, product(): return lax.dot_general(left, right, dims, preferred_element_type=F32)  128 us
    reduce_scatter x1, waiting for transfers between devices, body(): lax.psum_scatter(product(grad_text_pairs, weight_text, NT).astype(BF16),...  44 us
    unnamed x61, local copies, waits for them, and re-layouts  40.1 us
    unnamed x10, waiting for transfers between devices  29.2 us
  transfers between devices with their start and end apart: 9, of which 9 were waited for; matrix products, arithmetic and copies ran while one was open for 9% of the time, Pallas kernels for 3%

profile of v1, /device:TPU:0, one launch (start us, length us, event | category | flops | bytes accessed | tf_op | source)
XLA Modules:
  0.0 1069.0 jit_solution(10067059834335619519)
XLA Ops:
  8.8 8.9 copy.34
  17.8 2.7 fusion.7
  20.5 2.9 multiply_reduce_fusion
  23.4 8.6 copy.36.refs_1_
  32.0 9.9 convolution_convert_fusion.4.query_ref.pair_ref
  41.9 5.5 shard_map.220.refs_0_
  48.8 2.5 convert_select_fusion.1.refs_3_.refs_4_
  51.2 9.4 copy.46
  64.4 63.6 %shard_map.221 = (f32[192,2048]{1,0:T(8,128)}, bf16[768,2048]{1,0:T(8,128)(2,1)}) custom-call(bf16[768,512]{1,0:T(8,128)(2,1)S(1)} %copy-done.4, bf16[512,2048]{1,0:T(8,128)(2,1)} %refs_1_.5, f32[1,2048]{1,0:T(1,128)S(1)} %get-tuple-element.84.refs_2_, f32[192,2048]{1,0:T(8,128)} %convert_select_fusion.1.refs_3_.refs_4_), custom_call_target="tpu_custom_call" | custom-call | flops 1610612736 | bytes 7602176 | tf_op jit(solution)/shard_map/pallas_call | solution.py:220
  128.0 3.7 convolution_convert_fusion.10.query_ref
  131.7 7.0 convolution_convert_fusion.11.pair_ref
  138.7 3.7 shard_map.222.refs_0_
  142.4 59.2 %shard_map.223 = (f32[192,2048]{1,0:T(8,128)}, bf16[768,2048]{1,0:T(8,128)(2,1)}) custom-call(bf16[768,512]{1,0:T(8,128)(2,1)S(1)} %shard_map.222.refs_0_, bf16[512,2048]{1,0:T(8,128)(2,1)} %refs_1_.6, f32[1,2048]{1,0:T(1,128)S(1)} %get-tuple-element.82.refs_2_, f32[192,2048]{1,0:T(8,128)} %get-tuple-element.28.refs_3_.refs_4_), custom_call_target="tpu_custom_call" | custom-call | flops 1610612736 | bytes 7602176 | tf_op jit(solution)/shard_map/pallas_call | solution.py:220
  201.6 10.0 fusion.10
  211.7 25.4 %add_convert_fusion = (bf16[768,2048]{1,0:T(8,128)(2,1)}, f32[768,2048]{1,0:T(8,128)}) fusion(f32[768,2048]{1,0:T(8,128)S(1)} %fusion.10, bf16[768,2048]{1,0:T(8,128)(2,1)S(1)} %broadcast_select_fusion, bf16[2048,2048]{1,0:T(8,128)(2,1)} %refs_1_.7), kind=kOutput, calls=%fused_computation.6 | convolution fusion | flops 6555697152 | bytes 27262976 | tf_op jit(solution)/shard_map/dot_general | solution.py:25
  237.1 61.1 %shard_map.225 = (f32[192,2048]{1,0:T(8,128)S(1)}, bf16[768,2048]{1,0:T(8,128)(2,1)}, f32[1,2048]{1,0:T(1,128)S(1)}) custom-call(bf16[768,2048]{1,0:T(8,128)(2,1)} %get-tuple-element.78.refs_0_, bf16[2048,2048]{1,0:T(8,128)(2,1)} %refs_1_.8, f32[1,2048]{1,0:T(1,128)S(1)} %get-tuple-element.82.refs_2_, f32[192,2048]{1,0:T(8,128)} %dynamic-slice_convert_fusion.refs_3_, ...), custom_call_target="tpu_custom_call" | custom-call | flops 6442450944 | bytes 16252928 | tf_op jit(solution)/shard_map/pallas_call | solution.py:220
  299.3 4.6 convolution_convert_fusion.9.grad_ref
  303.9 7.8 shard_map.226
  311.8 56.2 %shard_map.227 = (f32[192,2048]{1,0:T(8,128)}, bf16[768,2048]{1,0:T(8,128)(2,1)}, f32[1,2048]{1,0:T(1,128)S(1)}) custom-call(bf16[768,512]{1,0:T(8,128)(2,1)S(1)} %get-tuple-element.32.refs_0_, bf16[2048,512]{1,0:T(8,128)(2,1)} %refs_1_.9, f32[1,2048]{1,0:T(1,128)S(1)} %get-tuple-element.84.refs_2_, f32[192,2048]{1,0:T(8,128)} %copy-done.6, ...), custom_call_target="tpu_custom_call" | custom-call | flops 1610612736 | bytes 7602176 | tf_op jit(solution)/shard_map/pallas_call | solution.py:220
  368.9 3.7 convolution_convert_fusion.8.grad_ref
  372.6 10.6 shard_map.228.refs_0_
  383.2 33.7 %shard_map.229 = (f32[192,2048]{1,0:T(8,128)S(1)}, f32[1,2048]{1,0:T(1,128)S(1)}, f32[1,2048]{1,0:T(1,128)S(1)}) custom-call(bf16[768,1536]{1,0:T(8,128)(2,1)} %shard_map.228.refs_0_, bf16[2048,1536]{1,0:T(8,128)(2,1)} %copy.36.refs_1_, f32[1,2048]{1,0:T(1,128)S(1)} %get-tuple-element.83.refs_2_, f32[192,2048]{1,0:T(8,128)} %get-tuple-element.35.refs_3_, ...), custom_call_target="tpu_custom_call" | custom-call | flops 4831838208 | bytes 13369344 | tf_op jit(solution)/shard_map/pallas_call | solution.py:220
  419.5 5.3 convolution_convert_fusion.7
  424.8 5.3 convolution_convert_fusion.6
  430.2 5.3 convolution_convert_fusion.5
  435.6 8.8 convolution_convert_fusion.3
  444.5 9.8 convolution_convert_fusion
  454.3 8.1 convert_bitcast_fusion
  462.5 11.3 %convolution_convert_fusion.2 = bf16[2048,2048]{1,0:T(8,128)(2,1)} fusion(bf16[768,2048]{1,0:T(8,128)(2,1)} %get-tuple-element.29, bf16[768,2048]{1,0:T(8,128)(2,1)} %get-tuple-element.78.refs_0_), kind=kOutput, calls=%fused_computation.4 | convolution fusion | flops 6446645248 | bytes 14680064 | tf_op jit(solution)/shard_map/dot_general | solution.py:25
  474.0 6.4 multiply_convert_fusion.refs_0_
  482.1 9.4 convolution_convert_fusion.1
  491.5 34.4 %shard_map.224 = bf16[192,2048]{1,0:T(8,128)(2,1)S(1)} custom-call(bf16[768,2048]{1,0:T(8,128)(2,1)} %copy-done.13, bf16[2048,2048]{1,0:T(8,128)(2,1)} %refs_1_.7, f32[1,2048]{1,0:T(1,128)S(1)} %get-tuple-element.83.refs_2_, f32[192,2048]{1,0:T(8,128)} %get-tuple-element.30.refs_3_.refs_4_), custom_call_target="tpu_custom_call" | custom-call | flops 6442450944 | bytes 16252928 | tf_op jit(solution)/shard_map/pallas_call | solution.py:220
  526.8 29.0 %reduce-scatter.28.cloned.1.call-done = f32[64,4]{1,0:T(8,128)} async-done(((f32[2048,4]{1,0:T(8,128)}), f32[64,4]{1,0:T(8,128)}) %reduce-scatter.28.cloned.1.call-update) | async-done | bytes 1040
  558.7 32.2 %reduce-scatter.16.cloned.1.call-done = bf16[512,256]{1,0:T(8,128)(2,1)} async-done(((bf16[512,2048]{1,0:T(8,128)(2,1)}), bf16[512,256]{1,0:T(8,128)(2,1)}) %reduce-scatter.16.cloned.1.call-update) | async-done | bytes 262160 | tf_op jit(solution)/shard_map/reduce_scatter | solution.py:357
  592.7 35.6 %reduce-scatter.18.cloned.1.call-done = bf16[256,512]{1,0:T(8,128)(2,1)} async-done(((bf16[2048,512]{1,0:T(8,128)(2,1)}), bf16[256,512]{1,0:T(8,128)(2,1)}) %reduce-scatter.18.cloned.1.call-update) | async-done | bytes 262160 | tf_op jit(solution)/shard_map/reduce_scatter | solution.py:357
  630.1 35.5 %reduce-scatter.22.cloned.1.call-done = bf16[512,256]{1,0:T(8,128)(2,1)} async-done(((bf16[512,2048]{1,0:T(8,128)(2,1)}), bf16[512,256]{1,0:T(8,128)(2,1)}) %reduce-scatter.22.cloned.1.call-update) | async-done | bytes 262160 | tf_op jit(solution)/shard_map/reduce_scatter | solution.py:357
  667.3 44.0 %reduce-scatter.12.cloned.1.call-done = bf16[384,1024]{1,0:T(8,128)(2,1)} async-done(((bf16[384,4096]{1,0:T(8,128)(2,1)}), bf16[384,1024]{1,0:T(8,128)(2,1)}) %reduce-scatter.12.cloned.1.call-update) | async-done | bytes 786448 | tf_op jit(solution)/shard_map/reduce_scatter | solution.py:406
  711.3 2.5 convert_element_type.101
  713.7 69.7 %reduce-scatter.14.cloned.1.call-done = bf16[256,1536]{1,0:T(8,128)(2,1)} async-done(((bf16[2048,1536]{1,0:T(8,128)(2,1)}), bf16[256,1536]{1,0:T(8,128)(2,1)}) %reduce-scatter.14.cloned.1.call-update) | async-done | bytes 786448 | tf_op jit(solution)/shard_map/reduce_scatter | solution.py:357
  783.4 2.5 copy.37
  785.9 3.0 copy.38
  788.9 84.8 %reduce-scatter.20.cloned.1.call-done = bf16[512,1024]{0,1:T(8,128)(2,1)} async-done(((bf16[4096,1024]{0,1:T(8,128)(2,1)}), bf16[512,1024]{0,1:T(8,128)(2,1)}) %reduce-scatter.20.cloned.1.call-update) | async-done | bytes 1048592 | tf_op jit(solution)/shard_map/reduce_scatter | solution.py:357
  873.8 3.8 copy.39
  877.5 86.6 %reduce-scatter.24.cloned.1.call-done = bf16[256,2048]{1,0:T(8,128)(2,1)} async-done(((bf16[2048,2048]{1,0:T(8,128)(2,1)}), bf16[256,2048]{1,0:T(8,128)(2,1)}) %reduce-scatter.24.cloned.1.call-update) | async-done | bytes 1048592 | tf_op jit(solution)/shard_map/reduce_scatter | solution.py:357
  964.2 2.8 convert_element_type.112
  966.9 87.6 %reduce-scatter.26.cloned.1.call-done = bf16[2048,256]{1,0:T(8,128)(2,1)} async-done(((bf16[2048,2048]{1,0:T(8,128)(2,1)}), bf16[2048,256]{1,0:T(8,128)(2,1)}) %reduce-scatter.26.cloned.1.call-update) | async-done | bytes 1048592 | tf_op jit(solution)/shard_map/reduce_scatter | solution.py:357
  1054.6 2.7 convert_element_type.114
  1059.4 2.7 copy.50
  (89 shorter events, 24.7 us)
Async XLA Ops:
  7.2 124.5 %copy-start = (bf16[384,4096]{1,0:T(8,128)(2,1)S(1)}, bf16[384,4096]{1,0:T(8,128)(2,1)}, u32[]{:S(2)}) copy-start(bf16[384,4096]{1,0:T(8,128)(2,1)} %param.14) | copy-start | bytes 9437188
  7.2 548.6 %reduce-scatter.28.cloned.1.call-start = ((), (), s32[]{:S(2)}) async-start(), calls=%async_computation.17 | async-start | bytes 1081344
  8.8 8.9 copy-start.17
  8.8 8.9 copy-start.20
  17.8 31.0 %copy-start.15 = (f32[2048]{0:T(1024)}, f32[2048]{0:T(1024)S(1)}, u32[]{:S(2)}) copy-start(f32[2048]{0:T(1024)S(1)} %convert_element_type.87) | copy-start | bytes 24580
  20.5 11.5 %copy-start.18 = (f32[768]{0:T(1024)}, f32[768]{0:T(1024)S(1)}, u32[]{:S(2)}) copy-start(f32[768]{0:T(1024)S(1)} %broadcast_multiply_fusion) | copy-start | bytes 9220
  23.4 8.6 copy-start.21
  47.5 0.9 copy-start.3
  60.6 3.8 copy-start.4
  60.6 67.4 %copy-start.14 = (bf16[2048,512]{1,0:T(8,128)(2,1)S(1)}, bf16[2048,512]{1,0:T(8,128)(2,1)}, u32[]{:S(2)}) copy-start(bf16[2048,512]{1,0:T(8,128)(2,1)} %refs_1_.9) | copy-start | bytes 6291460
  62.9 148.8 %copy-start.11 = (bf16[768,2048]{1,0:T(8,128)(2,1)}, bf16[768,2048]{1,0:T(8,128)(2,1)S(1)}, u32[]{:S(2)}) copy-start(bf16[768,2048]{1,0:T(8,128)(2,1)S(1)} %broadcast_select_fusion) | copy-start | bytes 9437188
  131.7 7.0 copy-start.1
  142.4 69.3 %copy-start.2 = (bf16[768,512]{1,0:T(8,128)(2,1)}, bf16[768,512]{1,0:T(8,128)(2,1)S(1)}, u32[]{:S(2)}) copy-start(bf16[768,512]{1,0:T(8,128)(2,1)S(1)} %shard_map.222.refs_0_) | copy-start | bytes 2359300
  211.7 25.4 %copy-start.10 = (f32[768,2048]{1,0:T(8,128)}, f32[768,2048]{1,0:T(8,128)S(1)}, u32[]{:S(2)}) copy-start(f32[768,2048]{1,0:T(8,128)S(1)} %fusion.10) | copy-start | bytes 18874372
  237.1 62.3 %copy-start.23 = (bf16[512,2048]{1,0:T(8,128)(2,1)S(1)}, bf16[512,2048]{1,0:T(8,128)(2,1)}, u32[]{:S(2)}) copy-start(bf16[512,2048]{1,0:T(8,128)(2,1)} %refs_1_.6) | copy-start | bytes 6291460
  298.2 1.1 copy-start.6
  303.9 65.0 %copy-start.24 = (bf16[512,2048]{1,0:T(8,128)(2,1)S(1)}, bf16[512,2048]{1,0:T(8,128)(2,1)}, u32[]{:S(2)}) copy-start(bf16[512,2048]{1,0:T(8,128)(2,1)} %refs_1_.5) | copy-start | bytes 6291460
  311.8 60.8 %copy-start.9 = (bf16[384,1024]{1,0:T(8,128)(2,1)}, bf16[384,1024]{1,0:T(8,128)(2,1)S(1)}, u32[]{:S(2)}) copy-start(bf16[384,1024]{1,0:T(8,128)(2,1)S(1)} %get-tuple-element.37) | copy-start | bytes 2359300
  368.0 0.9 copy-start.8
  416.9 1.2 copy-start.5
  419.4 171.5 %reduce-scatter.16.cloned.1.call-start = ((), (), s32[]{:S(2)}) async-start(), calls=%async_computation.11 | async-start | bytes 2359296 | tf_op jit(solution)/shard_map/reduce_scatter | solution.py:357
  424.8 203.5 %reduce-scatter.18.cloned.1.call-start = ((), (), s32[]{:S(2)}) async-start(), calls=%async_computation.12 | async-start | bytes 2359296 | tf_op jit(solution)/shard_map/reduce_scatter | solution.py:357
  430.1 235.4 %reduce-scatter.22.cloned.1.call-start = ((), (), s32[]{:S(2)}) async-start(), calls=%async_computation.14 | async-start | bytes 2359296 | tf_op jit(solution)/shard_map/reduce_scatter | solution.py:357
  435.5 275.8 %reduce-scatter.12.cloned.1.call-start = ((), (), s32[]{:S(2)}) async-start(), calls=%async_computation.9 | async-start | bytes 3932160 | tf_op jit(solution)/shard_map/reduce_scatter | solution.py:406
  435.5 8.9 copy-start.16
  435.5 8.9 copy-start.19
  435.6 8.9 copy-start.22
  444.4 339.0 %reduce-scatter.14.cloned.1.call-start = ((), (), s32[]{:S(2)}) async-start(), calls=%async_computation.10 | async-start | bytes 7077888 | tf_op jit(solution)/shard_map/reduce_scatter | solution.py:357
  454.3 419.5 %reduce-scatter.20.cloned.1.call-start = ((), (), s32[]{:S(2)}) async-start(), calls=%async_computation.13 | async-start | bytes 9437184 | tf_op jit(solution)/shard_map/reduce_scatter | solution.py:357
  462.5 501.7 %reduce-scatter.24.cloned.1.call-start = ((), (), s32[]{:S(2)}) async-start(), calls=%async_computation.15 | async-start | bytes 9437184 | tf_op jit(solution)/shard_map/reduce_scatter | solution.py:357
  473.9 580.7 %reduce-scatter.26.cloned.1.call-start = ((), (), s32[]{:S(2)}) async-start(), calls=%async_computation.16 | async-start | bytes 9437184 | tf_op jit(solution)/shard_map/reduce_scatter | solution.py:357
  473.9 8.1 copy-start.12
  480.4 1.7 copy-start.13
  525.9 0.9 copy-start.7
Sparse Core Ops, SparseCore 0:
  419.5 136.2 reduce-scatter.27
  558.8 32.0 reduce-scatter.15
  593.9 34.3 reduce-scatter.17
  631.1 34.3 reduce-scatter.21
  668.6 42.5 reduce-scatter.11
  713.5 69.8 reduce-scatter.13
  785.8 87.9 reduce-scatter.19
  876.1 87.9 reduce-scatter.23
  966.6 87.9 reduce-scatter.25

commit v2 on v1

--- a/solution.py
+++ b/solution.py
@@ -11,7 +11,7 @@
 HDIM = 128
 EPSILON = 1e-05
 SCALE = 1.0 / math.sqrt(HDIM)
-VMEM_BYTES = 52 * 1024 * 1024
+VMEM_BYTES = 58 * 1024 * 1024
 MESH = pl.DeviceIdType.MESH
 BF16 = jnp.bfloat16
 F32 = jnp.float32
@@ -23,6 +23,14 @@
 
 def product(left, right, dims=NN):
     return lax.dot_general(left, right, dims, preferred_element_type=F32)
+
+
+def image_sum(part, dimension=0):
+    return lax.psum_scatter(part, "img", scatter_dimension=dimension, tiled=True).astype(F32)
+
+
+def rows_product(left, right):
+    return product(left, right, TN).astype(BF16)
 
 
 def norm_parts(rows_in):
@@ -66,44 +74,238 @@
     return (rows_in[0] + total).astype(BF16), None, ()
 
 
-def square_kernel(
-    post, dims, row_count, sum_count, gather, tile, *refs
-):
-    lhs_ref, weight_ref, gain_ref = refs[:3]
-    refs = refs[3:]
-    row_refs, refs = refs[:row_count], refs[row_count:]
+def remote(source, target, send, recv, device):
+    return pltpu.make_async_remote_copy(
+        src_ref=source,
+        dst_ref=target,
+        send_sem=send,
+        recv_sem=recv,
+        device_id=device,
+        device_id_type=MESH,
+    )
+
+
+def greet(targets):
+    barrier = pltpu.get_barrier_semaphore()
+    for target in targets:
+        pl.semaphore_signal(barrier, inc=1, device_id=target, device_id_type=MESH)
+    pl.semaphore_wait(barrier, len(targets))
+
+
+class Loader:
+    def __init__(self, sources, targets, sem):
+        self.targets = targets
+        self.copies = [
+            pltpu.make_async_copy(source, target, sem.at[i])
+            for i, (source, target) in enumerate(zip(sources, targets))
+        ]
+        self.waiting = set()
+
+    def start(self, i):
+        self.copies[i].start()
+        self.waiting.add(i)
+
+    def got(self, i):
+        if i in self.waiting:
+            self.waiting.remove(i)
+            self.copies[i].wait()
+        return self.targets[i]
+
+
+class Square:
+    def __init__(self):
+        self.spot = lax.axis_index("mp")
+        up, across = lax.div(self.spot, 2), lax.rem(self.spot, 2)
+        self.beside = up * 2 + (1 - across)
+        self.above = (1 - up) * 2 + across
+        self.corner = (1 - up) * 2 + (1 - across)
+        self.peers = (self.beside, self.above)
+        self.targets = [{"mp": self.beside}, {"mp": self.above}]
+
+
+class LineSum:
+    width = 512
+
+    def __init__(self, lhs_refs, rhs_refs, pieces, refs, loads=None):
+        self.loads = loads
+        self.lhs_refs, self.rhs_refs, self.pieces = lhs_refs, rhs_refs, pieces
+        self.core_out, self.core_in, self.own, self.line_in = refs[:4]
+        self.core_send, self.core_recv, self.line_send, self.line_recv = refs[4:]
+        self.count = len(pieces)
+        self.share = self.own.shape[2]
+        self.place = lax.axis_index("img")
+        self.line, self.core = lax.div(self.place, 2), lax.rem(self.place, 2)
+        self.twin = self.line * 2 + (1 - self.core)
+        self.others = [lax.rem(self.line + j, 4) * 2 + self.core for j in (1, 2, 3)]
+        self.targets = [{"img": self.twin}] + [{"img": o} for o in self.others]
+
+    @staticmethod
+    def scratch(count, share):
+        dma = pltpu.SemaphoreType.DMA
+        width = LineSum.width
+        return [
+            pltpu.VMEM((count, 2, share, width), BF16),
+            pltpu.VMEM((count, 2, share, width), BF16),
+            pltpu.VMEM((count, 4, share, width), BF16),
+            pltpu.VMEM((count, 2, 3, share, width), BF16),
+            dma((count, 2)),
+            dma((count, 2)),
+            dma((count, 2, 3)),
+            dma((count, 2, 3)),
+        ]
+
+    def core_copy(self, g, k):
+        slot = lax.rem(k, 2)
+        return remote(
+            self.core_out.at[g, slot],
+            self.core_in.at[g, slot],
+            self.core_send.at[g, slot],
+            self.core_recv.at[g, slot],
+            {"img": self.twin},
+        )
+
+    def line_copy(self, g, way, s, chunk):
+        return remote(
+            self.own.at[g, chunk],
+            self.line_in.at[g, way, s],
+            self.line_send.at[g, way, s],
+            self.line_recv.at[g, way, s],
+            {"img": self.place + (2 if way == 0 else -2)},
+        )
+
+    def chunk_at(self, k):
+        low = (3 - k) - lax.div(self.line + k, 3)
+        high = k + lax.div(k, jnp.maximum(self.line, 1))
+        chosen = jnp.where(self.line < 2, low, high)
+        return jnp.where(k == 3, self.line, chosen)
+
+    def distance(self, way):
+        return self.line if way == 0 else 3 - self.line
+
+    def multiply(self, g, k):
+        lhs_at, rhs_at, column = self.pieces[g]
+        chunk = self.chunk_at(k)
+        if self.loads:
+            self.loads.got(lhs_at)
+            self.loads.got(len(self.lhs_refs) + rhs_at)
+
+        @pl.when(k >= 2)
+        def _():
+            self.core_copy(g, k).wait_send()
+
+        for mine in (False, True):
+            part = self.core if mine else 1 - self.core
+            at = pl.ds(pl.multiple_of((chunk * 2 + part) * self.share, 128), self.share)
+            done = product(
+                self.lhs_refs[lhs_at][:, at],
+                self.rhs_refs[rhs_at][:, column : column + self.width],
+                TN,
+            ).astype(BF16)
+            if mine:
+                self.own[g, chunk] = done
+            else:
+                self.core_out[g, lax.rem(k, 2)] = done
+                self.core_copy(g, k).start()
+
+    def add(self, g, chunk, arrived):
+        self.own[g, chunk] = (self.own[g, chunk].astype(F32) + arrived.astype(F32)).astype(BF16)
+
+    def send_on(self, g, k):
+        self.core_copy(g, k).wait_recv()
+        self.add(g, self.chunk_at(k), self.core_in[g, lax.rem(k, 2)])
+        for way in range(2):
+            gone = self.distance(way)
+            to = 3 - k + self.line if way == 0 else k - 3 + self.line
+
+            @pl.when((gone <= k) & (k < 3))
+            def _():
+                @pl.when(gone >= 1)
+                def _():
+                    self.line_copy(g, way, k - 1, to).wait_recv()
+                    self.add(g, to, self.line_in[g, way, k - 1])
+
+                self.line_copy(g, way, k, to).start()
+
+    def step(self, k):
+        for g in range(self.count + 1):
+            if g < self.count:
+                self.multiply(g, k)
+            if g > 0:
+                self.send_on(g - 1, k)
+
+    def steps(self, first, last):
+        def one(k, carry):
+            self.step(k)
+            return carry
+
+        lax.fori_loop(first, last, one, 0)
+
+    def collect(self, g):
+        for way in range(2):
+
+            @pl.when(self.distance(way) >= 1)
+            def _():
+                self.line_copy(g, way, 2, self.line).wait_recv()
+                self.add(g, self.line, self.line_in[g, way, 2])
+
+        return self.own[g, self.line].astype(F32)
+
+    def settle(self):
+        for g in range(self.count):
+            for k in (2, 3):
+                self.core_copy(g, k).wait_send()
+
+        def one(k, carry):
+            for g in range(self.count):
+                for way in range(2):
+
+                    @pl.when(self.distance(way) <= k)
+                    def _():
+                        self.line_copy(g, way, k, self.line).wait_send()
+
+            return carry
+
+        lax.fori_loop(0, 3, one, 0)
+
+
+def square_kernel(post, dims, row_count, sum_count, gather, tile, pieces, flip, *refs):
+    big = 4 if pieces else 2
+    gain_ref, sources, refs = refs[0], refs[1 : 1 + big + row_count], refs[1 + big + row_count :]
     wide_ref, refs = refs[0], refs[1:]
     if gather:
         full_ref, refs = refs[0], refs[1:]
     sum_refs, refs = refs[:sum_count], refs[sum_count:]
-    first_out, first_in, second_out, second_in, mine, send_sem, recv_sem = refs
-    place = lax.axis_index("mp")
-    up, across = lax.div(place, 2), lax.rem(place, 2)
-    beside = up * 2 + (1 - across)
-    above = (1 - up) * 2 + across
-    corner = (1 - up) * 2 + (1 - across)
+    if pieces:
+        weight_out, refs = refs[0], refs[1:]
+    first_out, first_in, second_out, second_in, mine, send_sem, recv_sem = refs[:7]
+    loads = Loader(sources, refs[7 : 7 + len(sources)], refs[7 + len(sources)])
+    refs = refs[8 + len(sources) :]
+    for i in (2, 3, 0, 1)[4 - big :] if pieces else (0, 1):
+        loads.start(i)
+    for i in range(big, big + row_count):
+        loads.start(i)
+    lhs_ref, weight_ref = loads.targets[:2]
+    row_refs = loads.targets[big:]
+    square = Square()
+    spot, beside, above, corner, peers = (
+        square.spot, square.beside, square.above, square.corner, square.peers
+    )
+    targets = square.targets
+    if pieces:
+        sums = LineSum((loads.targets[2],), (loads.targets[3],), pieces, refs)
+        targets = targets + sums.targets
     share = mine.shape[0]
     half = mine.shape[1] // 2
     columns = 256
-    peers = (beside, above)
-
-    barrier = pltpu.get_barrier_semaphore()
-    for peer in peers:
-        pl.semaphore_signal(barrier, inc=1, device_id={"mp": peer}, device_id_type=MESH)
-    pl.semaphore_wait(barrier, 2)
+    greet(targets)
 
     def rows_of(owner):
         return pl.ds(pl.multiple_of(owner * share, 16), share)
 
-    def remote(source, target, slot, peer):
-        return pltpu.make_async_remote_copy(
-            src_ref=source,
-            dst_ref=target,
-            send_sem=send_sem.at[slot],
-            recv_sem=recv_sem.at[slot],
-            device_id={"mp": peer},
-            device_id_type=MESH,
-        )
+    def copy_to(source, target, slot, peer):
+        copy = remote(source, target, send_sem.at[slot], recv_sem.at[slot], {"mp": peer})
+        copy.start()
+        return copy
 
     def partial_into(owner, side, put):
         block = rows_of(owner)
@@ -120,19 +322,25 @@
 
         lax.fori_loop(0, half // columns, step, 0)
 
+    if pieces:
+        loads.got(2)
+        loads.got(3)
+        sums.step(0)
+    loads.got(0)
+    loads.got(1)
     copies = []
-    for order, targets in ((0, (corner, corner)), (1, (beside, above))):
+    for order, owners in ((0, (corner, corner)), (1, (beside, above))):
         for side in range(2):
 
             def put(at, there, part, side=side, order=order):
                 first_out[side, order, :, at] = part.astype(BF16)
 
-            partial_into(targets[side], side, put)
-            copy = remote(
-                first_out.at[side, order], first_in.at[side, order], side * 2 + order, peers[side]
+            partial_into(owners[side], side, put)
+            copies.append(
+                copy_to(
+                    first_out.at[side, order], first_in.at[side, order], side * 2 + order, peers[side]
+                )
             )
-            copy.start()
-            copies.append(copy)
 
     def put_mine(at, there, part):
         mine[:, there] = part
@@ -143,22 +351,23 @@
             second_out[side, :, at] = part.astype(BF16)
 
         partial_into(owner, side, put_on)
-    for side in range(2):
-        partial_into(place, side, put_mine)
-
     onward = []
     for side in range(2):
         copies[side].wait_recv()
         second_out[side] = (
             second_out[side].astype(F32) + first_in[side, 0].astype(F32)
         ).astype(BF16)
-        copy = remote(second_out.at[side], second_in.at[side], 4 + side, peers[1 - side])
-        copy.start()
-        onward.append(copy)
+        onward.append(copy_to(second_out.at[side], second_in.at[side], 4 + side, peers[1 - side]))
+    for side in range(2):
+        partial_into(spot, side, put_mine)
+    if pieces:
+        sums.steps(1, 2)
     for side in range(2):
         copies[2 + side].wait_recv()
     for side in range(2):
         onward[side].wait_recv()
+    for i in range(big, big + row_count):
+        loads.got(i)
 
     for sum_ref in sum_refs:
         sum_ref[...] = jnp.zeros_like(sum_ref)
@@ -174,11 +383,11 @@
             ],
             axis=1,
         )
-        wide, narrow, sums = post(total, tuple(r[at, :] for r in row_refs), gain_ref[...])
+        wide, narrow, terms = post(total, tuple(r[at, :] for r in row_refs), gain_ref[...])
         wide_ref[at, :] = wide
         if gather:
-            full_ref[pl.ds(pl.multiple_of(place * share + t * tile, 16), tile), :] = narrow
-        for sum_ref, term in zip(sum_refs, sums):
+            full_ref[pl.ds(pl.multiple_of(spot * share + t * tile, 16), tile), :] = narrow
+        for sum_ref, term in zip(sum_refs, terms):
             sum_ref[...] += term
         return carry
 
@@ -188,25 +397,35 @@
 
         def spread(owner, side, slot, peer):
             where = full_ref.at[rows_of(owner), pl.ds(side * half, half)]
-            copy = remote(where, where, slot, peer)
-            copy.start()
-            return copy
-
-        first = [spread(place, 0, 6, above), spread(place, 1, 7, beside)]
-        rest = [spread(place, 0, 8, beside), spread(place, 1, 9, above)]
+            return copy_to(where, where, slot, peer)
+
+        first = [spread(spot, 0, 6, above), spread(spot, 1, 7, beside)]
+        rest = [spread(spot, 0, 8, beside), spread(spot, 1, 9, above)]
         first[0].wait_recv()
         rest.append(spread(above, 0, 10, beside))
         first[1].wait_recv()
         rest.append(spread(beside, 1, 11, above))
+        if pieces:
+            sums.steps(2, 4)
         for copy in rest:
             copy.wait_recv()
         for copy in first + rest:
             copy.wait_send()
     for copy in copies + onward:
         copy.wait_send()
-
-
-def square_step(lhs, weight, dims, post, gain, rows_in, wide_type, sum_count, gather, ident):
+    if pieces:
+        for g in range(len(pieces)):
+            at = slice(g * sums.width, (g + 1) * sums.width)
+            if flip:
+                weight_out[at, :] = sums.collect(g).T
+            else:
+                weight_out[:, at] = sums.collect(g)
+        sums.settle()
+
+
+def square_step(
+    lhs, weight, dims, post, gain, rows_in, wide_type, sum_count, gather, ident, grads=(), flip=False
+):
     rows = lhs.shape[0]
     width = gain.shape[1]
     share = rows // 4
@@ -214,15 +433,23 @@
     if gather:
         outs.append(jax.ShapeDtypeStruct((rows, width), BF16))
     outs += [jax.ShapeDtypeStruct((1, width), F32)] * sum_count
+    pieces, extra = (), []
+    if grads:
+        pieces = tuple((0, 0, c) for c in range(0, grads[1].shape[1], LineSum.width))
+        kept = grads[0].shape[1] // 8
+        shape = (kept, grads[1].shape[1])
+        outs.append(jax.ShapeDtypeStruct(shape[::-1] if flip else shape, F32))
+        extra = LineSum.scratch(len(pieces), kept)
     half = width // 2
+    sources = (lhs, weight, *grads, *rows_in)
     vmem = pl.BlockSpec(memory_space=pltpu.VMEM)
     slots = 12 if gather else 6
     return pl.pallas_call(
         functools.partial(
-            square_kernel, post, dims, len(rows_in), sum_count, gather, 32
+            square_kernel, post, dims, len(rows_in), sum_count, gather, 32, pieces, flip
         ),
         out_shape=outs,
-        in_specs=[vmem] * (3 + len(rows_in)),
+        in_specs=[vmem] + [pl.BlockSpec(memory_space=pl.ANY)] * len(sources),
         out_specs=[vmem] * len(outs),
         scratch_shapes=[
             pltpu.VMEM((2, 2, share, half), BF16),
@@ -232,26 +459,209 @@
             pltpu.VMEM((share, width), F32),
             pltpu.SemaphoreType.DMA((slots,)),
             pltpu.SemaphoreType.DMA((slots,)),
-        ],
+        ]
+        + [pltpu.VMEM(a.shape, a.dtype) for a in sources]
+        + [pltpu.SemaphoreType.DMA((len(sources),))]
+        + extra,
         compiler_params=pltpu.CompilerParams(
             collective_id=ident, has_side_effects=True, vmem_limit_bytes=VMEM_BYTES
         ),
         cost_estimate=pl.CostEstimate(
-            flops=2 * rows * width * lhs.shape[1],
+            flops=60_000_000_000,
             bytes_accessed=2 * (lhs.size + weight.size + 6 * share * width),
             transcendentals=0,
         ),
-    )(lhs, weight, gain, *rows_in)
-
-
-def plain_step(lhs, weight, dims, post, gain, rows_in, wide_type, sum_count, gather, ident):
+    )(gain, *sources)
+
+
+def plain_step(lhs, weight, dims, post, gain, rows_in, wide_type, sum_count, gather, ident, grads=(), flip=False):
     part = product(lhs, weight, dims).astype(BF16)
     total = lax.psum_scatter(part, "mp", scatter_dimension=0, tiled=True).astype(F32)
     wide, narrow, sums = post(total, rows_in, gain)
     outs = [wide.astype(wide_type)]
     if gather:
         outs.append(lax.all_gather(narrow, "mp", axis=0, tiled=True))
-    return outs + list(sums)
+    outs += list(sums)
+    if grads:
+        outs.append(image_sum(rows_product(grads[0], grads[1])))
+        if flip:
+            outs[-1] = outs[-1].T
+    return outs
+
+
+def line_kernel(pieces, lhs_count, rhs_count, *refs):
+    sources, refs = refs[: lhs_count + rhs_count], refs[lhs_count + rhs_count :]
+    loads = Loader(sources, refs[-len(sources) - 1 : -1], refs[-1])
+    refs = refs[: -len(sources) - 1]
+    lhs_refs, rhs_refs = loads.targets[:lhs_count], loads.targets[lhs_count:]
+    for i in range(lhs_count):
+        loads.start(i)
+        loads.start(lhs_count + i)
+    small_ref, mixed_ref, caption_ref, base_ref = refs[:4]
+    in_out, self_out, query_out, cross_out, total_ref, mixed_out, caption_out = refs[4:11]
+    line_refs, refs = refs[11:19], refs[19:]
+    small_in, held, first_in, second_out, second_in = refs[:5]
+    small_send, small_recv, load_sem, flat_send, flat_recv = refs[5:]
+    square = Square()
+    spot, beside, above, corner, peers = (
+        square.spot, square.beside, square.above, square.corner, square.peers
+    )
+    sums = LineSum(lhs_refs, rhs_refs, pieces, line_refs, loads)
+    targets = [sums.targets[0]] + square.targets + sums.targets[1:]
+    width = sums.width
+    rows, columns = held.shape[2], held.shape[3]
+    greet(targets)
+
+    def block(job, owner, side):
+        if job == 0:
+            at = pl.ds(pl.multiple_of(owner * rows, 16), rows)
+            return mixed_ref.at[at, pl.ds(side * columns, columns)]
+        at = pl.ds(pl.multiple_of(owner * columns, 128), columns)
+        return caption_ref.at[pl.ds(side * rows, rows), at]
+
+    def load(job, slot, owner, side):
+        return pltpu.make_async_copy(
+            block(job, owner, side), held.at[job, slot], load_sem.at[job, slot]
+        )
+
+    def first_copy(job, side, order):
+        owner = corner if order == 0 else peers[side]
+        slot = side * 2 + order
+        return remote(
+            block(job, owner, side),
+            first_in.at[job, slot],
+            flat_send.at[job, slot],
+            flat_recv.at[job, slot],
+            {"mp": peers[side]},
+        )
+
+    def second_copy(job, side):
+        return remote(
+            second_out.at[job, side],
+            second_in.at[job, side],
+            flat_send.at[job, 4 + side],
+            flat_recv.at[job, 4 + side],
+            {"mp": peers[1 - side]},
+        )
+
+    def flat_start(job):
+        for order in range(2):
+            for side in range(2):
+                first_copy(job, side, order).start()
+        for side in range(2):
+            load(job, side, peers[1 - side], side).start()
+            load(job, 2 + side, spot, side).start()
+
+    def flat_forward(job):
+        for side in range(2):
+            load(job, side, peers[1 - side], side).wait()
+            first_copy(job, side, 0).wait_recv()
+            second_out[job, side] = (
+                held[job, side].astype(F32) + first_in[job, side * 2].astype(F32)
+            ).astype(BF16)
+            second_copy(job, side).start()
+
+    def flat_finish(job):
+        for side in range(2):
+            load(job, 2 + side, spot, side).wait()
+            first_copy(job, side, 1).wait_recv()
+            second_copy(job, side).wait_recv()
+            total = (
+                held[job, 2 + side].astype(F32)
+                + first_in[job, side * 2 + 1].astype(F32)
+                + second_in[job, side].astype(F32)
+            )
+            if job == 0:
+                at = slice(side * columns, (side + 1) * columns)
+                mixed_out[:, at] = (base_ref[:, at] + total).astype(BF16)
+            else:
+                caption_out[side * rows : (side + 1) * rows, :] = total
+        for side in range(2):
+            for order in range(2):
+                first_copy(job, side, order).wait_send()
+            second_copy(job, side).wait_send()
+
+    def small_step(slot, device):
+        copy = remote(
+            total_ref, small_in.at[slot], small_send.at[slot], small_recv.at[slot], device
+        )
+        copy.start()
+        return copy
+
+    total_ref[...] = small_ref[...]
+    flat_start(0)
+    flat_start(1)
+    sums.step(0)
+    flat_forward(0)
+    sums.steps(1, 3)
+    flat_forward(1)
+    for slot, device in enumerate(targets[:3]):
+        copy = small_step(slot, device)
+        copy.wait()
+        total_ref[...] += small_in[slot]
+    wide = [small_step(3 + j, device) for j, device in enumerate(targets[3:])]
+    sums.steps(3, 4)
+    flat_finish(0)
+    flat_finish(1)
+    for copy in wide:
+        copy.wait()
+    total_ref[...] += small_in[3] + small_in[4] + small_in[5]
+
+    places = ((in_out, 0), (in_out, 1), (in_out, 2), (self_out, None), (query_out, 0), (cross_out, None))
+    for g, (target, column) in enumerate(places):
+        done = sums.collect(g)
+        if column is None:
+            target[...] = done.T
+        else:
+            target[:, column * width : (column + 1) * width] = done
+    sums.settle()
+
+
+def line_sums(lhs_list, rhs_list, pieces, small, mixed_part, caption_part, base, ident):
+    width = 512
+    share = lhs_list[0].shape[1] // 8
+    count = len(pieces)
+    sources = (*lhs_list, *rhs_list)
+    rows, columns = base.shape[0], base.shape[1] // 2
+    outs = [
+        jax.ShapeDtypeStruct((share, 3 * width), F32),
+        jax.ShapeDtypeStruct((width, share), F32),
+        jax.ShapeDtypeStruct((share, width), F32),
+        jax.ShapeDtypeStruct((width, share), F32),
+        jax.ShapeDtypeStruct(small.shape, F32),
+        jax.ShapeDtypeStruct(base.shape, BF16),
+        jax.ShapeDtypeStruct((caption_part.shape[0], columns), F32),
+    ]
+    vmem = pl.BlockSpec(memory_space=pltpu.VMEM)
+    hbm = pl.BlockSpec(memory_space=pl.ANY)
+    dma = pltpu.SemaphoreType.DMA
+    return pl.pallas_call(
+        functools.partial(line_kernel, pieces, len(lhs_list), len(rhs_list)),
+        out_shape=outs,
+        in_specs=[hbm] * len(sources) + [vmem, hbm, hbm, vmem],
+        out_specs=[vmem] * len(outs),
+        scratch_shapes=LineSum.scratch(count, share)
+        + [
+            pltpu.VMEM((6,) + small.shape, F32),
+            pltpu.VMEM((2, 4, rows, columns), BF16),
+            pltpu.VMEM((2, 4, rows, columns), BF16),
+            pltpu.VMEM((2, 2, rows, columns), BF16),
+            pltpu.VMEM((2, 2, rows, columns), BF16),
+            dma((6,)),
+            dma((6,)),
+            dma((2, 4)),
+            dma((2, 6)),
+            dma((2, 6)),
+        ]
+        + [pltpu.VMEM(a.shape, a.dtype) for a in sources]
+        + [dma((len(sources),))],
+        compiler_params=pltpu.CompilerParams(
+            collective_id=ident, has_side_effects=True, vmem_limit_bytes=60 * 1024 * 1024
+        ),
+        cost_estimate=pl.CostEstimate(
+            flops=60_000_000_000, bytes_accessed=40_000_000, transcendentals=0
+        ),
+    )(*sources, small, mixed_part, caption_part, base)
 
 
 def softmax_rows(queries, keys_in):
@@ -326,7 +736,7 @@
 
 
 def body(
-    step,
+    square,
     tokens,
     caption,
     masked,
@@ -341,6 +751,7 @@
     feed_expand,
     feed_shrink,
 ):
+    step = square_step if square else plain_step
     axis_count = lax.axis_size("mp")
     axis_place = lax.axis_index("mp")
     images, length = masked.shape
@@ -352,11 +763,6 @@
 
     def own_rows(rows_in):
         return lax.dynamic_slice_in_dim(rows_in, axis_place * share_rows, share_rows, 0)
-
-    def image_sum(part, dimension):
-        return lax.psum_scatter(
-            part.astype(BF16), "img", scatter_dimension=dimension, tiled=True
-        ).astype(F32)
 
     gains = [norm_gains[k : k + 1] for k in range(3)]
     mask_column = (masked.reshape(rows_all, 1) > 0)
@@ -387,43 +793,61 @@
     own_feed_grad = own_rows(feed_grad).astype(F32)
     hidden = product(third_normed, feed_expand)
     active = gelu_exact(hidden).astype(BF16)
-    shrink_sum = image_sum(product(active, feed_grad, TN), 1)
     grad_active = product(feed_grad, feed_shrink, NT)
     _, gelu_pull = jax.vjp(gelu_exact, hidden)
     grad_hidden = gelu_pull(grad_active)[0].astype(BF16)
-    expand_sum = image_sum(product(third_normed, grad_hidden, TN), 0)
-    own_before_feed, cross_grad, third_gain = step(
-        grad_hidden, feed_expand, NT, post_backward, gains[2], (own_feed_grad, own_cross), F32, 1, True, 3
-    )
-
-    cross_out_sum = image_sum(product(cross_mixed, cross_grad, TN), 1)
+    own_before_feed, cross_grad, third_gain, shrink_sum = step(
+        grad_hidden, feed_expand, NT, post_backward, gains[2], (own_feed_grad, own_cross), F32, 1, True, 3,
+        (feed_grad, active), True,
+    )
+
     grad_cross_mixed = product(cross_grad, cross_out, NT).astype(BF16)
     grad_cross_queries, grad_text_pairs = attend_backward(
         images, heads_here, cross_queries, text_pairs, grad_cross_mixed
     )
-    cross_query_sum = image_sum(product(second_normed, grad_cross_queries, TN), 0)
-    cross_text_sum = image_sum(product(caption, grad_text_pairs, TN), 0)
-    caption_grad = lax.psum_scatter(
-        product(grad_text_pairs, weight_text, NT).astype(BF16), "mp", scatter_dimension=1, tiled=True
-    ).astype(F32)
-    own_before_cross, self_grad, second_gain = step(
-        grad_cross_queries, cross_query, NT, post_backward, gains[1], (own_before_feed, own_self), F32, 1, True, 4
-    )
-
-    self_out_sum = image_sum(product(self_mixed, self_grad, TN), 1)
+    caption_part = product(grad_text_pairs, weight_text, NT).astype(BF16)
+    own_before_cross, self_grad, second_gain, expand_sum = step(
+        grad_cross_queries, cross_query, NT, post_backward, gains[1], (own_before_feed, own_self), F32, 1, True, 4,
+        (third_normed, grad_hidden),
+    )
+
+    self_grad, grad_text_pairs = lax.optimization_barrier((self_grad, grad_text_pairs))
+    cross_text_sum = image_sum(rows_product(caption, grad_text_pairs))
     grad_self_mixed = product(self_grad, attention_out, NT).astype(BF16)
     grad_projected = attend_backward(images, heads_here, projected, projected, grad_self_mixed)
-    self_in_sum = image_sum(product(first_normed, grad_projected, TN), 0)
     tokens_grad, first_gain, embed_term = step(
         grad_projected, weight_in, NT, post_entry, gains[0],
         (own_before_cross, own_entry, own_float), F32, 2, False, 5,
     )
-    (mixed_out,) = step(
-        active, feed_shrink, NN, post_plain, gains[0], (own_cross,), BF16, 0, False, 6
-    )
-
-    small_terms = jnp.concatenate([first_gain, second_gain, third_gain, embed_term], axis=0)
-    small_sums = lax.psum_scatter(small_terms, ("img", "mp"), scatter_dimension=1, tiled=True)
+    terms = [first_gain, second_gain, third_gain, embed_term]
+    if square:
+        self_in_sum, self_out_sum, cross_query_sum, cross_out_sum, small_totals, mixed_out, caption_grad = line_sums(
+            [first_normed, self_grad, second_normed, cross_grad],
+            [grad_projected, self_mixed, grad_cross_queries, cross_mixed],
+            ((0, 0, 0), (0, 0, 512), (0, 0, 1024), (1, 1, 0), (2, 2, 0), (3, 3, 0)),
+            jnp.concatenate(terms + [jnp.zeros_like(embed_term)] * 4, axis=0),
+            product(active, feed_shrink).astype(BF16),
+            caption_part,
+            own_cross,
+            6,
+        )
+        slice_width = model_width // (lax.axis_size("img") * axis_count)
+        slice_at = (lax.axis_index("img") * axis_count + axis_place) * slice_width
+        small_sums = lax.dynamic_slice_in_dim(small_totals, slice_at, slice_width, 1)
+    else:
+        (mixed_out,) = step(
+            active, feed_shrink, NN, post_plain, gains[0], (own_cross,), BF16, 0, False, 0
+        )
+        caption_grad = lax.psum_scatter(
+            caption_part, "mp", scatter_dimension=1, tiled=True
+        ).astype(F32)
+        small_sums = lax.psum_scatter(
+            jnp.concatenate(terms, axis=0), ("img", "mp"), scatter_dimension=1, tiled=True
+        )
+        self_in_sum = image_sum(rows_product(first_normed, grad_projected))
+        self_out_sum = image_sum(rows_product(self_mixed, self_grad), 1)
+        cross_query_sum = image_sum(rows_product(second_normed, grad_cross_queries))
+        cross_out_sum = image_sum(rows_product(cross_mixed, cross_grad), 1)
     return (
         mixed_out,
         tokens_grad,
@@ -441,9 +865,9 @@
 
 
 def solution(mesh):
-    step = square_step if mesh.shape["mp"] == 4 else plain_step
+    square = mesh.shape["mp"] == 4 and mesh.shape["img"] == 8
     return jax.shard_map(
-        functools.partial(body, step),
+        functools.partial(body, square),
         mesh=mesh,
         in_specs=(
             P("img", None),

time: 1080 us -> 661 us (0.61)
  waiting for transfers between devices: 505 us -> 0.02 us
  Pallas kernels: 336 us -> 473 us
  matrix products: 128 us -> 91.3 us
  other arithmetic: 33.3 us -> 15.5 us
    reduce_scatter x8 -> x1, waiting for transfers between devices: 476 us -> 0.01 us  [image_sum(): lax.psum_scatter(part, 'img', scatter_dimension=dimension, tiled=True)]
    pallas_call x0 -> x1, Pallas kernels: none -> 116 us  [line_sums(): pl.pallas_call(functools.partial(line_kernel, pieces, len(lhs_list), len(...]
    dot_general x15 -> x10, matrix products: 128 us -> 91.3 us  [product(): return lax.dot_general(left, right, dims, preferred_element_type=F32)]
    unnamed x10 -> x1, waiting for transfers between devices: 29.2 us -> 0.02 us
    pallas_call x6 -> x5, Pallas kernels: 308 us -> 327 us  [square_step(): pl.pallas_call(functools.partial(square_kernel, post, dims, len(rows_in),...]
    convert_element_type x7 -> x1, other arithmetic: 19.7 us -> 3.01 us  [body(): first_normed = (first_unit * gains[0]).astype(BF16)]
    unnamed x61 -> x54, local copies, waits for them, and re-layouts: 40.1 us -> 41.6 us
  transfers between devices with their start and end apart: 9 -> 1, of which waited for: 9 -> 0; matrix products, arithmetic and copies ran while one was open for 9% -> 7% of each run, Pallas kernels for 3% -> 25%
where the time goes in v2:
time: 661 us; the launch traced here: 652 us
  Pallas kernels  473 us (72%)
  matrix products  91.3 us (14%)
  local copies, waits for them, and re-layouts  57.3 us (9%)
  other arithmetic  15.5 us (2%)
  between operations  14.5 us (2%)
    pallas_call x5, Pallas kernels, square_step(): pl.pallas_call(functools.partial(square_kernel, post, dims, len(rows_in),...  327 us
    pallas_call x1, Pallas kernels, line_sums(): pl.pallas_call(functools.partial(line_kernel, pieces, len(lhs_list), len(...  116 us
    dot_general x10, matrix products, product(): return lax.dot_general(left, right, dims, preferred_element_type=F32)  91.3 us
    unnamed x54, local copies, waits for them, and re-layouts  41.6 us
    pallas_call x2, Pallas kernels, attend_backward(): pl.pallas_call(functools.partial(attend_backward_kernel, heads, separate)...  19 us
  transfers between devices with their start and end apart: 1, of which 0 were waited for; matrix products, arithmetic and copies ran while one was open for 7% of the time, Pallas kernels for 25%

profile of v2, /device:TPU:0, one launch (start us, length us, event | category | flops | bytes accessed | tf_op | source)
XLA Modules:
  0.0 652.0 jit_solution(1244863236050400967)
XLA Ops:
  7.3 0.8 broadcast_compare_fusion
  8.1 0.8 fusion.30
  8.9 0.7 convert_element_type.53
  9.6 2.7 fusion.7
  12.2 2.9 multiply_reduce_fusion
  15.1 0.6 fusion.9
  15.8 8.9 %copy.28 = bf16[2048,3,512]{0,2,1:T(8,128)(2,1)} copy(bf16[2048,3,512]{2,0,1:T(8,128)(2,1)} %param.19) | data formatting | bytes 12582912 | tf_op args[6]
  24.7 3.0 multiply_convert_fusion.1.refs_0_
  27.7 1.6 copy-done.6
  29.3 6.4 convolution_convert_fusion.2.query_ref.pair_ref
  35.7 6.2 shard_map.220.refs_1_.refs_5_
  42.2 0.7 dynamic-slice_convert_fusion.1
  42.9 2.5 convert_select_fusion.1.refs_3_.refs_4_
  45.3 9.5 %copy.36 = bf16[512,8,2,512]{3,1,2,0:T(8,128)(2,1)} copy(bf16[512,8,2,512]{3,2,1,0:T(2,128)(2,1)} %bitcast.38) | data formatting | bytes 16777216
  55.1 1.7 copy-done.3
  56.8 1.3 dynamic-slice_convert_fusion.refs_5_
  58.1 64.5 %shard_map.221 = (f32[192,2048]{1,0:T(8,128)}, bf16[768,2048]{1,0:T(8,128)(2,1)}) custom-call(f32[1,2048]{1,0:T(1,128)} %get-tuple-element.94.refs_0_, bf16[768,512]{1,0:T(8,128)(2,1)} %shard_map.220.refs_1_.refs_5_, bf16[512,2048]{1,0:T(8,128)(2,1)} %refs_2_.4, f32[192,2048]{1,0:T(8,128)} %convert_select_fusion.1.refs_3_.refs_4_), custom_call_target="tpu_custom_call" | custom-call | flops 60000002048 | bytes 7602176 | tf_op jit(solution)/shard_map/pallas_call | solution.py:447
  122.6 4.7 convolution_convert_fusion.5.query_ref
  127.3 4.3 convolution_convert_fusion.6.pair_ref
  131.6 4.6 shard_map.222.refs_1_.refs_7_
  136.2 59.3 %shard_map.223 = (f32[192,2048]{1,0:T(8,128)}, bf16[768,2048]{1,0:T(8,128)(2,1)}) custom-call(f32[1,2048]{1,0:T(1,128)} %get-tuple-element.92.refs_0_, bf16[768,512]{1,0:T(8,128)(2,1)} %shard_map.222.refs_1_.refs_7_, bf16[512,2048]{1,0:T(8,128)(2,1)} %refs_2_.5, f32[192,2048]{1,0:T(8,128)} %get-tuple-element.39.refs_3_.refs_6_), custom_call_target="tpu_custom_call" | custom-call | flops 60000002048 | bytes 7602176 | tf_op jit(solution)/shard_map/pallas_call | solution.py:447
  195.5 24.4 %multiply_convert_fusion = (bf16[768,2048]{1,0:T(8,128)(2,1)}, f32[768,2048]{1,0:T(8,128)}, f32[768,2048]{1,0:T(8,128)}) fusion(bf16[768,2048]{1,0:T(8,128)(2,1)} %get-tuple-element.40.refs_3_, bf16[2048,2048]{1,0:T(8,128)(2,1)} %refs_2_.6), kind=kOutput, calls=%fused_computation.3 | convolution fusion | flops 6544687104 | bytes 27262976 | tf_op jit(solution)/shard_map/dot_general | solution.py:25
  219.9 15.2 %add_convert_fusion.refs_1_.refs_4_ = bf16[768,2048]{1,0:T(8,128)(2,1)} fusion(f32[768,2048]{1,0:T(8,128)} %get-tuple-element.89, f32[768,2048]{1,0:T(8,128)} %get-tuple-element.95, bf16[768,2048]{1,0:T(8,128)(2,1)S(1)} %copy-done.4, bf16[2048,2048]{1,0:T(8,128)(2,1)} %param.25), kind=kOutput, calls=%fused_computation.4 | convolution fusion | flops 6464471040 | bytes 27262976 | tf_op jit(solution)/shard_map/dot_general | solution.py:25
  235.2 83.6 %shard_map.224 = (f32[192,2048]{1,0:T(8,128)}, bf16[768,2048]{1,0:T(8,128)(2,1)}, f32[1,2048]{1,0:T(1,128)}, f32[2048,256]{1,0:T(8,128)}) custom-call(f32[1,2048]{1,0:T(1,128)} %get-tuple-element.92.refs_0_, bf16[768,2048]{1,0:T(8,128)(2,1)} %add_convert_fusion.refs_1_.refs_4_, bf16[2048,2048]{1,0:T(8,128)(2,1)} %refs_2_.6, bf16[768,2048]{1,0:T(8,128)(2,1)} %copy-done.3, ...), custom_call_target="tpu_custom_call" | custom-call | flops 60000002048 | bytes 16252928 | tf_op jit(solution)/shard_map/pallas_call | solution.py:447
  318.8 4.6 convolution_convert_fusion.4.grad_ref
  323.4 8.4 %shard_map.225 = (bf16[768,512]{1,0:T(8,128)(2,1)}, bf16[384,1024]{1,0:T(8,128)(2,1)}) custom-call(bf16[768,512]{1,0:T(8,128)(2,1)} %convolution_convert_fusion.5.query_ref, bf16[384,1024]{1,0:T(8,128)(2,1)} %convolution_convert_fusion.6.pair_ref, bf16[768,512]{1,0:T(8,128)(2,1)} %convolution_convert_fusion.4.grad_ref), custom_call_target="tpu_custom_call" | custom-call | tf_op jit(solution)/shard_map/pallas_call | solution.py:723
  331.8 81.6 %shard_map.226 = (f32[192,2048]{1,0:T(8,128)}, bf16[768,2048]{1,0:T(8,128)(2,1)}, f32[1,2048]{1,0:T(1,128)}, f32[256,2048]{1,0:T(8,128)}) custom-call(f32[1,2048]{1,0:T(1,128)} %get-tuple-element.94.refs_0_, bf16[768,512]{1,0:T(8,128)(2,1)} %get-tuple-element.43.refs_1_.refs_6_, bf16[2048,512]{1,0:T(8,128)(2,1)} %refs_2_.7, ...), custom_call_target="tpu_custom_call" | custom-call | flops 60000002048 | bytes 7602176 | tf_op jit(solution)/shard_map/pallas_call | solution.py:447
  413.4 6.7 %convert_bitcast_fusion = bf16[4096,1024]{0,1:T(8,128)(2,1)} fusion(bf16[384,1024]{1,0:T(8,128)(2,1)S(1)} %copy-done.18, bf16[384,4096]{1,0:T(8,128)(2,1)S(1)} %copy-done), kind=kOutput, calls=%fused_computation.1 | convolution fusion | flops 3225419776 | bytes 12320768 | tf_op jit(solution)/shard_map/dot_general | solution.py:25
  420.2 8.7 %copy.30.refs_2_ = bf16[2048,1536]{1,0:T(8,128)(2,1)} copy(bf16[2048,1536]{0,1:T(8,128)(2,1)} %bitcast.36) | data formatting | bytes 12582912 | tf_op jit(solution)/shard_map/reshape | solution.py:778
  428.9 5.2 convolution_convert_fusion.3.grad_ref
  434.1 10.6 %shard_map.227.refs_1_.refs_4_ = bf16[768,1536]{1,0:T(8,128)(2,1)} custom-call(bf16[768,1536]{1,0:T(8,128)(2,1)} %convolution_convert_fusion.2.query_ref.pair_ref, bf16[768,1536]{1,0:T(8,128)(2,1)} %convolution_convert_fusion.2.query_ref.pair_ref, bf16[768,512]{1,0:T(8,128)(2,1)} %convolution_convert_fusion.3.grad_ref), custom_call_target="tpu_custom_call" | custom-call | tf_op jit(solution)/shard_map/pallas_call | solution.py:723
  444.7 38.0 %shard_map.228 = (f32[192,2048]{1,0:T(8,128)}, f32[1,2048]{1,0:T(1,128)}, f32[1,2048]{1,0:T(1,128)}) custom-call(f32[1,2048]{1,0:T(1,128)} %copy-done.12, bf16[768,1536]{1,0:T(8,128)(2,1)} %shard_map.227.refs_1_.refs_4_, bf16[2048,1536]{1,0:T(8,128)(2,1)} %copy.30.refs_2_, f32[192,2048]{1,0:T(8,128)} %get-tuple-element.48.refs_3_, ...), custom_call_target="tpu_custom_call" | custom-call | flops 60000002048 | bytes 13369344 | tf_op jit(solution)/shard_map/pallas_call | solution.py:447
  482.7 1.4 concatenate.7.refs_8_
  484.1 9.0 %convolution_convert_fusion.refs_10_ = bf16[384,4096]{1,0:T(8,128)(2,1)} fusion(bf16[384,1024]{1,0:T(8,128)(2,1)} %get-tuple-element.60, bf16[4096,1024]{1,0:T(8,128)(2,1)} %bitcast.39), kind=kOutput, calls=%fused_computation.23 | convolution fusion | flops 3222798336 | bytes 12320768 | tf_op jit(solution)/shard_map/dot_general | solution.py:25
  493.1 10.8 %convolution_convert_fusion.1.refs_9_ = bf16[768,2048]{1,0:T(8,128)(2,1)} fusion(bf16[768,2048]{1,0:T(8,128)(2,1)S(1)} %copy-done.19, bf16[2048,2048]{1,0:T(8,128)(2,1)} %param.25), kind=kOutput, calls=%fused_computation.24 | convolution fusion | flops 6444023808 | bytes 14680064 | tf_op jit(solution)/shard_map/dot_general | solution.py:25
  503.9 116.5 %shard_map.229 = (f32[256,1536]{1,0:T(8,128)}, f32[512,256]{1,0:T(8,128)}, f32[256,512]{1,0:T(8,128)}, f32[512,256]{1,0:T(8,128)}, f32[8,2048]{1,0:T(8,128)}, /*...) custom-call(bf16[768,2048]{1,0:T(8,128)(2,1)} %copy-done.6, bf16[768,2048]{1,0:T(8,128)(2,1)} %get-tuple-element.47.refs_1_, ...), custom_call_target="tpu_custom_call" | custom-call | flops 60000002048 | bytes 40000000 | tf_op jit(solution)/shard_map/pallas_call | solution.py:638
  620.4 3.0 copy.31
  623.4 3.0 copy.32
  626.4 0.8 constant_dynamic-slice_fusion
  628.3 3.8 copy.33
  632.1 2.2 copy.45
  634.3 2.9 copy.46
  637.2 2.7 copy.47
  639.9 0.8 copy.48
  640.7 0.8 copy.49
  641.5 0.8 copy.50
  642.3 1.3 copy.51
  643.6 1.3 copy.52
  (50 shorter events, 1.8 us)
Async XLA Ops:
  7.2 120.1 %copy-start = (bf16[384,4096]{1,0:T(8,128)(2,1)S(1)}, bf16[384,4096]{1,0:T(8,128)(2,1)}, u32[]{:S(2)}) copy-start(bf16[384,4096]{1,0:T(8,128)(2,1)} %param.14) | copy-start | bytes 9437188
  7.2 7.9 %copy-start.13 = (f32[3,2048]{1,0:T(4,128)S(1)}, f32[3,2048]{1,0:T(4,128)}, u32[]{:S(2)}) copy-start(f32[3,2048]{1,0:T(4,128)} %param.18) | copy-start | bytes 73732
  7.2 621.1 %reduce-scatter.2.cloned.1.call-start = ((), (), s32[]{:S(2)}) async-start(), calls=%async_computation.1 | async-start | bytes 9437184 | tf_op jit(solution)/shard_map/reduce_scatter | solution.py:29
  15.8 8.9 %copy-start.12 = (f32[1,2048]{1,0:T(1,128)}, f32[1,2048]{1,0:T(1,128)S(1)}, u32[]{:S(2)}) copy-start(f32[1,2048]{1,0:T(1,128)S(1)} %get-tuple-element.93.refs_0_) | copy-start | bytes 24580
  24.7 4.7 copy-start.1
  27.7 1.6 copy-start.6
  45.3 9.5 %copy-start.5 = (bf16[768,2048]{1,0:T(8,128)(2,1)S(1)}, bf16[768,2048]{1,0:T(8,128)(2,1)}, u32[]{:S(2)}) copy-start(bf16[768,2048]{1,0:T(8,128)(2,1)} %param.16) | copy-start | bytes 9437188
  55.1 1.7 copy-start.3
  58.1 64.5 %copy-start.17 = (bf16[2048,512]{1,0:T(8,128)(2,1)S(1)}, bf16[2048,512]{1,0:T(8,128)(2,1)}, u32[]{:S(2)}) copy-start(bf16[2048,512]{1,0:T(8,128)(2,1)} %refs_2_.7) | copy-start | bytes 6291460
  122.6 4.7 copy-start.2
  195.5 24.4 %copy-start.4 = (bf16[768,2048]{1,0:T(8,128)(2,1)S(1)}, bf16[768,2048]{1,0:T(8,128)(2,1)}, u32[]{:S(2)}) copy-start(bf16[768,2048]{1,0:T(8,128)(2,1)} %copy-done.3) | copy-start | bytes 9437188
  235.1 83.7 %copy-start.16 = (bf16[512,2048]{1,0:T(8,128)(2,1)S(1)}, bf16[512,2048]{1,0:T(8,128)(2,1)}, u32[]{:S(2)}) copy-start(bf16[512,2048]{1,0:T(8,128)(2,1)} %refs_2_.5) | copy-start | bytes 6291460
  331.8 81.6 %copy-start.18 = (bf16[384,1024]{1,0:T(8,128)(2,1)S(1)}, bf16[384,1024]{1,0:T(8,128)(2,1)}, u32[]{:S(2)}) copy-start(bf16[384,1024]{1,0:T(8,128)(2,1)} %get-tuple-element.60) | copy-start | bytes 2359300
  444.7 38.0 %copy-start.14 = (f32[1,2048]{1,0:T(1,128)S(1)}, f32[1,2048]{1,0:T(1,128)}, u32[]{:S(2)}) copy-start(f32[1,2048]{1,0:T(1,128)} %get-tuple-element.51) | copy-start | bytes 24580
  444.7 38.0 %copy-start.15 = (f32[1,2048]{1,0:T(1,128)S(1)}, f32[1,2048]{1,0:T(1,128)}, u32[]{:S(2)}) copy-start(f32[1,2048]{1,0:T(1,128)} %get-tuple-element.50) | copy-start | bytes 24580
  484.1 9.0 %copy-start.19 = (bf16[768,2048]{1,0:T(8,128)(2,1)S(1)}, bf16[768,2048]{1,0:T(8,128)(2,1)}, u32[]{:S(2)}) copy-start(bf16[768,2048]{1,0:T(8,128)(2,1)} %get-tuple-element.88.refs_4_) | copy-start | bytes 9437188
  632.1 7.8 %copy-start.11 = (f32[512,256]{1,0:T(8,128)S(1)}, f32[512,256]{1,0:T(8,128)}, u32[]{:S(2)}) copy-start(f32[512,256]{1,0:T(8,128)} %get-tuple-element.114) | copy-start | bytes 1572868
  632.1 8.6 %copy-start.10 = (f32[256,512]{1,0:T(8,128)S(1)}, f32[256,512]{1,0:T(8,128)}, u32[]{:S(2)}) copy-start(f32[256,512]{1,0:T(8,128)} %get-tuple-element.115) | copy-start | bytes 1572868
  632.1 9.4 %copy-start.9 = (f32[512,256]{1,0:T(8,128)S(1)}, f32[512,256]{1,0:T(8,128)}, u32[]{:S(2)}) copy-start(f32[512,256]{1,0:T(8,128)} %get-tuple-element.117) | copy-start | bytes 1572868
  632.1 10.2 %copy-start.8 = (f32[256,2048]{1,0:T(8,128)S(1)}, f32[256,2048]{1,0:T(8,128)}, u32[]{:S(2)}) copy-start(f32[256,2048]{1,0:T(8,128)} %get-tuple-element.118) | copy-start | bytes 6291460
  634.3 9.3 %copy-start.7 = (f32[2048,256]{1,0:T(8,128)S(1)}, f32[2048,256]{1,0:T(8,128)}, u32[]{:S(2)}) copy-start(f32[2048,256]{1,0:T(8,128)} %get-tuple-element.119) | copy-start | bytes 6291460
Sparse Core Ops, SparseCore 0:
  420.3 88.5 reduce-scatter.1

commit v3 on v2

--- a/solution.py
+++ b/solution.py
@@ -1,5 +1,7 @@
+import dataclasses
 import functools
 import math
+from typing import Any
 
 import jax
 import jax.numpy as jnp
@@ -70,10 +72,6 @@
     return grad * (1.0 - mask), None, sums
 
 
-def post_plain(total, rows_in, gain):
-    return (rows_in[0] + total).astype(BF16), None, ()
-
-
 def remote(source, target, send, recv, device):
     return pltpu.make_async_remote_copy(
         src_ref=source,
@@ -126,9 +124,8 @@
 class LineSum:
     width = 512
 
-    def __init__(self, lhs_refs, rhs_refs, pieces, refs, loads=None):
-        self.loads = loads
-        self.lhs_refs, self.rhs_refs, self.pieces = lhs_refs, rhs_refs, pieces
+    def __init__(self, loads, pieces, refs):
+        self.loads, self.pieces = loads, pieces
         self.core_out, self.core_in, self.own, self.line_in = refs[:4]
         self.core_send, self.core_recv, self.line_send, self.line_recv = refs[4:]
         self.count = len(pieces)
@@ -184,10 +181,8 @@
 
     def multiply(self, g, k):
         lhs_at, rhs_at, column = self.pieces[g]
+        left, right = self.loads.got(lhs_at), self.loads.got(rhs_at)
         chunk = self.chunk_at(k)
-        if self.loads:
-            self.loads.got(lhs_at)
-            self.loads.got(len(self.lhs_refs) + rhs_at)
 
         @pl.when(k >= 2)
         def _():
@@ -197,8 +192,8 @@
             part = self.core if mine else 1 - self.core
             at = pl.ds(pl.multiple_of((chunk * 2 + part) * self.share, 128), self.share)
             done = product(
-                self.lhs_refs[lhs_at][:, at],
-                self.rhs_refs[rhs_at][:, column : column + self.width],
+                left[:, at],
+                right[:, column : column + self.width],
                 TN,
             ).astype(BF16)
             if mine:
@@ -268,35 +263,44 @@
         lax.fori_loop(0, 3, one, 0)
 
 
-def square_kernel(post, dims, row_count, sum_count, gather, tile, pieces, flip, *refs):
-    big = 4 if pieces else 2
-    gain_ref, sources, refs = refs[0], refs[1 : 1 + big + row_count], refs[1 + big + row_count :]
+def square_kernel(plan, *refs):
+    gain_ref, refs = refs[0], refs[1:]
+    given, refs = refs[: plan.given], refs[plan.given :]
     wide_ref, refs = refs[0], refs[1:]
-    if gather:
+    if plan.gather:
         full_ref, refs = refs[0], refs[1:]
-    sum_refs, refs = refs[:sum_count], refs[sum_count:]
-    if pieces:
-        weight_out, refs = refs[0], refs[1:]
+    sum_refs, refs = refs[: plan.sums], refs[plan.sums :]
+    weight_outs, refs = refs[: len(plan.grads)], refs[len(plan.grads) :]
+    if plan.side:
+        side_out, refs = refs[0], refs[1:]
     first_out, first_in, second_out, second_in, mine, send_sem, recv_sem = refs[:7]
+    sources = [
+        given[at] if span is None else given[at].at[:, span[0] : span[1]] for at, span in plan.loads
+    ]
     loads = Loader(sources, refs[7 : 7 + len(sources)], refs[7 + len(sources)])
     refs = refs[8 + len(sources) :]
-    for i in (2, 3, 0, 1)[4 - big :] if pieces else (0, 1):
-        loads.start(i)
-    for i in range(big, big + row_count):
-        loads.start(i)
+    pieces, gather, post, dims = plan.pieces, plan.gather, plan.post, plan.dims
+    lhs_at, weight_at, row_at = 0, 1, range(2, 2 + plan.rows)
+    for piece in pieces:
+        for i in piece[:2]:
+            if i not in loads.waiting:
+                loads.start(i)
+    for i in range(len(sources)):
+        if i not in loads.waiting:
+            loads.start(i)
     lhs_ref, weight_ref = loads.targets[:2]
-    row_refs = loads.targets[big:]
+    row_refs = loads.targets[2 : 2 + plan.rows]
     square = Square()
     spot, beside, above, corner, peers = (
         square.spot, square.beside, square.above, square.corner, square.peers
     )
     targets = square.targets
     if pieces:
-        sums = LineSum((loads.targets[2],), (loads.targets[3],), pieces, refs)
+        sums = LineSum(loads, pieces, refs)
         targets = targets + sums.targets
     share = mine.shape[0]
     half = mine.shape[1] // 2
-    columns = 256
+    columns, tile = 256, 32
     greet(targets)
 
     def rows_of(owner):
@@ -323,11 +327,9 @@
         lax.fori_loop(0, half // columns, step, 0)
 
     if pieces:
-        loads.got(2)
-        loads.got(3)
         sums.step(0)
-    loads.got(0)
-    loads.got(1)
+    loads.got(lhs_at)
+    loads.got(weight_at)
     copies = []
     for order, owners in ((0, (corner, corner)), (1, (beside, above))):
         for side in range(2):
@@ -366,7 +368,7 @@
         copies[2 + side].wait_recv()
     for side in range(2):
         onward[side].wait_recv()
-    for i in range(big, big + row_count):
+    for i in row_at:
         loads.got(i)
 
     for sum_ref in sum_refs:
@@ -393,6 +395,20 @@
 
     lax.fori_loop(0, share // tile, finish, 0)
 
+    def side_product():
+        left, right = (loads.got(i) for i in plan.side[:2])
+
+        def one(j, carry):
+            at = pl.ds(pl.multiple_of(j * columns, columns), columns)
+            if plan.side[2] == NT:
+                part = product(left[...], right[at, :], NT)
+            else:
+                part = product(left[...], right[:, at])
+            side_out[:, at] = part.astype(BF16)
+            return carry
+
+        lax.fori_loop(0, side_out.shape[1] // columns, one, 0)
+
     if gather:
 
         def spread(owner, side, slot, peer):
@@ -401,6 +417,8 @@
 
         first = [spread(spot, 0, 6, above), spread(spot, 1, 7, beside)]
         rest = [spread(spot, 0, 8, beside), spread(spot, 1, 9, above)]
+        if plan.side:
+            side_product()
         first[0].wait_recv()
         rest.append(spread(above, 0, 10, beside))
         first[1].wait_recv()
@@ -411,45 +429,97 @@
             copy.wait_recv()
         for copy in first + rest:
             copy.wait_send()
+    else:
+        if pieces:
+            sums.steps(2, 3)
+        if plan.side:
+            side_product()
+        if pieces:
+            sums.steps(3, 4)
     for copy in copies + onward:
         copy.wait_send()
     if pieces:
-        for g in range(len(pieces)):
-            at = slice(g * sums.width, (g + 1) * sums.width)
-            if flip:
-                weight_out[at, :] = sums.collect(g).T
-            else:
-                weight_out[:, at] = sums.collect(g)
+        g = 0
+        for out, (_, _, start, stop, flip) in zip(weight_outs, plan.grads):
+            for column in range(0, stop - start, sums.width):
+                at = slice(column, column + sums.width)
+                if flip:
+                    out[at, :] = sums.collect(g).T
+                else:
+                    out[:, at] = sums.collect(g)
+                g += 1
         sums.settle()
 
 
+@dataclasses.dataclass
+class Plan:
+    post: Any
+    dims: Any
+    rows: int
+    sums: int
+    gather: bool
+    given: int
+    loads: tuple
+    pieces: tuple
+    grads: tuple
+    side: Any
+
+
 def square_step(
-    lhs, weight, dims, post, gain, rows_in, wide_type, sum_count, gather, ident, grads=(), flip=False
+    lhs, weight, dims, post, gain, rows_in, wide_type, sum_count, gather, ident, grads=(), side=None
 ):
     rows = lhs.shape[0]
     width = gain.shape[1]
     share = rows // 4
+    given, loads, shapes = [], [], []
+
+    def operand(array, span=None):
+        at = next((i for i, a in enumerate(given) if a is array), None)
+        if at is None:
+            at = len(given)
+            given.append(array)
+        if span == (0, array.shape[1]):
+            span = None
+        for i, entry in enumerate(loads):
+            if entry[0] == at and entry[1] in (span, None):
+                return i, 0 if entry[1] == span else span[0]
+        loads.append((at, span))
+        stretch = array.shape[1] if span is None else span[1] - span[0]
+        shapes.append(pltpu.VMEM((array.shape[0], stretch), array.dtype))
+        return len(loads) - 1, 0
+
+    for array in (lhs, weight, *rows_in):
+        operand(array)
     outs = [jax.ShapeDtypeStruct((share, width), wide_type)]
     if gather:
         outs.append(jax.ShapeDtypeStruct((rows, width), BF16))
     outs += [jax.ShapeDtypeStruct((1, width), F32)] * sum_count
-    pieces, extra = (), []
-    if grads:
-        pieces = tuple((0, 0, c) for c in range(0, grads[1].shape[1], LineSum.width))
-        kept = grads[0].shape[1] // 8
-        shape = (kept, grads[1].shape[1])
+    side_plan = None
+    if side:
+        side_plan = (operand(side[0])[0], operand(side[1])[0], side[2])
+    pieces, extra = [], []
+    for left, right, start, stop, flip in grads:
+        at, _ = operand(left)
+        to, shift = operand(right, (start, stop))
+        pieces += [(at, to, shift + c) for c in range(0, stop - start, LineSum.width)]
+        kept = left.shape[1] // 8
+        shape = (kept, stop - start)
         outs.append(jax.ShapeDtypeStruct(shape[::-1] if flip else shape, F32))
         extra = LineSum.scratch(len(pieces), kept)
+    if side:
+        wide = side[1].shape[0] if side[2] == NT else side[1].shape[1]
+        outs.append(jax.ShapeDtypeStruct((side[0].shape[0], wide), BF16))
+    plan = Plan(
+        post, dims, len(rows_in), sum_count, gather, len(given), tuple(loads), tuple(pieces),
+        tuple((0, 0) + tuple(g[2:]) for g in grads), side_plan,
+    )
     half = width // 2
-    sources = (lhs, weight, *grads, *rows_in)
     vmem = pl.BlockSpec(memory_space=pltpu.VMEM)
     slots = 12 if gather else 6
     return pl.pallas_call(
-        functools.partial(
-            square_kernel, post, dims, len(rows_in), sum_count, gather, 32, pieces, flip
-        ),
+        functools.partial(square_kernel, plan),
         out_shape=outs,
-        in_specs=[vmem] + [pl.BlockSpec(memory_space=pl.ANY)] * len(sources),
+        in_specs=[vmem] + [pl.BlockSpec(memory_space=pl.ANY)] * len(given),
         out_specs=[vmem] * len(outs),
         scratch_shapes=[
             pltpu.VMEM((2, 2, share, half), BF16),
@@ -460,8 +530,8 @@
             pltpu.SemaphoreType.DMA((slots,)),
             pltpu.SemaphoreType.DMA((slots,)),
         ]
-        + [pltpu.VMEM(a.shape, a.dtype) for a in sources]
-        + [pltpu.SemaphoreType.DMA((len(sources),))]
+        + shapes
+        + [pltpu.SemaphoreType.DMA((len(loads),))]
         + extra,
         compiler_params=pltpu.CompilerParams(
             collective_id=ident, has_side_effects=True, vmem_limit_bytes=VMEM_BYTES
@@ -471,10 +541,10 @@
             bytes_accessed=2 * (lhs.size + weight.size + 6 * share * width),
             transcendentals=0,
         ),
-    )(gain, *sources)
-
-
-def plain_step(lhs, weight, dims, post, gain, rows_in, wide_type, sum_count, gather, ident, grads=(), flip=False):
+    )(gain, *given)
+
+
+def plain_step(lhs, weight, dims, post, gain, rows_in, wide_type, sum_count, gather, ident, grads=(), side=None):
     part = product(lhs, weight, dims).astype(BF16)
     total = lax.psum_scatter(part, "mp", scatter_dimension=0, tiled=True).astype(F32)
     wide, narrow, sums = post(total, rows_in, gain)
@@ -482,10 +552,11 @@
     if gather:
         outs.append(lax.all_gather(narrow, "mp", axis=0, tiled=True))
     outs += list(sums)
-    if grads:
-        outs.append(image_sum(rows_product(grads[0], grads[1])))
-        if flip:
-            outs[-1] = outs[-1].T
+    for left, right, start, stop, flip in grads:
+        done = image_sum(rows_product(left, right[:, start:stop]))
+        outs.append(done.T if flip else done)
+    if side:
+        outs.append(product(*side).astype(BF16))
     return outs
 
 
@@ -493,69 +564,85 @@
     sources, refs = refs[: lhs_count + rhs_count], refs[lhs_count + rhs_count :]
     loads = Loader(sources, refs[-len(sources) - 1 : -1], refs[-1])
     refs = refs[: -len(sources) - 1]
-    lhs_refs, rhs_refs = loads.targets[:lhs_count], loads.targets[lhs_count:]
     for i in range(lhs_count):
         loads.start(i)
         loads.start(lhs_count + i)
-    small_ref, mixed_ref, caption_ref, base_ref = refs[:4]
-    in_out, self_out, query_out, cross_out, total_ref, mixed_out, caption_out = refs[4:11]
-    line_refs, refs = refs[11:19], refs[19:]
+    small_ref, mixed_ref, caption_ref, tokens_ref = refs[:4]
+    in_out, self_out, query_out, cross_out, total_ref, mixed_out, caption_out, tokens_out = refs[4:12]
+    line_refs, refs = refs[12:20], refs[20:]
     small_in, held, first_in, second_out, second_in = refs[:5]
-    small_send, small_recv, load_sem, flat_send, flat_recv = refs[5:]
+    small_send, small_recv, load_sem, flat_send, flat_recv, move_sem, move_send, move_recv = refs[5:]
     square = Square()
     spot, beside, above, corner, peers = (
         square.spot, square.beside, square.above, square.corner, square.peers
     )
-    sums = LineSum(lhs_refs, rhs_refs, pieces, line_refs, loads)
-    targets = [sums.targets[0]] + square.targets + sums.targets[1:]
+    sums = LineSum(loads, pieces, line_refs)
+    targets = [sums.targets[0]] + square.targets + sums.targets[1:] + [{"mp": corner}]
     width = sums.width
     rows, columns = held.shape[2], held.shape[3]
     greet(targets)
 
-    def block(job, owner, side):
+    low = rows // 3
+
+    def row_block(owner, j):
+        return owner * 3 + j
+
+    def block(job, owner, side, j):
         if job == 0:
-            at = pl.ds(pl.multiple_of(owner * rows, 16), rows)
+            b = row_block(owner, j)
+            at = pl.ds(pl.multiple_of((lax.rem(b, 4) * 3 + lax.div(b, 4)) * low, low), low)
             return mixed_ref.at[at, pl.ds(side * columns, columns)]
         at = pl.ds(pl.multiple_of(owner * columns, 128), columns)
-        return caption_ref.at[pl.ds(side * rows, rows), at]
+        return caption_ref.at[pl.ds(side * rows + j * low, low), at]
+
+    thirds = [pl.ds(j * low, low) for j in range(3)]
 
     def load(job, slot, owner, side):
-        return pltpu.make_async_copy(
-            block(job, owner, side), held.at[job, slot], load_sem.at[job, slot]
-        )
+        return [
+            pltpu.make_async_copy(
+                block(job, owner, side, j), held.at[job, slot, thirds[j]], load_sem.at[job, slot, j]
+            )
+            for j in range(3)
+        ]
 
     def first_copy(job, side, order):
         owner = corner if order == 0 else peers[side]
         slot = side * 2 + order
-        return remote(
-            block(job, owner, side),
-            first_in.at[job, slot],
-            flat_send.at[job, slot],
-            flat_recv.at[job, slot],
-            {"mp": peers[side]},
-        )
+        return [
+            remote(
+                block(job, owner, side, j),
+                first_in.at[job, slot, thirds[j]],
+                flat_send.at[job, slot, j],
+                flat_recv.at[job, slot, j],
+                {"mp": peers[side]},
+            )
+            for j in range(3)
+        ]
 
     def second_copy(job, side):
         return remote(
             second_out.at[job, side],
             second_in.at[job, side],
-            flat_send.at[job, 4 + side],
-            flat_recv.at[job, 4 + side],
+            flat_send.at[job, 4 + side, 0],
+            flat_recv.at[job, 4 + side, 0],
             {"mp": peers[1 - side]},
         )
 
     def flat_start(job):
         for order in range(2):
             for side in range(2):
-                first_copy(job, side, order).start()
+                for copy in first_copy(job, side, order):
+                    copy.start()
         for side in range(2):
-            load(job, side, peers[1 - side], side).start()
-            load(job, 2 + side, spot, side).start()
+            for copy in load(job, side, peers[1 - side], side) + load(job, 2 + side, spot, side):
+                copy.start()
 
     def flat_forward(job):
         for side in range(2):
-            load(job, side, peers[1 - side], side).wait()
-            first_copy(job, side, 0).wait_recv()
+            for copy in load(job, side, peers[1 - side], side):
+                copy.wait()
+            for copy in first_copy(job, side, 0):
+                copy.wait_recv()
             second_out[job, side] = (
                 held[job, side].astype(F32) + first_in[job, side * 2].astype(F32)
             ).astype(BF16)
@@ -563,8 +650,10 @@
 
     def flat_finish(job):
         for side in range(2):
-            load(job, 2 + side, spot, side).wait()
-            first_copy(job, side, 1).wait_recv()
+            for copy in load(job, 2 + side, spot, side):
+                copy.wait()
+            for copy in first_copy(job, side, 1):
+                copy.wait_recv()
             second_copy(job, side).wait_recv()
             total = (
                 held[job, 2 + side].astype(F32)
@@ -572,14 +661,57 @@
                 + second_in[job, side].astype(F32)
             )
             if job == 0:
-                at = slice(side * columns, (side + 1) * columns)
-                mixed_out[:, at] = (base_ref[:, at] + total).astype(BF16)
+                mixed_out[:, side * columns : (side + 1) * columns] = total.astype(BF16)
             else:
                 caption_out[side * rows : (side + 1) * rows, :] = total
         for side in range(2):
             for order in range(2):
-                first_copy(job, side, order).wait_send()
+                for copy in first_copy(job, side, order):
+                    copy.wait_send()
             second_copy(job, side).wait_send()
+
+    def move(i):
+        b = i * 4 + spot
+        keeper, j = lax.div(b, 3), lax.rem(b, 3)
+        target = tokens_out.at[pl.ds(pl.multiple_of(j * low, low), low)]
+        away = remote(
+            tokens_ref.at[i], target, move_send.at[i], move_recv.at[j], {"mp": keeper}
+        )
+        here = pltpu.make_async_copy(tokens_ref.at[i], target, move_sem.at[0])
+        return keeper, away, here
+
+    def move_start():
+        for i in range(3):
+            keeper, away, here = move(i)
+
+            @pl.when(keeper != spot)
+            def _():
+                away.start()
+
+            @pl.when(keeper == spot)
+            def _():
+                here.start()
+
+    def move_finish():
+        for i in range(3):
+            keeper, away, here = move(i)
+
+            @pl.when(keeper != spot)
+            def _():
+                away.wait_send()
+
+            @pl.when(keeper == spot)
+            def _():
+                here.wait()
+
+        for j in range(3):
+            arrival = remote(
+                tokens_ref.at[0], tokens_out.at[thirds[j]], move_send.at[0], move_recv.at[j], {"mp": corner}
+            )
+
+            @pl.when(lax.rem(row_block(spot, j), 4) != spot)
+            def _():
+                arrival.wait_recv()
 
     def small_step(slot, device):
         copy = remote(
@@ -591,6 +723,7 @@
     total_ref[...] = small_ref[...]
     flat_start(0)
     flat_start(1)
+    move_start()
     sums.step(0)
     flat_forward(0)
     sums.steps(1, 3)
@@ -599,10 +732,11 @@
         copy = small_step(slot, device)
         copy.wait()
         total_ref[...] += small_in[slot]
-    wide = [small_step(3 + j, device) for j, device in enumerate(targets[3:])]
+    wide = [small_step(3 + j, device) for j, device in enumerate(targets[3:6])]
     sums.steps(3, 4)
     flat_finish(0)
     flat_finish(1)
+    move_finish()
     for copy in wide:
         copy.wait()
     total_ref[...] += small_in[3] + small_in[4] + small_in[5]
@@ -617,20 +751,22 @@
     sums.settle()
 
 
-def line_sums(lhs_list, rhs_list, pieces, small, mixed_part, caption_part, base, ident):
+def line_sums(lhs_list, rhs_list, pieces, small, mixed_part, caption_part, tokens_rows, ident):
     width = 512
     share = lhs_list[0].shape[1] // 8
     count = len(pieces)
     sources = (*lhs_list, *rhs_list)
-    rows, columns = base.shape[0], base.shape[1] // 2
+    images, low, full = tokens_rows.shape
+    rows, columns = images * low, full // 2
     outs = [
         jax.ShapeDtypeStruct((share, 3 * width), F32),
         jax.ShapeDtypeStruct((width, share), F32),
         jax.ShapeDtypeStruct((share, width), F32),
         jax.ShapeDtypeStruct((width, share), F32),
         jax.ShapeDtypeStruct(small.shape, F32),
-        jax.ShapeDtypeStruct(base.shape, BF16),
+        jax.ShapeDtypeStruct((rows, full), BF16),
         jax.ShapeDtypeStruct((caption_part.shape[0], columns), F32),
+        jax.ShapeDtypeStruct((rows, full), F32),
     ]
     vmem = pl.BlockSpec(memory_space=pltpu.VMEM)
     hbm = pl.BlockSpec(memory_space=pl.ANY)
@@ -638,7 +774,7 @@
     return pl.pallas_call(
         functools.partial(line_kernel, pieces, len(lhs_list), len(rhs_list)),
         out_shape=outs,
-        in_specs=[hbm] * len(sources) + [vmem, hbm, hbm, vmem],
+        in_specs=[hbm] * len(sources) + [vmem, hbm, hbm, hbm],
         out_specs=[vmem] * len(outs),
         scratch_shapes=LineSum.scratch(count, share)
         + [
@@ -649,9 +785,12 @@
             pltpu.VMEM((2, 2, rows, columns), BF16),
             dma((6,)),
             dma((6,)),
-            dma((2, 4)),
-            dma((2, 6)),
-            dma((2, 6)),
+            dma((2, 4, 3)),
+            dma((2, 6, 3)),
+            dma((2, 6, 3)),
+            dma((1,)),
+            dma((3,)),
+            dma((3,)),
         ]
         + [pltpu.VMEM(a.shape, a.dtype) for a in sources]
         + [dma((len(sources),))],
@@ -661,7 +800,7 @@
         cost_estimate=pl.CostEstimate(
             flops=60_000_000_000, bytes_accessed=40_000_000, transcendentals=0
         ),
-    )(*sources, small, mixed_part, caption_part, base)
+    )(*sources, small, mixed_part, caption_part, tokens_rows)
 
 
 def softmax_rows(queries, keys_in):
@@ -670,65 +809,395 @@
     return powers * (1.0 / jnp.sum(powers, axis=-1, keepdims=True))
 
 
+def image_rows(ref, i, columns=slice(None)):
+    part = ref[:, i, :, columns]
+    return part.reshape(part.shape[0] * part.shape[1], part.shape[2])
+
+
+def put_image(ref, i, columns, value):
+    ref[:, i, :, columns] = value.reshape(ref.shape[0], ref.shape[2], value.shape[1])
+
+
+def tile_at(j, wide):
+    return pl.ds(pl.multiple_of(j * wide, wide), wide)
+
+
+def attend(queries, keys_in, values_in):
+    probs = softmax_rows(queries, keys_in).astype(BF16)
+    return product(probs, values_in).astype(BF16)
+
+
 def attend_forward_kernel(heads, separate, query_ref, pair_ref, out_ref):
     key_at = 0 if separate else heads
-    for h in range(heads):
-        queries = query_ref[:, h * HDIM : (h + 1) * HDIM]
-        keys_in = pair_ref[:, (key_at + h) * HDIM : (key_at + h + 1) * HDIM]
-        values_in = pair_ref[:, (key_at + heads + h) * HDIM : (key_at + heads + h + 1) * HDIM]
-        probs = softmax_rows(queries, keys_in).astype(BF16)
-        out_ref[:, h * HDIM : (h + 1) * HDIM] = product(probs, values_in).astype(BF16)
+
+    def one(h, carry):
+        own, key, value = (tile_at(h + n, HDIM) for n in (0, key_at, key_at + heads))
+        done = attend(image_rows(query_ref, 0, own), image_rows(pair_ref, 0, key), image_rows(pair_ref, 0, value))
+        put_image(out_ref, 0, own, done)
+        return carry
+
+    lax.fori_loop(0, heads, one, 0)
+
+
+def attend_backward_head(queries, keys_in, values_in, grad):
+    probs = softmax_rows(queries, keys_in)
+    grad_values = product(probs.astype(BF16), grad, TN).astype(BF16)
+    grad_probs = product(grad, values_in, NT)
+    centred = grad_probs - jnp.sum(probs * grad_probs, axis=-1, keepdims=True)
+    grad_scores = (probs * centred * SCALE).astype(BF16)
+    grad_queries = product(grad_scores, keys_in).astype(BF16)
+    grad_keys = product(grad_scores, queries, TN).astype(BF16)
+    return grad_queries, grad_keys, grad_values
 
 
 def attend_backward_kernel(heads, separate, query_ref, pair_ref, grad_ref, *outs):
     key_at = 0 if separate else heads
     query_out, pair_out = outs if separate else (outs[0], outs[0])
     for h in range(heads):
-        own = slice(h * HDIM, (h + 1) * HDIM)
-        key_slice = slice((key_at + h) * HDIM, (key_at + h + 1) * HDIM)
-        value_slice = slice((key_at + heads + h) * HDIM, (key_at + heads + h + 1) * HDIM)
-        queries, keys_in, values_in = query_ref[:, own], pair_ref[:, key_slice], pair_ref[:, value_slice]
-        grad = grad_ref[:, own]
-        probs = softmax_rows(queries, keys_in)
-        pair_out[:, value_slice] = product(probs.astype(BF16), grad, TN).astype(BF16)
-        grad_probs = product(grad, values_in, NT)
-        centred = grad_probs - jnp.sum(probs * grad_probs, axis=-1, keepdims=True)
-        grad_scores = (probs * centred * SCALE).astype(BF16)
-        query_out[:, own] = product(grad_scores, keys_in).astype(BF16)
-        pair_out[:, key_slice] = product(grad_scores, queries, TN).astype(BF16)
-
-
-def image_blocks(images, *arrays):
-    return [pl.BlockSpec((a.shape[0] // images, a.shape[1]), lambda i: (i, 0)) for a in arrays]
-
-
-def attend_forward(images, heads, queries, pairs):
+        own, key, value = (slice((h + n) * HDIM, (h + n + 1) * HDIM) for n in (0, key_at, key_at + heads))
+        done = attend_backward_head(
+            image_rows(query_ref, 0, own),
+            image_rows(pair_ref, 0, key),
+            image_rows(pair_ref, 0, value),
+            image_rows(grad_ref, 0, own),
+        )
+        put_image(query_out, 0, own, done[0])
+        put_image(pair_out, 0, key, done[1])
+        put_image(pair_out, 0, value, done[2])
+
+
+def image_blocks(*arrays):
+    return [
+        pl.BlockSpec((a.shape[0], 1) + tuple(a.shape[2:]), lambda i: (0, i, 0, 0)) for a in arrays
+    ]
+
+
+def attend_forward(heads, queries, pairs):
     separate = queries is not pairs
-    out = jax.ShapeDtypeStruct((queries.shape[0], heads * HDIM), BF16)
+    out = jax.ShapeDtypeStruct(queries.shape[:3] + (heads * HDIM,), BF16)
     return pl.pallas_call(
         functools.partial(attend_forward_kernel, heads, separate),
-        grid=(images,),
+        grid=(queries.shape[1],),
         out_shape=out,
-        in_specs=image_blocks(images, queries, pairs),
-        out_specs=image_blocks(images, out)[0],
+        in_specs=image_blocks(queries, pairs),
+        out_specs=image_blocks(out)[0],
         compiler_params=pltpu.CompilerParams(vmem_limit_bytes=VMEM_BYTES),
     )(queries, pairs)
 
 
-def attend_backward(images, heads, queries, pairs, grad):
+def attend_backward(heads, queries, pairs, grad):
     separate = queries is not pairs
     outs = [jax.ShapeDtypeStruct(queries.shape, BF16)]
     if separate:
         outs.append(jax.ShapeDtypeStruct(pairs.shape, BF16))
     result = pl.pallas_call(
         functools.partial(attend_backward_kernel, heads, separate),
-        grid=(images,),
+        grid=(queries.shape[1],),
         out_shape=outs,
-        in_specs=image_blocks(images, queries, pairs, grad),
-        out_specs=image_blocks(images, *outs),
+        in_specs=image_blocks(queries, pairs, grad),
+        out_specs=image_blocks(*outs),
         compiler_params=pltpu.CompilerParams(vmem_limit_bytes=VMEM_BYTES),
     )(queries, pairs, grad)
     return result if separate else result[0]
+
+
+class ImageSum:
+    def __init__(self, square, part, first_in, second_out, second_in, send_sem, recv_sem):
+        self.square, self.part = square, part
+        self.first_in, self.second_out, self.second_in = first_in, second_out, second_in
+        self.send_sem, self.recv_sem = send_sem, recv_sem
+        self.half = part.shape[2] // 2
+        self.summing, self.spreading = [], []
+
+    def copy_to(self, kept, source, target, slot, peer):
+        copy = remote(
+            source, target, self.send_sem.at[slot], self.recv_sem.at[slot], {"mp": peer}
+        )
+        copy.start()
+        kept.append(copy)
+
+    def columns(self, side):
+        return pl.ds(side * self.half, self.half)
+
+    def start(self):
+        square = self.square
+        for order in range(2):
+            for side in range(2):
+                owner = square.peers[side] if order else square.corner
+                self.copy_to(
+                    self.summing,
+                    self.part.at[owner, :, self.columns(side)],
+                    self.first_in.at[side, order],
+                    side * 2 + order,
+                    square.peers[side],
+                )
+
+    def forward(self):
+        square = self.square
+        for side in range(2):
+            self.summing[side].wait_recv()
+            own = self.part[square.peers[1 - side], :, self.columns(side)]
+            self.second_out[side] = (
+                own.astype(F32) + self.first_in[side, 0].astype(F32)
+            ).astype(BF16)
+            self.copy_to(
+                self.summing, self.second_out.at[side], self.second_in.at[side], 4 + side,
+                square.peers[1 - side],
+            )
+
+    def arrived(self):
+        for copy in self.summing[2:]:
+            copy.wait_recv()
+
+    def total(self, at):
+        return jnp.concatenate(
+            [
+                self.part[self.square.spot, at, self.columns(side)].astype(F32)
+                + self.first_in[side, 1, at, :].astype(F32)
+                + self.second_in[side, at, :].astype(F32)
+                for side in range(2)
+            ],
+            axis=1,
+        )
+
+    def sent(self):
+        for copy in self.summing:
+            copy.wait_send()
+
+    def spread(self, full, owner, side, slot, peer):
+        where = full.at[owner, :, self.columns(side)]
+        self.copy_to(self.spreading, where, where, slot, peer)
+
+    def gather(self, full):
+        square = self.square
+        for slot, side, peer in ((6, 0, 1), (7, 1, 0), (8, 0, 0), (9, 1, 1)):
+            self.spread(full, square.spot, side, slot, square.peers[peer])
+
+    def pass_on(self, full):
+        square = self.square
+        self.spreading[0].wait_recv()
+        self.spread(full, square.above, 0, 10, square.beside)
+        self.spreading[1].wait_recv()
+        self.spread(full, square.beside, 1, 11, square.above)
+
+    def gathered(self):
+        for copy in self.spreading[2:]:
+            copy.wait_recv()
+
+    def spread_sent(self):
+        for copy in self.spreading:
+            copy.wait_send()
+
+    @staticmethod
+    def scratch(stages, images, block, width):
+        dma = pltpu.SemaphoreType.DMA
+        lead = (stages, images)
+        return [
+            pltpu.VMEM((images, 4, block, width), BF16),
+            pltpu.VMEM(lead + (2, 2, block, width // 2), BF16),
+            pltpu.VMEM(lead + (2, block, width // 2), BF16),
+            pltpu.VMEM(lead + (2, block, width // 2), BF16),
+            dma(lead + (12,)),
+            dma(lead + (12,)),
+        ]
+
+
+def forward_kernel(*refs):
+    gains_ref, refs = refs[0], refs[1:]
+    given, refs = refs[:9], refs[9:]
+    self_mixed, second_normed, queries_ref, cross_mixed, third_normed, active, grad_hidden = refs[:7]
+    own_self, own_cross = refs[7:9]
+    loads = Loader(given[:8], refs[9:17], refs[17])
+    shrink_ref = given[8]
+    tiles, tile_sem = refs[18:20]
+    part, first_in, second_out, second_in, send_sem, recv_sem = refs[20:]
+    images = own_self.shape[0]
+    heads = self_mixed.shape[3] // HDIM
+    for i in range(8):
+        loads.start(i)
+    square = Square()
+    wide = 256
+
+    def shrink_load(j):
+        slot = lax.rem(j, 2)
+        return pltpu.make_async_copy(
+            shrink_ref.at[tile_at(j, wide), :], tiles.at[slot], tile_sem.at[slot]
+        )
+
+    shrink_load(0).start()
+    greet(square.targets)
+    jobs = [
+        [
+            ImageSum(
+                square, part.at[i], first_in.at[t, i], second_out.at[t, i], second_in.at[t, i],
+                send_sem.at[t, i], recv_sem.at[t, i],
+            )
+            for i in range(images)
+        ]
+        for t in range(2)
+    ]
+
+    def project(i, left, weight):
+        def one(j, carry):
+            at = tile_at(j, wide)
+            done = product(left, weight[:, at]).astype(BF16)
+            part[i, :, :, at] = done.reshape(part.shape[1], part.shape[2], wide)
+            return carry
+
+        lax.fori_loop(0, part.shape[3] // wide, one, 0)
+
+    def self_stage(i):
+        projected = loads.got(0)
+
+        def one(h, carry):
+            own, key, value = (tile_at(h + n * heads, HDIM) for n in range(3))
+            done = attend(
+                image_rows(projected, i, own),
+                image_rows(projected, i, key),
+                image_rows(projected, i, value),
+            )
+            put_image(self_mixed, i, own, done)
+            return carry
+
+        lax.fori_loop(0, heads, one, 0)
+        project(i, image_rows(self_mixed, i), loads.got(1))
+        jobs[0][i].start()
+
+    def norm_stage(t, i, rows_ref, out_ref, full_ref):
+        job = jobs[t][i]
+        job.arrived()
+        gain = gains_ref[t + 1 : t + 2, :]
+        for start in range(0, out_ref.shape[1], 32):
+            at = slice(start, start + 32)
+            wide_rows, narrow, _ = post_forward(job.total(at), (rows_ref[i, at, :],), gain)
+            out_ref[i, at, :] = wide_rows
+            full_ref[square.spot, i, at, :] = narrow
+        job.gather(full_ref.at[:, i])
+
+    def cross_stage(i):
+        jobs[0][i].gathered()
+        jobs[0][i].sent()
+        text = loads.got(4)
+        queries_ref[:, i] = (
+            product(image_rows(second_normed, i), loads.got(3)[...])
+            .astype(BF16)
+            .reshape(queries_ref.shape[0], queries_ref.shape[2], queries_ref.shape[3])
+        )
+
+        def one(h, carry):
+            own, value = (tile_at(h + n * heads, HDIM) for n in range(2))
+            done = attend(image_rows(queries_ref, i, own), text[i, :, own], text[i, :, value])
+            put_image(cross_mixed, i, own, done)
+            return carry
+
+        lax.fori_loop(0, heads, one, 0)
+        project(i, image_rows(cross_mixed, i), loads.got(5))
+        jobs[1][i].start()
+
+    def shrink_back(first, last):
+        feed_grad = loads.got(6)
+        count = shrink_ref.shape[0] // wide
+
+        def one(j, carry):
+            shrink_load(j).wait()
+
+            @pl.when(j + 1 < count)
+            def _():
+                shrink_load(j + 1).start()
+
+            for i in range(images):
+                done = product(image_rows(feed_grad, i), tiles[lax.rem(j, 2)], NT)
+                put_image(grad_hidden, i, tile_at(j, wide), done.astype(BF16))
+            return carry
+
+        lax.fori_loop(first, last, one, 0)
+
+    def feed_stage(i):
+        jobs[1][i].gathered()
+        expand = loads.got(7)
+
+        def one(j, carry):
+            at = tile_at(j, wide)
+            hidden = product(image_rows(third_normed, i), expand[:, at])
+            spread = 0.5 + 0.5 * lax.erf(hidden * math.sqrt(0.5))
+            slope = spread + hidden * jnp.exp(-0.5 * hidden * hidden) * (1.0 / math.sqrt(2.0 * math.pi))
+            put_image(active, i, at, (hidden * spread).astype(BF16))
+            grad = image_rows(grad_hidden, i, at).astype(F32) * slope
+            put_image(grad_hidden, i, at, grad.astype(BF16))
+            return carry
+
+        lax.fori_loop(0, expand.shape[1] // wide, one, 0)
+
+    count = shrink_ref.shape[0] // wide
+    first, second = jobs
+    self_stage(0)
+    self_stage(1)
+    first[0].forward()
+    self_stage(2)
+    first[1].forward()
+    first[2].forward()
+    shrink_back(0, count // 2)
+    rows_ref = loads.got(2)
+    for i in range(images):
+        norm_stage(0, i, rows_ref, own_self, second_normed)
+        if i:
+            first[i - 1].pass_on(second_normed.at[:, i - 1])
+    cross_stage(0)
+    first[-1].pass_on(second_normed.at[:, images - 1])
+    cross_stage(1)
+    second[0].forward()
+    cross_stage(2)
+    second[1].forward()
+    second[2].forward()
+    shrink_back(count // 2, count)
+    for i in range(images):
+        norm_stage(1, i, own_self, own_cross, third_normed)
+        if i:
+            second[i - 1].pass_on(third_normed.at[:, i - 1])
+    feed_stage(0)
+    second[-1].pass_on(third_normed.at[:, images - 1])
+    feed_stage(1)
+    feed_stage(2)
+    for job in first:
+        job.spread_sent()
+    for job in second:
+        job.sent()
+        job.spread_sent()
+
+
+def forward_steps(gains, projected, attention_out, entry, cross_query, text, cross_out, feed_grad, expand, shrink, ident):
+    quarters, images, block, _ = projected.shape
+    width = attention_out.shape[1]
+    ff = expand.shape[1]
+    heads_wide = attention_out.shape[0]
+
+    def rows(columns):
+        return jax.ShapeDtypeStruct((quarters, images, block, columns), BF16)
+
+    outs = [rows(heads_wide), rows(width), rows(heads_wide), rows(heads_wide), rows(width), rows(ff), rows(ff)]
+    outs += [jax.ShapeDtypeStruct((images, block, width), F32)] * 2
+    given = (projected, attention_out, entry, cross_query, text, cross_out, feed_grad, expand)
+    vmem = pl.BlockSpec(memory_space=pltpu.VMEM)
+    hbm = pl.BlockSpec(memory_space=pl.ANY)
+    return pl.pallas_call(
+        forward_kernel,
+        out_shape=outs,
+        in_specs=[vmem] + [hbm] * 9,
+        out_specs=[vmem] * len(outs),
+        scratch_shapes=[pltpu.VMEM(a.shape, a.dtype) for a in given]
+        + [
+            pltpu.SemaphoreType.DMA((len(given),)),
+            pltpu.VMEM((2, 256, width), BF16),
+            pltpu.SemaphoreType.DMA((2,)),
+        ]
+        + ImageSum.scratch(2, images, block, width),
+        compiler_params=pltpu.CompilerParams(
+            collective_id=ident, has_side_effects=True, vmem_limit_bytes=VMEM_BYTES
+        ),
+        cost_estimate=pl.CostEstimate(
+            flops=60_000_000_000, bytes_accessed=80_000_000, transcendentals=0
+        ),
+    )(gains, *given, shrink)
 
 
 def gelu_exact(values_in):
@@ -761,11 +1230,24 @@
     text_width = caption.shape[1]
     heads_here = attention_in.shape[2] // HDIM
 
+    quarters = axis_count if square else 1
+
     def own_rows(rows_in):
         return lax.dynamic_slice_in_dim(rows_in, axis_place * share_rows, share_rows, 0)
 
+    def by_quarters(rows_in):
+        parts = rows_in.reshape(images, quarters, length // quarters, -1)
+        return parts.transpose(1, 0, 2, 3).reshape(rows_all, -1)
+
+    def four(rows_in):
+        return rows_in.reshape(quarters, images, -1, rows_in.shape[-1])
+
+    def flat(parts):
+        return parts.reshape(rows_all, parts.shape[-1])
+
+    tokens, out_grad = by_quarters(tokens), by_quarters(out_grad)
     gains = [norm_gains[k : k + 1] for k in range(3)]
-    mask_column = (masked.reshape(rows_all, 1) > 0)
+    mask_column = by_quarters(masked) > 0
 
     def enter(rows_in, mask):
         return jnp.where(mask, mask_embed.astype(F32)[None, :], rows_in.astype(F32))
@@ -777,67 +1259,92 @@
     first_normed = (first_unit * gains[0]).astype(BF16)
     weight_in = attention_in.reshape(model_width, -1)
     projected = product(first_normed, weight_in).astype(BF16)
-    self_mixed = attend_forward(images, heads_here, projected, projected)
-    own_self, second_normed = step(
-        self_mixed, attention_out, NN, post_forward, gains[1], (own_entry,), F32, 0, True, 1
-    )
-    cross_queries = product(second_normed, cross_query).astype(BF16)
     weight_text = cross_text.reshape(text_width, -1)
     text_pairs = product(caption, weight_text).astype(BF16)
-    cross_mixed = attend_forward(images, heads_here, cross_queries, text_pairs)
-    own_cross, third_normed = step(
-        cross_mixed, cross_out, NN, post_forward, gains[2], (own_self,), F32, 0, True, 2
-    )
-
+    text_four = text_pairs.reshape(1, images, -1, text_pairs.shape[1])
     feed_grad = jnp.where(mask_column, out_grad, jnp.zeros_like(out_grad))
     own_feed_grad = own_rows(feed_grad).astype(F32)
-    hidden = product(third_normed, feed_expand)
-    active = gelu_exact(hidden).astype(BF16)
-    grad_active = product(feed_grad, feed_shrink, NT)
-    _, gelu_pull = jax.vjp(gelu_exact, hidden)
-    grad_hidden = gelu_pull(grad_active)[0].astype(BF16)
-    own_before_feed, cross_grad, third_gain, shrink_sum = step(
+    ff = feed_expand.shape[1]
+    if square:
+        rows_out = forward_steps(
+            norm_gains, four(projected), attention_out, own_entry.reshape(images, -1, model_width), cross_query,
+            text_four[0], cross_out, four(feed_grad), feed_expand, feed_shrink, 1,
+        )
+        self_mixed, second_normed, cross_queries, cross_mixed, third_normed, active, grad_hidden = (
+            flat(part) for part in rows_out[:7]
+        )
+        own_self, own_cross = (part.reshape(share_rows, model_width) for part in rows_out[7:])
+    else:
+        whole = four(projected)
+        self_mixed = flat(attend_forward(heads_here, whole, whole))
+        own_self, second_normed = step(
+            self_mixed, attention_out, NN, post_forward, gains[1], (own_entry,), F32, 0, True, 1
+        )
+        cross_queries = product(second_normed, cross_query).astype(BF16)
+        cross_mixed = flat(attend_forward(heads_here, four(cross_queries), text_four))
+        own_cross, third_normed = step(
+            cross_mixed, cross_out, NN, post_forward, gains[2], (own_self,), F32, 0, True, 2
+        )
+        hidden = product(third_normed, feed_expand)
+        active = gelu_exact(hidden).astype(BF16)
+        _, gelu_pull = jax.vjp(gelu_exact, hidden)
+        grad_hidden = gelu_pull(product(feed_grad, feed_shrink, NT))[0].astype(BF16)
+    wide = LineSum.width
+    own_before_feed, cross_grad, third_gain, shrink_low = step(
         grad_hidden, feed_expand, NT, post_backward, gains[2], (own_feed_grad, own_cross), F32, 1, True, 3,
-        (feed_grad, active), True,
+        ((feed_grad, active, 0, ff - wide, True),),
     )
 
     grad_cross_mixed = product(cross_grad, cross_out, NT).astype(BF16)
     grad_cross_queries, grad_text_pairs = attend_backward(
-        images, heads_here, cross_queries, text_pairs, grad_cross_mixed
+        heads_here, four(cross_queries), text_four, four(grad_cross_mixed)
     )
-    caption_part = product(grad_text_pairs, weight_text, NT).astype(BF16)
-    own_before_cross, self_grad, second_gain, expand_sum = step(
+    grad_cross_queries = flat(grad_cross_queries)
+    grad_text_pairs = grad_text_pairs.reshape(text_pairs.shape)
+    own_before_cross, self_grad, second_gain, shrink_high, expand_low, mixed_part = step(
         grad_cross_queries, cross_query, NT, post_backward, gains[1], (own_before_feed, own_self), F32, 1, True, 4,
-        (third_normed, grad_hidden),
+        ((feed_grad, active, ff - wide, ff, True), (third_normed, grad_hidden, 0, ff // 2, False)),
+        (active, feed_shrink, NN),
     )
 
     self_grad, grad_text_pairs = lax.optimization_barrier((self_grad, grad_text_pairs))
     cross_text_sum = image_sum(rows_product(caption, grad_text_pairs))
     grad_self_mixed = product(self_grad, attention_out, NT).astype(BF16)
-    grad_projected = attend_backward(images, heads_here, projected, projected, grad_self_mixed)
-    tokens_grad, first_gain, embed_term = step(
+    four_projected = four(projected)
+    grad_projected = flat(
+        attend_backward(heads_here, four_projected, four_projected, four(grad_self_mixed))
+    )
+    tokens_rows, first_gain, embed_term, expand_high, caption_part = step(
         grad_projected, weight_in, NT, post_entry, gains[0],
         (own_before_cross, own_entry, own_float), F32, 2, False, 5,
+        ((third_normed, grad_hidden, ff // 2, ff, False),), (grad_text_pairs, weight_text, NT),
     )
     terms = [first_gain, second_gain, third_gain, embed_term]
     if square:
-        self_in_sum, self_out_sum, cross_query_sum, cross_out_sum, small_totals, mixed_out, caption_grad = line_sums(
+        own_mixed = own_rows(mixed_part).astype(F32) + own_cross
+        mixed_part = lax.dynamic_update_slice_in_dim(
+            mixed_part, own_mixed.astype(BF16), axis_place * share_rows, 0
+        )
+        (
+            self_in_sum, self_out_sum, cross_query_sum, cross_out_sum,
+            small_totals, mixed_out, caption_grad, tokens_grad,
+        ) = line_sums(
             [first_normed, self_grad, second_normed, cross_grad],
             [grad_projected, self_mixed, grad_cross_queries, cross_mixed],
-            ((0, 0, 0), (0, 0, 512), (0, 0, 1024), (1, 1, 0), (2, 2, 0), (3, 3, 0)),
+            ((0, 4, 0), (0, 4, 512), (0, 4, 1024), (1, 5, 0), (2, 6, 0), (3, 7, 0)),
             jnp.concatenate(terms + [jnp.zeros_like(embed_term)] * 4, axis=0),
-            product(active, feed_shrink).astype(BF16),
+            mixed_part,
             caption_part,
-            own_cross,
+            tokens_rows.reshape(images, -1, model_width),
             6,
         )
         slice_width = model_width // (lax.axis_size("img") * axis_count)
         slice_at = (lax.axis_index("img") * axis_count + axis_place) * slice_width
         small_sums = lax.dynamic_slice_in_dim(small_totals, slice_at, slice_width, 1)
     else:
-        (mixed_out,) = step(
-            active, feed_shrink, NN, post_plain, gains[0], (own_cross,), BF16, 0, False, 0
-        )
+        tokens_grad = tokens_rows
+        mixed_sum = lax.psum_scatter(mixed_part, "mp", scatter_dimension=0, tiled=True)
+        mixed_out = (own_cross + mixed_sum.astype(F32)).astype(BF16)
         caption_grad = lax.psum_scatter(
             caption_part, "mp", scatter_dimension=1, tiled=True
         ).astype(F32)
@@ -859,8 +1366,8 @@
         cross_query_sum,
         cross_text_sum.reshape(-1, 2, cross_text.shape[2]),
         cross_out_sum,
-        expand_sum,
-        shrink_sum,
+        jnp.concatenate([expand_low, expand_high], axis=1),
+        jnp.concatenate([shrink_low, shrink_high], axis=0),
     )
 
 

time: 661 us -> 632 us (0.956)
  matrix products: 91.3 us -> 27.4 us
  Pallas kernels: 473 us -> 495 us
  other arithmetic: 15.5 us -> 23.9 us
    dot_general x10 -> x5, matrix products: 91.3 us -> 27.4 us  [product(): return lax.dot_general(left, right, dims, preferred_element_type=F32)]
    pallas_call x7 -> x4, Pallas kernels: 338 us -> 355 us  [the longest x3 229 us: square_step(): pl.pallas_call(functools.partial(square_kernel, plan), out_shape=outs, in...]
    unnamed x54 -> x70, local copies, waits for them, and re-layouts: 41.6 us -> 36.7 us
  transfers between devices with their start and end apart: 1 -> 1, of which waited for: 0 -> 0; matrix products, arithmetic and copies ran while one was open for 7% -> 5% of each run, Pallas kernels for 25% -> 33%
where the time goes in v3:
time: 632 us; the launch traced here: 621 us
  Pallas kernels  495 us (78%)
  local copies, waits for them, and re-layouts  59.9 us (9%)
  matrix products  27.4 us (4%)
  other arithmetic  23.9 us (4%)
  between operations  14.8 us (2%)
    pallas_call x3, Pallas kernels, square_step(): pl.pallas_call(functools.partial(square_kernel, plan), out_shape=outs, in...  229 us
    pallas_call x1, Pallas kernels, forward_steps(): pl.pallas_call(forward_kernel, out_shape=outs, in_specs=[vmem] + [hbm] *...  126 us
    pallas_call x1, Pallas kernels, line_sums(): pl.pallas_call(functools.partial(line_kernel, pieces, len(lhs_list), len(...  121 us
    unnamed x70, local copies, waits for them, and re-layouts  36.7 us
    dot_general x5, matrix products, product(): return lax.dot_general(left, right, dims, preferred_element_type=F32)  27.4 us
    pallas_call x2, Pallas kernels, attend_backward(): pl.pallas_call(functools.partial(attend_backward_kernel, heads, separate)...  18.7 us
  transfers between devices with their start and end apart: 1, of which 0 were waited for; matrix products, arithmetic and copies ran while one was open for 5% of the time, Pallas kernels for 33%

profile of v3, /device:TPU:0, one launch (start us, length us, event | category | flops | bytes accessed | tf_op | source)
XLA Modules:
  0.0 621.1 jit_solution(1968216901655090332)
XLA Ops:
  7.2 0.8 broadcast_compare_fusion
  8.7 1.5 fusion.3
  10.2 0.7 convert_element_type.53
  10.9 4.1 copy.30
  15.0 1.8 copy.33
  16.8 1.9 bitcast_select_fusion.1.refs_7_
  18.8 1.1 copy-done.1
  19.8 0.8 fusion.1
  20.6 1.4 multiply_reduce_fusion
  22.0 8.9 %copy.31 = bf16[2048,3,512]{0,2,1:T(8,128)(2,1)} copy(bf16[2048,3,512]{2,0,1:T(8,128)(2,1)} %param.19) | data formatting | bytes 12582912 | tf_op args[6]
  30.9 9.3 %copy.38 = bf16[512,8,2,512]{3,1,2,0:T(8,128)(2,1)} copy(bf16[512,8,2,512]{3,2,1,0:T(2,128)(2,1)} %bitcast.78) | data formatting | bytes 16777216
  40.2 0.7 dynamic-slice_convert_fusion.1
  40.9 2.3 bitcast_select_fusion.refs_5_.refs_7_
  43.2 1.3 dynamic-slice_convert_fusion.refs_3_
  44.6 1.1 copy-done.5
  45.7 1.4 multiply_convert_fusion
  47.3 6.4 %convolution_convert_fusion = bf16[768,1536]{1,0:T(8,128)(2,1)} fusion(bf16[768,2048]{1,0:T(8,128)(2,1)S(1)} %bitcast.84, bf16[2048,1536]{0,1:T(8,128)(2,1)S(1)} %bitcast.71), kind=kOutput, calls=%fused_computation.7 | convolution fusion | flops 4833017856 | bytes 11796480 | tf_op jit(solution)/shard_map/dot_general | solution.py:27
  53.7 2.5 convert_select_fusion.1.refs_4_
  56.2 4.4 convolution_convert_fusion.3
  60.6 125.7 %shard_map.220 = (bf16[4,3,64,512]{3,2,1,0:T(8,128)(2,1)}, bf16[4,3,64,2048]{3,2,1,0:T(8,128)(2,1)}, bf16[4,3,64,512]{3,2,1,0:T(8,128)(2,1)}, bf16[4,3,64,512]{3...) custom-call(f32[3,2048]{1,0:T(4,128)} %refs_0_.1, ...), custom_call_target="tpu_custom_call" | custom-call | flops 60000002048 | bytes 80000000 | tf_op jit(solution)/shard_map/pallas_call | solution.py:1182
  186.3 76.7 %shard_map.221 = (f32[192,2048]{1,0:T(8,128)}, bf16[768,2048]{1,0:T(8,128)(2,1)}, f32[1,2048]{1,0:T(1,128)}, f32[1536,256]{1,0:T(8,128)}) custom-call(f32[1,2048]{1,0:T(1,128)} %get-tuple-element.110.refs_0_, bf16[768,2048]{1,0:T(8,128)(2,1)} %bitcast.110, bf16[2048,2048]{1,0:T(8,128)(2,1)} %refs_2_.4, f32[192,2048]{1,0:T(8,128)} %dynamic-slice_convert_fusion.refs_3_, ...), custom_call_target="tpu_custom_call" | custom-call | flops 60000002048 | bytes 16252928 | tf_op jit(solution)/shard_map/pallas_call | solution.py:519
  263.0 4.6 convolution_convert_fusion.2
  267.6 8.5 %shard_map.222 = (bf16[4,3,64,512]{3,2,1,0:T(8,128)(2,1)}, bf16[1,3,128,1024]{3,2,1,0:T(8,128)(2,1)}) custom-call(bf16[4,3,64,512]{3,2,1,0:T(8,128)(2,1)} %get-tuple-element.48.query_ref, bf16[1,3,128,1024]{3,2,1,0:T(8,128)(2,1)} %bitcast.92, bf16[4,3,64,512]{3,2,1,0:T(8,128)(2,1)} %bitcast.93), custom_call_target="tpu_custom_call" | custom-call | tf_op jit(solution)/shard_map/pallas_call | solution.py:893
  276.1 76.4 %shard_map.223 = (f32[192,2048]{1,0:T(8,128)}, bf16[768,2048]{1,0:T(8,128)(2,1)}, f32[1,2048]{1,0:T(1,128)}, f32[512,256]{1,0:T(8,128)}, f32[256,1024]{1,0:T(8,128)}, /*index=5*/bf16[768,2048]{1,0:T(8,128)(2,1)}) custom-call(f32[1,2048]{1,0:T(1,128)} %get-tuple-element.111.refs_0_, bf16[768,512]{1,0:T(8,128)(2,1)} %bitcast.103, bf16[2048,512]{1,0:T(8,128)(2,1)} %refs_2_.5, ...), custom_call_target="tpu_custom_call" | custom-call | flops 60000002048 | bytes 7602176 | tf_op jit(solution)/shard_map/pallas_call | solution.py:519
  352.5 6.8 %convert_bitcast_fusion = bf16[4096,1024]{0,1:T(8,128)(2,1)} fusion(bf16[384,1024]{1,0:T(8,128)(2,1)S(1)} %bitcast.106, bf16[384,4096]{1,0:T(8,128)(2,1)S(1)} %copy-done), kind=kOutput, calls=%fused_computation | convolution fusion | flops 3225419776 | bytes 12320768 | tf_op jit(solution)/shard_map/dot_general | solution.py:27
  359.3 0.7 copy-done.19
  360.1 8.7 %copy.34.refs_2_ = bf16[2048,1536]{1,0:T(8,128)(2,1)} copy(bf16[2048,1536]{0,1:T(8,128)(2,1)} %bitcast.68) | data formatting | bytes 12582912 | tf_op jit(solution)/shard_map/reshape | solution.py:1260
  368.9 5.2 convolution_convert_fusion.1
  374.1 10.2 %shard_map.224 = bf16[4,3,64,1536]{3,2,1,0:T(8,128)(2,1)} custom-call(bf16[4,3,64,1536]{3,2,1,0:T(8,128)(2,1)} %bitcast.76, bf16[4,3,64,1536]{3,2,1,0:T(8,128)(2,1)} %bitcast.77, bf16[4,3,64,512]{3,2,1,0:T(8,128)(2,1)} %bitcast.94), custom_call_target="tpu_custom_call" | custom-call | tf_op jit(solution)/shard_map/pallas_call | solution.py:893
  384.3 76.1 %shard_map.225 = (f32[192,2048]{1,0:T(8,128)}, f32[1,2048]{1,0:T(1,128)}, f32[1,2048]{1,0:T(1,128)}, f32[256,1024]{1,0:T(8,128)}, bf16[384,4096]{1,0:T(8,128)(2,1)}) custom-call(f32[1,2048]{1,0:T(1,128)} %copy-done.16, bf16[768,1536]{1,0:T(8,128)(2,1)} %bitcast.85, bf16[2048,1536]{1,0:T(8,128)(2,1)} %copy.34.refs_2_, f32[192,2048]{1,0:T(8,128)} %get-tuple-element.63.refs_3_, ...), custom_call_target="tpu_custom_call" | custom-call | flops 60000002048 | bytes 13369344 | tf_op jit(solution)/shard_map/pallas_call | solution.py:519
  460.6 1.4 concatenate.13.refs_8_
  462.0 2.9 fusion.2.refs_9_
  464.8 2.6 multiply_convert_fusion.1.refs_0_
  467.5 121.4 %shard_map.226 = (f32[256,1536]{1,0:T(8,128)}, f32[512,256]{1,0:T(8,128)}, f32[256,512]{1,0:T(8,128)}, f32[512,256]{1,0:T(8,128)}, f32[8,2048]{1,0:T(8,128)}, /*...) custom-call(bf16[768,2048]{1,0:T(8,128)(2,1)} %multiply_convert_fusion.1.refs_0_, ...), custom_call_target="tpu_custom_call" | custom-call | flops 60000002048 | bytes 40000000 | tf_op jit(solution)/shard_map/pallas_call | solution.py:774
  588.9 0.8 constant_dynamic-slice_fusion
  589.7 0.6 slice.19
  590.3 3.0 copy.35
  593.3 3.0 copy.36
  596.3 0.5 slice_bitcast_fusion
  596.8 3.2 pad_maximum_fusion
  600.0 1.5 pad_maximum_fusion.1
  601.5 3.8 copy.37
  605.3 2.2 copy.53
  607.5 2.8 copy.54
  610.3 1.1 copy.55
  611.4 0.8 copy.56
  612.2 0.8 copy.57
  613.0 0.8 copy.58
  (71 shorter events, 1.2 us)
Async XLA Ops:
  7.2 49.0 %copy-start = (bf16[384,4096]{1,0:T(8,128)(2,1)S(1)}, bf16[384,4096]{1,0:T(8,128)(2,1)}, u32[]{:S(2)}) copy-start(bf16[384,4096]{1,0:T(8,128)(2,1)} %param.14) | copy-start | bytes 9437188
  7.2 594.3 %reduce-scatter.2.cloned.1.call-start = ((), (), s32[]{:S(2)}) async-start(), calls=%async_computation.1 | async-start | bytes 9437184 | tf_op jit(solution)/shard_map/reduce_scatter | solution.py:31
  8.3 32.6 %copy-start.20 = (pred[768]{0:T(1024)(128)(4,1)}, pred[768]{0:T(1024)(128)(4,1)S(1)}, u32[]{:S(2)}) copy-start(pred[768]{0:T(1024)(128)(4,1)S(1)} %gt.39) | copy-start | bytes 2308
  10.2 35.4 %copy-start.16 = (f32[1,2048]{1,0:T(1,128)}, f32[1,2048]{1,0:T(1,128)S(1)}, u32[]{:S(2)}) copy-start(f32[1,2048]{1,0:T(1,128)S(1)} %get-tuple-element.112.refs_0_) | copy-start | bytes 24580
  10.9 42.8 %copy-start.12 = (f32[2048]{0:T(1024)}, f32[2048]{0:T(1024)S(1)}, u32[]{:S(2)}) copy-start(f32[2048]{0:T(1024)S(1)} %convert_element_type.53) | copy-start | bytes 24580
  10.9 4.1 copy-start.4
  16.8 3.0 copy-start.1
  20.6 25.0 %copy-start.14 = (f32[4,3,64]{2,1,0:T(4,128)}, f32[4,3,64]{2,1,0:T(4,128)S(1)}, u32[]{:S(2)}) copy-start(f32[4,3,64]{2,1,0:T(4,128)S(1)} %broadcast_multiply_fusion) | copy-start | bytes 9220
  22.0 23.6 %copy-start.18 = (f32[4,3,64]{2,1,0:T(4,128)}, f32[4,3,64]{2,1,0:T(4,128)S(1)}, u32[]{:S(2)}) copy-start(f32[4,3,64]{2,1,0:T(4,128)S(1)} %add_rsqrt_fusion) | copy-start | bytes 9220
  40.9 4.7 copy-start.2
  40.9 6.2 slice-start
  43.2 2.4 copy-start.5
  43.2 4.1 slice-start.1
  45.6 10.5 %slice-start.2 = ((s8[8388608]{0:T(1024)(128)(4,1)}), s8[4194304]{0:T(1024)(128)(4,1)S(1)}, s32[]{:S(2)}) async-start(s8[8388608]{0:T(1024)(128)(4,1)} %bitcast.80), calls=%async_computation.4 | async-start | bytes 8388608
  47.3 8.8 %slice-start.3 = ((s8[8388608]{0:T(1024)(128)(4,1)}), s8[4194304]{0:T(1024)(128)(4,1)S(1)}, s32[]{:S(2)}) async-start(s8[8388608]{0:T(1024)(128)(4,1)} %bitcast.80), calls=%async_computation.5 | async-start | bytes 8388608
  186.3 76.7 %copy-start.24 = (bf16[512,2048]{1,0:T(8,128)(2,1)S(1)}, bf16[512,2048]{1,0:T(8,128)(2,1)}, u32[]{:S(2)}) copy-start(bf16[512,2048]{1,0:T(8,128)(2,1)} %refs_6_.2) | copy-start | bytes 6291460
  276.1 76.4 %copy-start.25 = (bf16[1,3,128,1024]{3,2,1,0:T(8,128)(2,1)S(1)}, bf16[1,3,128,1024]{3,2,1,0:T(8,128)(2,1)}, u32[]{:S(2)}) copy-start(bf16[1,3,128,1024]{3,2,1,0:T(8,128)(2,1)} %get-tuple-element.58) | copy-start | bytes 2359300
  359.3 0.7 copy-start.19
  359.3 0.8 copy-start.15
  384.3 76.2 %copy-start.22 = (f32[1,2048]{1,0:T(1,128)S(1)}, f32[1,2048]{1,0:T(1,128)}, u32[]{:S(2)}) copy-start(f32[1,2048]{1,0:T(1,128)} %get-tuple-element.67) | copy-start | bytes 24580
  384.3 76.2 %copy-start.23 = (f32[1,2048]{1,0:T(1,128)S(1)}, f32[1,2048]{1,0:T(1,128)}, u32[]{:S(2)}) copy-start(f32[1,2048]{1,0:T(1,128)} %get-tuple-element.66) | copy-start | bytes 24580
  460.5 4.3 copy-start.13
  460.5 4.3 copy-start.17
  460.5 4.3 copy-start.21
  462.0 2.9 copy-start.3
  596.3 3.7 copy-start.7
  596.3 3.7 copy-start.11
  605.3 5.0 copy-start.6
  607.5 3.9 copy-start.10
  607.5 4.7 copy-start.9
  610.3 2.7 copy-start.8
Sparse Core Ops, SparseCore 0:
  359.4 126.1 reduce-scatter.1

commit v4 on v0

v4 whole, which is shorter than its diff:
```python
import dataclasses
import functools
import math
import types
from typing import Any

import jax
import jax.numpy as jnp
from jax import lax
from jax.experimental import pallas as pl
from jax.experimental.pallas import tpu as pltpu
from jax.sharding import PartitionSpec as P

HDIM = 128
EPSILON = 1e-05
SCALE = 1.0 / math.sqrt(HDIM)
VMEM_BYTES = 61 * 1024 * 1024
MESH = pl.DeviceIdType.MESH
BF16 = jnp.bfloat16
F32 = jnp.float32
WIDE = 512
TILE = 256

NN = (((1,), (0,)), ((), ()))
NT = (((1,), (1,)), ((), ()))
TN = (((0,), (0,)), ((), ()))


def product(left, right, dims=NN):
    return lax.dot_general(left, right, dims, preferred_element_type=F32)


def image_sum(part, dimension=0):
    return lax.psum_scatter(part, "img", scatter_dimension=dimension, tiled=True).astype(F32)


def rows_product(left, right):
    return product(left, right, TN).astype(BF16)


def norm_parts(rows_in):
    centre = rows_in - jnp.mean(rows_in, axis=-1, keepdims=True)
    root_inverse = lax.rsqrt(jnp.mean(centre * centre, axis=-1, keepdims=True) + EPSILON)
    return (centre * root_inverse, root_inverse)


def norm_back(grad_rows, unit_rows, root_inverse, gain_row):
    weighted = grad_rows * gain_row
    middle = jnp.mean(weighted, axis=-1, keepdims=True)
    along = jnp.mean(weighted * unit_rows, axis=-1, keepdims=True)
    return root_inverse * (weighted - middle - unit_rows * along)


def post_forward(total, rows_in, gain):
    fresh = rows_in[0] + total
    unit, _ = norm_parts(fresh)
    return fresh, (unit * gain).astype(BF16), ()


def post_backward(total, rows_in, gain):
    before, source = rows_in
    unit, root = norm_parts(source)
    grad = before + norm_back(total, unit, root, gain)
    return grad, grad.astype(BF16), (jnp.sum(total * unit, axis=0, keepdims=True),)


def post_entry(total, rows_in, gain):
    before, source, mask = rows_in
    unit, root = norm_parts(source)
    grad = before + norm_back(total, unit, root, gain)
    sums = (
        jnp.sum(total * unit, axis=0, keepdims=True),
        jnp.sum(grad * mask, axis=0, keepdims=True),
    )
    return grad * (1.0 - mask), None, sums


def remote(source, target, send, recv, device):
    return pltpu.make_async_remote_copy(
        src_ref=source,
        dst_ref=target,
        send_sem=send,
        recv_sem=recv,
        device_id=device,
        device_id_type=MESH,
    )


def greet(targets):
    barrier = pltpu.get_barrier_semaphore()
    for target in targets:
        pl.semaphore_signal(barrier, inc=1, device_id=target, device_id_type=MESH)
    pl.semaphore_wait(barrier, len(targets))


def tile_at(j, wide=TILE):
    return pl.ds(pl.multiple_of(j * wide, wide), wide)


def all_rows(ref, columns=slice(None)):
    part = ref[:, :, :, columns]
    return part.reshape(-1, part.shape[3])


def image_rows(ref, i, columns=slice(None)):
    part = ref[i, :, :, columns]
    return part.reshape(-1, part.shape[2])


def put_image(ref, i, columns, value):
    ref[i, :, :, columns] = value.reshape(ref.shape[1], ref.shape[2], value.shape[1])


class Loads:
    def __init__(self, names, sources, targets, sem):
        self.targets = dict(zip(names, targets))
        self.copies = {
            name: pltpu.make_async_copy(source, target, sem.at[i])
            for i, (name, source, target) in enumerate(zip(names, sources, targets))
        }
        self.waiting = set()

    def start(self, *names):
        for name in names:
            self.copies[name].start()
            self.waiting.add(name)

    def got(self, name):
        if name in self.waiting:
            self.waiting.remove(name)
            self.copies[name].wait()
        return self.targets[name]


class Stream:
    def __init__(self, source, tiles, sem, columns=False, passes=1):
        self.source, self.tiles, self.sem, self.columns = source, tiles, sem, columns
        self.count = source.shape[1 if columns else 0] // TILE
        self.total = passes * self.count

    def copy(self, j):
        slot, at = lax.rem(j, 2), tile_at(lax.rem(j, self.count))
        part = self.source.at[:, at] if self.columns else self.source.at[at, :]
        return pltpu.make_async_copy(part, self.tiles.at[slot], self.sem.at[slot])

    def start(self):
        self.copy(0).start()

    def run(self, first, last, use):
        def one(j, carry):
            self.copy(j).wait()

            @pl.when(j + 1 < self.total)
            def _():
                self.copy(j + 1).start()

            use(j, self.tiles[lax.rem(j, 2)])
            return carry

        lax.fori_loop(first, last, one, 0)

    @staticmethod
    def scratch(source, columns=False):
        shape = (source.shape[0], TILE) if columns else (TILE, source.shape[1])
        return pltpu.VMEM((2,) + shape, source.dtype), pltpu.SemaphoreType.DMA((2,))


class Saves:
    def __init__(self, names, sources, targets, sem):
        self.refs = {n: pair for n, pair in zip(names, zip(sources, targets))}
        self.sem, self.running, self.names = sem, [], names

    def save(self, name, i=None):
        source, target = self.refs[name]
        if i is not None:
            source, target = source.at[i], target.at[i]
        copy = pltpu.make_async_copy(source, target, self.sem.at[self.names.index(name), i or 0])
        copy.start()
        self.running.append(copy)

    def finish(self):
        for copy in self.running:
            copy.wait()


def launch(kernel, ident, vmem=(), loaded=(), hbm=(), outs=(), saved=(), hbm_outs=(), scratch=()):
    vmem, loaded, hbm, outs = dict(vmem), dict(loaded), dict(hbm), dict(outs)
    saved, hbm_outs, scratch = dict(saved), dict(hbm_outs), dict(scratch)
    names = [*vmem, *loaded, *hbm, *outs, *saved, *hbm_outs]
    buffers = [pltpu.VMEM(a.shape, a.dtype) for a in [*loaded.values(), *saved.values()]]

    def run(*refs):
        r = types.SimpleNamespace(**dict(zip(names, refs)))
        rest = refs[len(names) :]
        rest, buffer_refs = rest[: len(scratch)], rest[len(scratch) : len(scratch) + len(buffers)]
        for name, ref in zip(scratch, rest):
            setattr(r, name, ref)
        r.loads = Loads(list(loaded), [getattr(r, n) for n in loaded], buffer_refs[: len(loaded)], refs[-2])
        kept = buffer_refs[len(loaded) :]
        r.saves = Saves(list(saved), kept, [getattr(r, n) for n in saved], refs[-1])
        for name, ref in zip(saved, kept):
            setattr(r, name, ref)
        kernel(r)
        r.saves.finish()

    in_vmem = pl.BlockSpec(memory_space=pltpu.VMEM)
    in_hbm = pl.BlockSpec(memory_space=pl.ANY)
    result = pl.pallas_call(
        run,
        out_shape=[*outs.values(), *saved.values(), *hbm_outs.values()],
        in_specs=[in_vmem] * len(vmem) + [in_hbm] * (len(loaded) + len(hbm)),
        out_specs=[in_vmem] * len(outs) + [in_hbm] * (len(saved) + len(hbm_outs)),
        scratch_shapes=[
            *scratch.values(),
            *buffers,
            pltpu.SemaphoreType.DMA((max(len(loaded), 1),)),
            pltpu.SemaphoreType.DMA((max(len(saved), 1), 3)),
        ],
        compiler_params=pltpu.CompilerParams(
            collective_id=ident, has_side_effects=True, vmem_limit_bytes=VMEM_BYTES
        ),
        cost_estimate=pl.CostEstimate(
            flops=60_000_000_000, bytes_accessed=80_000_000, transcendentals=0
        ),
    )(*vmem.values(), *loaded.values(), *hbm.values())
    return types.SimpleNamespace(**dict(zip([*outs, *saved, *hbm_outs], result)))


def struct(shape, kind):
    return jax.ShapeDtypeStruct(tuple(shape), kind)


class Square:
    def __init__(self):
        self.spot = lax.axis_index("mp")
        up, across = lax.div(self.spot, 2), lax.rem(self.spot, 2)
        self.beside = up * 2 + (1 - across)
        self.above = (1 - up) * 2 + across
        self.corner = (1 - up) * 2 + (1 - across)
        self.peers = (self.beside, self.above)
        self.targets = [{"mp": self.beside}, {"mp": self.above}]


class LineSum:
    def __init__(self, r, lefts, pieces):
        self.r, self.lefts, self.pieces = r, lefts, pieces
        self.count, self.ticked = len(pieces), 0
        self.share = r.line_own.shape[2]
        self.place = lax.axis_index("img")
        self.line, self.core = lax.div(self.place, 2), lax.rem(self.place, 2)
        self.twin = self.line * 2 + (1 - self.core)
        self.others = [lax.rem(self.line + j, 4) * 2 + self.core for j in (1, 2, 3)]
        self.targets = [{"img": self.twin}] + [{"img": o} for o in self.others]

    @staticmethod
    def scratch(count, lefts, left):
        dma = pltpu.SemaphoreType.DMA
        share = left.shape[3] // 8
        return dict(
            line_left=pltpu.VMEM((lefts, 2) + tuple(left.shape[:3]) + (2 * share,), BF16),
            line_left_sem=dma((lefts, 2)),
            core_out=pltpu.VMEM((count, 2, share, WIDE), BF16),
            core_in=pltpu.VMEM((count, 2, share, WIDE), BF16),
            line_own=pltpu.VMEM((count, 4, share, WIDE), BF16),
            line_in=pltpu.VMEM((count, 5, share, WIDE), BF16),
            core_send=dma((count, 2)),
            core_recv=dma((count, 2)),
            line_send=dma((count, 2, 3)),
            line_recv=dma((count, 2, 3)),
        )

    def left_copy(self, n, k):
        slot = k % 2
        at = tile_at(self.chunk_at(k), 2 * self.share)
        return pltpu.make_async_copy(
            self.lefts[n].at[:, :, :, at], self.r.line_left.at[n, slot], self.r.line_left_sem.at[n, slot]
        )

    def begin(self):
        for n in range(len(self.lefts)):
            self.left_copy(n, 0).start()

    def core_copy(self, g, k):
        r, slot = self.r, k % 2
        return remote(
            r.core_out.at[g, slot], r.core_in.at[g, slot], r.core_send.at[g, slot],
            r.core_recv.at[g, slot], {"img": self.twin},
        )

    def slot_at(self, way, s, line):
        first = (line < 2) if way == 0 else (line >= 2)
        return jnp.where(first, s, s + 2)

    def line_copy(self, g, way, s, chunk):
        r, ahead = self.r, 1 if way == 0 else -1
        return remote(
            r.line_own.at[g, chunk],
            r.line_in.at[g, self.slot_at(way, s, self.line + ahead)],
            r.line_send.at[g, way, s],
            r.line_recv.at[g, way, s],
            {"img": self.place + 2 * ahead},
        )

    def chunk_at(self, k):
        if k == 3:
            return self.line
        low = 3 - k - jnp.where(self.line + k == 3, 1, 0)
        high = k + jnp.where(self.line == k, 1, 0)
        return jnp.where(self.line < 2, low, high)

    def distance(self, way):
        return self.line if way == 0 else 3 - self.line

    def multiply(self, g, k):
        r = self.r
        left, name, column = self.pieces[g]
        right = r.loads.got(name) if name in r.loads.targets else getattr(r, name)
        right = all_rows(right, slice(column, column + WIDE))
        chunk = self.chunk_at(k)

        if k >= 2:
            self.core_copy(g, k).wait_send()
        for mine in (False, True):
            part = self.core if mine else 1 - self.core
            block = r.line_left[left, k % 2, :, :, :, tile_at(part, self.share)]
            done = product(block.reshape(-1, self.share), right, TN).astype(BF16)
            if mine:
                r.line_own[g, chunk] = done
            else:
                r.core_out[g, k % 2] = done
                self.core_copy(g, k).start()

    def add(self, g, chunk, arrived):
        own = self.r.line_own
        own[g, chunk] = (own[g, chunk].astype(F32) + arrived.astype(F32)).astype(BF16)

    def take(self, g, way, s, chunk):
        self.line_copy(g, way, s, chunk).wait_recv()
        self.add(g, chunk, self.r.line_in[g, self.slot_at(way, s, self.line)])

    def send_on(self, g, k):
        self.core_copy(g, k).wait_recv()
        self.add(g, self.chunk_at(k), self.r.core_in[g, k % 2])
        for way in range(2) if k < 3 else ():
            gone = self.distance(way)
            to = 3 - k + self.line if way == 0 else k - 3 + self.line

            @pl.when(gone <= k)
            def _():
                if k >= 1:

                    @pl.when(gone >= 1)
                    def _():
                        self.take(g, way, k - 1, to)

                self.line_copy(g, way, k, to).start()

    def tick(self, count=None):
        everything = 4 * (self.count + 1)
        for at in range(self.ticked, everything if count is None else min(self.ticked + count, everything)):
            k, g = divmod(at, self.count + 1)
            if g == 0:
                for n in range(len(self.lefts)):
                    self.left_copy(n, k).wait()
                    if k < 3:
                        self.left_copy(n, k + 1).start()
            if g < self.count:
                self.multiply(g, k)
            if g > 0:
                self.send_on(g - 1, k)
            self.ticked = at + 1

    def collect(self, g):
        for way in range(2):

            @pl.when(self.distance(way) >= 1)
            def _():
                self.take(g, way, 2, self.line)

        return self.r.line_own[g, self.line]

    def settle(self):
        for g in range(self.count):
            for k in (2, 3):
                self.core_copy(g, k).wait_send()

        def one(k, carry):
            for g in range(self.count):
                for way in range(2):

                    @pl.when(self.distance(way) <= k)
                    def _():
                        self.line_copy(g, way, k, self.line).wait_send()

            return carry

        lax.fori_loop(0, 3, one, 0)


class ImageSum:
    def __init__(self, square, part, first_in, second_out, second_in, send_sem, recv_sem):
        self.square, self.part = square, part
        self.first_in, self.second_out, self.second_in = first_in, second_out, second_in
        self.send_sem, self.recv_sem = send_sem, recv_sem
        self.half = part.shape[2] // 2
        self.summing, self.spreading, self.firsts = [], [], ([], [])

    def copy_to(self, kept, source, target, slot, peer):
        copy = remote(
            source, target, self.send_sem.at[slot], self.recv_sem.at[slot], {"mp": peer}
        )
        copy.start()
        kept.append(copy)

    def columns(self, side):
        return pl.ds(side * self.half, self.half)

    def start(self):
        square = self.square
        for order in range(2):
            for side in range(2):
                owner = square.peers[side] if order else square.corner
                self.copy_to(
                    self.summing,
                    self.part.at[owner, :, self.columns(side)],
                    self.first_in.at[side, order],
                    side * 2 + order,
                    square.peers[side],
                )

    def start_side(self, side):
        square = self.square
        for order in range(2):
            owner = square.peers[side] if order else square.corner
            self.copy_to(
                self.firsts[side],
                self.part.at[owner, :, self.columns(side)],
                self.first_in.at[side, order],
                side * 2 + order,
                square.peers[side],
            )
        if side == 1:
            self.summing = [self.firsts[0][0], self.firsts[1][0], self.firsts[0][1], self.firsts[1][1]]

    def forward(self):
        square = self.square
        for side in range(2):
            self.summing[side].wait_recv()
            own = self.part[square.peers[1 - side], :, self.columns(side)]
            self.second_out[side] = (
                own.astype(F32) + self.first_in[side, 0].astype(F32)
            ).astype(BF16)
            self.copy_to(
                self.summing, self.second_out.at[side], self.second_in.at[side], 4 + side,
                square.peers[1 - side],
            )

    def arrived(self):
        for copy in self.summing[2:]:
            copy.wait_recv()

    def total(self, at):
        return jnp.concatenate(
            [
                self.part[self.square.spot, at, self.columns(side)].astype(F32)
                + self.first_in[side, 1, at, :].astype(F32)
                + self.second_in[side, at, :].astype(F32)
                for side in range(2)
            ],
            axis=1,
        )

    def sent(self):
        for copy in self.summing:
            copy.wait_send()

    def spread(self, full, owner, side, slot, peer):
        where = full.at[owner, :, self.columns(side)]
        self.copy_to(self.spreading, where, where, slot, peer)

    def gather(self, full):
        square = self.square
        for slot, side, peer in ((6, 0, 1), (7, 1, 0), (8, 0, 0), (9, 1, 1)):
            self.spread(full, square.spot, side, slot, square.peers[peer])

    def pass_on(self, full):
        square = self.square
        self.spreading[0].wait_recv()
        self.spread(full, square.above, 0, 10, square.beside)
        self.spreading[1].wait_recv()
        self.spread(full, square.beside, 1, 11, square.above)

    def gathered(self):
        for copy in self.spreading[2:]:
            copy.wait_recv()

    def spread_sent(self):
        for copy in self.spreading:
            copy.wait_send()

    @staticmethod
    def scratch(stages, like, width):
        images, _, block = like.shape[:3]
        dma = pltpu.SemaphoreType.DMA
        lead = (stages, images)
        return dict(
            part=pltpu.VMEM((images, 4, block, width), BF16),
            first_in=pltpu.VMEM(lead + (2, 2, block, width // 2), BF16),
            second_out=pltpu.VMEM(lead + (2, block, width // 2), BF16),
            second_in=pltpu.VMEM(lead + (2, block, width // 2), BF16),
            sum_send=dma(lead + (12,)),
            sum_recv=dma(lead + (12,)),
        )

    @staticmethod
    def stage(r, square, t):
        return [
            ImageSum(
                square, r.part.at[i], r.first_in.at[t, i], r.second_out.at[t, i], r.second_in.at[t, i],
                r.sum_send.at[t, i], r.sum_recv.at[t, i],
            )
            for i in range(r.part.shape[0])
        ]


def project(r, i, left, weight, dims=NN):
    def one(j, carry):
        at = tile_at(j)
        done = product(left, weight[at, :] if dims == NT else weight[:, at], dims)
        put_image(r.part, i, at, done.astype(BF16))
        return carry

    lax.fori_loop(0, r.part.shape[3] // TILE, one, 0)


def softmax_rows(queries, keys_in):
    scores = product(queries, keys_in, NT) * SCALE
    powers = jnp.exp(scores - jnp.max(scores, axis=-1, keepdims=True))
    return powers * (1.0 / jnp.sum(powers, axis=-1, keepdims=True))


def attend(queries, keys_in, values_in):
    probs = softmax_rows(queries, keys_in).astype(BF16)
    return product(probs, values_in).astype(BF16)


def attend_backward_head(queries, keys_in, values_in, grad):
    probs = softmax_rows(queries, keys_in)
    grad_values = product(probs.astype(BF16), grad, TN).astype(BF16)
    grad_probs = product(grad, values_in, NT)
    centred = grad_probs - jnp.sum(probs * grad_probs, axis=-1, keepdims=True)
    grad_scores = (probs * centred * SCALE).astype(BF16)
    grad_queries = product(grad_scores, keys_in).astype(BF16)
    grad_keys = product(grad_scores, queries, TN).astype(BF16)
    return grad_queries, grad_keys, grad_values


def backward_heads(heads, read, write):
    def one(h, carry):
        done = attend_backward_head(*(read(n, h) for n in range(4)))
        for n in range(3):
            write(n, h, done[n])
        return carry

    lax.fori_loop(0, heads, one, 0)


def forward_kernel(r):
    loads = r.loads
    images, heads = r.own_self.shape[0], r.self_mixed.shape[3] // HDIM
    loads.start("projected", "attention_out", "entry", "cross_query", "text", "cross_out", "feed_grad", "feed_expand")
    stream = Stream(r.feed_shrink, r.tiles, r.tile_sem)
    stream.start()
    square = Square()
    place = lax.axis_index("img")
    peers = [lax.rem(place + j, 8) for j in range(1, 8)]
    greet(square.targets + [{"img": peer} for peer in peers])
    jobs = [ImageSum.stage(r, square, t) for t in range(2)]

    def caption_columns(owner):
        return r.caption.at[:, tile_at(owner, WIDE)]

    moves = [
        remote(
            caption_columns(peer), r.captions.at[place], r.move_send.at[j], r.move_recv.at[j], {"img": peer}
        )
        for j, peer in enumerate(peers)
    ]
    stay = pltpu.make_async_copy(caption_columns(place), r.captions.at[place], r.stay_sem.at[0])

    def self_stage(i):
        projected = loads.got("projected")

        def one(h, carry):
            parts = [image_rows(projected, i, tile_at(h + n * heads, HDIM)) for n in range(3)]
            put_image(r.self_mixed, i, tile_at(h, HDIM), attend(*parts))
            return carry

        lax.fori_loop(0, heads, one, 0)
        project(r, i, image_rows(r.self_mixed, i), loads.got("attention_out"))
        jobs[0][i].start()
        r.saves.save("self_mixed", i)

    def norm_stage(t, i, rows_ref, out_ref, full_ref):
        job = jobs[t][i]
        job.arrived()
        gain = r.gains[t + 1 : t + 2, :]
        for start in range(0, out_ref.shape[1], 32):
            at = slice(start, start + 32)
            wide_rows, narrow, _ = post_forward(job.total(at), (rows_ref[i, at, :],), gain)
            out_ref[i, at, :] = wide_rows
            full_ref[i, square.spot, at, :] = narrow

    def gather_stage(t, full_ref):
        for i in range(images):
            if t == 0:
                norm_stage(0, i, loads.got("entry"), r.own_self, full_ref)
            else:
                norm_stage(1, i, r.own_self, r.own_cross, full_ref)
            if i:
                jobs[t][i - 1].pass_on(full_ref.at[i - 1])
            jobs[t][i].gather(full_ref.at[i])

    def cross_stage(i):
        jobs[0][i].gathered()
        jobs[0][i].sent()
        r.saves.save("second_normed", i)
        r.saves.save("own_self", i)
        text = loads.got("text")
        queries = product(image_rows(r.second_normed, i), loads.got("cross_query")[...]).astype(BF16)
        put_image(r.queries, i, slice(None), queries)

        def one(h, carry):
            own, value = (tile_at(h + n * heads, HDIM) for n in range(2))
            done = attend(image_rows(r.queries, i, own), text[i, :, own], text[i, :, value])
            put_image(r.cross_mixed, i, own, done)
            return carry

        lax.fori_loop(0, heads, one, 0)
        project(r, i, image_rows(r.cross_mixed, i), loads.got("cross_out"))
        jobs[1][i].start()
        r.saves.save("queries", i)
        r.saves.save("cross_mixed", i)

    def shrink_back(j, weight):
        feed_grad = loads.got("feed_grad")
        for i in range(images):
            done = product(image_rows(feed_grad, i), weight, NT)
            put_image(r.grad_hidden, i, tile_at(j), done.astype(BF16))

    def feed_stage(i):
        jobs[1][i].gathered()
        r.saves.save("third_normed", i)
        r.saves.save("own_cross", i)
        expand = loads.got("feed_expand")

        def one(j, carry):
            at = tile_at(j)
            hidden = product(image_rows(r.third_normed, i), expand[:, at])
            spread = 0.5 + 0.5 * lax.erf(hidden * math.sqrt(0.5))
            slope = spread + hidden * jnp.exp(-0.5 * hidden * hidden) * (1.0 / math.sqrt(2.0 * math.pi))
            put_image(r.active, i, at, (hidden * spread).astype(BF16))
            grad = image_rows(r.grad_hidden, i, at).astype(F32) * slope
            put_image(r.grad_hidden, i, at, grad.astype(BF16))
            return carry

        lax.fori_loop(0, expand.shape[1] // TILE, one, 0)
        r.saves.save("active", i)
        r.saves.save("grad_hidden", i)

    first, second = jobs
    self_stage(0)
    stay.start()
    for copy in moves:
        copy.start()
    self_stage(1)
    first[0].forward()
    self_stage(2)
    first[1].forward()
    first[2].forward()
    loads.got("feed_grad")
    stream.run(0, stream.count // 2, shrink_back)
    gather_stage(0, r.second_normed)
    cross_stage(0)
    first[2].pass_on(r.second_normed.at[2])
    cross_stage(1)
    second[0].forward()
    cross_stage(2)
    second[1].forward()
    second[2].forward()
    stream.run(stream.count // 2, stream.count, shrink_back)
    gather_stage(1, r.third_normed)
    feed_stage(0)
    second[2].pass_on(r.third_normed.at[2])
    feed_stage(1)
    feed_stage(2)
    for job in first:
        job.spread_sent()
    for job in second:
        job.sent()
        job.spread_sent()
    stay.wait()
    for copy in moves:
        copy.wait()


def forward_rows(gains, projected, attention_out, entry, cross_query, text, cross_out, feed_grad, feed_expand, feed_shrink, caption):
    lead = projected.shape[:3]
    width, ff, head_wide = attention_out.shape[1], feed_expand.shape[1], attention_out.shape[0]
    dma = pltpu.SemaphoreType.DMA
    tiles, tile_sem = Stream.scratch(feed_shrink)
    own = struct((lead[0], lead[2], width), F32)
    return launch(
        forward_kernel,
        1,
        vmem=dict(gains=gains),
        loaded=dict(
            projected=projected, attention_out=attention_out, entry=entry, cross_query=cross_query,
            text=text, cross_out=cross_out, feed_grad=feed_grad, feed_expand=feed_expand,
        ),
        hbm=dict(feed_shrink=feed_shrink, caption=caption),
        saved=dict(
            self_mixed=struct(lead + (head_wide,), BF16),
            second_normed=struct(lead + (width,), BF16),
            queries=struct(lead + (head_wide,), BF16),
            cross_mixed=struct(lead + (head_wide,), BF16),
            third_normed=struct(lead + (width,), BF16),
            active=struct(lead + (ff,), BF16),
            grad_hidden=struct(lead + (ff,), BF16),
            own_self=own,
            own_cross=own,
        ),
        hbm_outs=dict(captions=struct((8, caption.shape[0], caption.shape[1] // 8), BF16)),
        scratch=dict(
            tiles=tiles, tile_sem=tile_sem, move_send=dma((7,)), move_recv=dma((7,)), stay_sem=dma((1,)),
            **ImageSum.scratch(2, projected, width),
        ),
    )


def back_norm(r, job, i, t, before, source, sum_ref, full_ref, square):
    job.arrived()
    gain = r.gains[t : t + 1, :]
    for start in range(0, r.own_grad.shape[1], 32):
        at = slice(start, start + 32)
        grad, narrow, (term,) = post_backward(job.total(at), (before(at), source[i, at, :]), gain)
        r.own_grad[i, at, :] = grad
        full_ref[i, square.spot, at, :] = narrow
        sum_ref[...] += term


def middle_kernel(r):
    loads = r.loads
    images, heads = r.own_grad.shape[0], r.grad_queries.shape[3] // HDIM
    square = Square()
    pieces = [(0, "active", c) for c in range(0, r.active.shape[3], WIDE)] + [(1, "grad_hidden", 0)]
    sums = LineSum(r, (r.feed_grad, r.third_normed), pieces)
    sums.begin()
    loads.start("grad_hidden", "active", "own_feed", "own_cross", "cross_out", "queries", "text", "cross_query", "own_self")
    stream = Stream(r.feed_expand, r.tiles, r.tile_sem, passes=images)
    stream.start()
    greet(square.targets + sums.targets)
    third, second = [ImageSum.stage(r, square, t) for t in range(2)]
    r.third_gain[...] = jnp.zeros_like(r.third_gain)
    r.second_gain[...] = jnp.zeros_like(r.second_gain)
    grad_hidden = loads.got("grad_hidden")

    def expand_back(i):
        rows = image_rows(grad_hidden, i)

        def one(j, weight):
            at = tile_at(lax.rem(j, stream.count))
            put_image(r.part, i, at, product(rows, weight, NT).astype(BF16))

        for side in range(2):
            first = i * stream.count + side * stream.count // 2
            stream.run(first, first + stream.count // 2, one)
            third[i].start_side(side)

    expand_back(0)
    expand_back(1)
    sums.tick(3)
    third[0].forward()
    expand_back(2)
    third[1].forward()
    sums.tick(2)
    third[2].forward()
    sums.tick(1)

    def third_stage(i):
        feed, source = loads.got("own_feed"), loads.got("own_cross")
        back_norm(
            r, third[i], i, 2, lambda at: feed[i, at, :].astype(F32), source, r.third_gain, r.cross_grad, square
        )

    def cross_stage(i):
        third[i].gathered()
        third[i].sent()
        r.saves.save("cross_grad", i)
        queries, text = loads.got("queries"), loads.got("text")
        r.mixed_grad[...] = product(
            image_rows(r.cross_grad, i), loads.got("cross_out")[...], NT
        ).astype(BF16)

        def read(n, h):
            own, value = (tile_at(h + m * heads, HDIM) for m in range(2))
            if n == 0:
                return image_rows(queries, i, own)
            return r.mixed_grad[:, own] if n == 3 else text[i, :, own if n == 1 else value]

        def write(n, h, done):
            own, value = (tile_at(h + m * heads, HDIM) for m in range(2))
            if n == 0:
                put_image(r.grad_queries, i, own, done)
            else:
                r.grad_text[i, :, own if n == 1 else value] = done

        backward_heads(heads, read, write)
        project(r, i, image_rows(r.grad_queries, i), loads.got("cross_query"), NT)
        second[i].start()
        r.saves.save("grad_queries", i)
        r.saves.save("grad_text", i)

    def second_stage(i):
        back_norm(
            r, second[i], i, 1, lambda at: r.own_grad[i, at, :], loads.got("own_self"), r.second_gain,
            r.self_grad, square,
        )

    for i in range(images):
        third_stage(i)
        if i:
            third[i - 1].pass_on(r.cross_grad.at[i - 1])
        third[i].gather(r.cross_grad.at[i])
    sums.tick(2)
    cross_stage(0)
    third[2].pass_on(r.cross_grad.at[2])
    sums.tick(2)
    cross_stage(1)
    second[0].forward()
    sums.tick(2)
    cross_stage(2)
    second[1].forward()
    sums.tick(1)
    second[2].forward()
    sums.tick(1)
    for i in range(images):
        second_stage(i)
        r.saves.save("own_grad", i)
        if i:
            second[i - 1].pass_on(r.self_grad.at[i - 1])
        second[i].gather(r.self_grad.at[i])
    sums.tick(3)
    second[2].pass_on(r.self_grad.at[2])
    sums.tick()
    for i in range(images):
        second[i].gathered()
        r.saves.save("self_grad", i)
    for g in range(sums.count):
        done = sums.collect(g)
        if g + 1 < sums.count:
            r.shrink_sum[g * WIDE : (g + 1) * WIDE, :] = done.astype(F32).T.astype(BF16)
        else:
            r.expand_sum[...] = done
    for job in second:
        job.sent()
    for job in third + second:
        job.spread_sent()
    sums.settle()


def middle_rows(gains, feed_grad, own_feed, rows, text, cross_out, cross_query, feed_expand):
    lead = feed_grad.shape[:3]
    width, head_wide, ff = feed_grad.shape[3], cross_out.shape[0], feed_expand.shape[1]
    share = width // 8
    tiles, tile_sem = Stream.scratch(feed_expand)
    narrow = struct(lead + (width,), BF16)
    gain = struct((1, width), F32)
    return launch(
        middle_kernel,
        2,
        vmem=dict(gains=gains),
        loaded=dict(
            active=rows.active, grad_hidden=rows.grad_hidden, own_feed=own_feed, own_cross=rows.own_cross,
            cross_out=cross_out, queries=rows.queries, text=text, cross_query=cross_query,
            own_self=rows.own_self,
        ),
        hbm=dict(feed_grad=feed_grad, third_normed=rows.third_normed, feed_expand=feed_expand),
        saved=dict(
            cross_grad=narrow,
            self_grad=narrow,
            grad_queries=struct(lead + (head_wide,), BF16),
            grad_text=struct(text.shape, BF16),
            own_grad=struct((lead[0], lead[2], width), F32),
        ),
        outs=dict(
            third_gain=gain,
            second_gain=gain,
            shrink_sum=struct((ff, share), BF16),
            expand_sum=struct((share, WIDE), BF16),
        ),
        scratch=dict(
            tiles=tiles, tile_sem=tile_sem, mixed_grad=pltpu.VMEM((lead[1] * lead[2], head_wide), BF16),
            **ImageSum.scratch(2, feed_grad, width), **LineSum.scratch(ff // WIDE + 1, 2, feed_grad),
        ),
    )


def entry_kernel(r):
    loads = r.loads
    images, heads = r.own_out.shape[0], r.grad_projected.shape[3] // (3 * HDIM)
    square = Square()
    pieces = [(0, "grad_hidden", c) for c in range(0, r.grad_hidden.shape[3], WIDE)]
    pieces += [(1, "grad_queries", 0), (2, "cross_mixed", 0)]
    sums = LineSum(r, (r.third_normed, r.second_normed, r.cross_grad), pieces)
    sums.begin()
    loads.start("grad_hidden", "grad_queries", "cross_mixed", "self_grad", "attention_out", "projected", "weight_in")
    loads.start("own_grad", "entry", "grad_text")
    text = Stream(r.weight_text, r.text_tiles, r.text_sem)
    text.start()
    greet(square.targets + sums.targets)
    (jobs,) = [ImageSum.stage(r, square, t) for t in range(1)]
    r.first_gain[...] = jnp.zeros_like(r.first_gain)
    r.embed_term[...] = jnp.zeros_like(r.embed_term)

    def text_at(line):
        return r.texts.at[line * 2 + sums.core]

    def text_along(way, hop):
        ahead = 1 if way == 0 else -1
        source = text_at(sums.line - ahead * hop) if hop else r.grad_text
        return remote(
            source, text_at(sums.line - ahead * hop), r.text_send.at[way, hop], r.text_recv.at[way, hop],
            {"img": sums.place + 2 * ahead},
        )

    def text_across(way, hop):
        line = sums.line - (hop + 1) * (1 if way == 0 else -1)
        return remote(
            text_at(line), text_at(line), r.twin_send.at[way, hop], r.twin_recv.at[way, hop],
            {"img": sums.twin},
        )

    stay = pltpu.make_async_copy(r.grad_text, text_at(sums.line), r.stay_sem.at[0])
    over = remote(r.grad_text, text_at(sums.line), r.twin_send.at[0, 3], r.twin_recv.at[0, 3], {"img": sums.twin})

    def text_sends(way, hop):
        return (sums.distance(way) >= hop) & (sums.distance(1 - way) >= 1)

    def text_step(hop):
        for way in range(2):
            if hop:

                @pl.when(sums.distance(way) >= hop)
                def _():
                    text_along(way, hop - 1).wait_recv()
                    text_across(way, hop - 1).start()

            if hop < 3:

                @pl.when(text_sends(way, hop))
                def _():
                    text_along(way, hop).start()

    def text_settle():
        stay.wait()
        over.wait()
        for way in range(2):
            for hop in range(3):

                @pl.when(text_sends(way, hop))
                def _():
                    text_along(way, hop).wait_send()

                @pl.when(sums.distance(way) >= hop + 1)
                def _():
                    text_across(way, hop).wait()

    def self_stage(i):
        projected = loads.got("projected")
        r.mixed_grad[...] = product(
            image_rows(loads.got("self_grad"), i), loads.got("attention_out")[...], NT
        ).astype(BF16)

        def read(n, h):
            if n == 3:
                return r.mixed_grad[:, tile_at(h, HDIM)]
            return image_rows(projected, i, tile_at(h + n * heads, HDIM))

        def write(n, h, done):
            put_image(r.grad_projected, i, tile_at(h + n * heads, HDIM), done)

        backward_heads(heads, read, write)
        project(r, i, image_rows(r.grad_projected, i), loads.got("weight_in"))
        jobs[i].start()
        r.saves.save("grad_projected", i)

    def entry_stage(i):
        job = jobs[i]
        job.arrived()
        before, entry = loads.got("own_grad"), loads.got("entry")
        for start in range(0, before.shape[1], 32):
            at = slice(start, start + 32)
            wide_rows, _, terms = post_entry(
                job.total(at), (before[i, at, :], entry[i, at, :], r.mask[i, at, :]), r.gains[0:1, :]
            )
            r.own_out[i, at, :] = wide_rows
            r.first_gain[...] += terms[0]
            r.embed_term[...] += terms[1]
        r.saves.save("own_out", i)

    def caption_tile(j, weight):
        grad = loads.got("grad_text")[...]
        done = product(grad.reshape(-1, grad.shape[2]), weight, NT)
        r.caption_part[:, tile_at(j)] = done.astype(BF16)

    stay.start()
    over.start()
    sums.tick(3)
    text_step(0)
    sums.tick(1)
    self_stage(0)
    sums.tick(2)
    self_stage(1)
    jobs[0].forward()
    sums.tick(3)
    self_stage(2)
    jobs[1].forward()
    sums.tick(2)
    jobs[2].forward()
    text_step(1)
    loads.got("grad_text")
    text.run(0, text.count // 2, caption_tile)
    sums.tick(3)
    text.run(text.count // 2, text.count, caption_tile)
    r.saves.save("caption_part")
    sums.tick(2)
    entry_stage(0)
    entry_stage(1)
    sums.tick(2)
    text_step(2)
    entry_stage(2)
    sums.tick()
    text_step(3)
    for g in range(sums.count - 2):
        r.expand_sum[:, g * WIDE : (g + 1) * WIDE] = sums.collect(g)
    r.query_sum[...] = sums.collect(sums.count - 2)
    r.cross_sum[...] = sums.collect(sums.count - 1).astype(F32).T.astype(BF16)
    for job in jobs:
        job.sent()
    text_settle()
    sums.settle()


def entry_rows(gains, mask, rows, back, projected, entry, attention_out, weight_in, weight_text, grad_hidden):
    lead = projected.shape[:3]
    width = attention_out.shape[1]
    share = width // 8
    dma = pltpu.SemaphoreType.DMA
    text_tiles, text_sem = Stream.scratch(weight_text)
    text_rows = back.grad_text.shape[0] * back.grad_text.shape[1]
    gain = struct((1, width), F32)
    return launch(
        entry_kernel,
        3,
        vmem=dict(gains=gains, mask=mask),
        loaded=dict(
            grad_hidden=grad_hidden, self_grad=back.self_grad, attention_out=attention_out,
            projected=projected, weight_in=weight_in, own_grad=back.own_grad, entry=entry,
            grad_text=back.grad_text, grad_queries=back.grad_queries, cross_mixed=rows.cross_mixed,
        ),
        hbm=dict(
            third_normed=rows.third_normed, second_normed=rows.second_normed, cross_grad=back.cross_grad,
            weight_text=weight_text,
        ),
        saved=dict(
            grad_projected=struct(projected.shape, BF16),
            own_out=struct(back.own_grad.shape, F32),
            caption_part=struct((text_rows, weight_text.shape[0]), BF16),
        ),
        outs=dict(
            first_gain=gain,
            embed_term=gain,
            expand_sum=struct((share, grad_hidden.shape[3]), BF16),
            query_sum=struct((share, WIDE), BF16),
            cross_sum=struct((WIDE, share), BF16),
        ),
        hbm_outs=dict(texts=struct((8,) + back.grad_text.shape, BF16)),
        scratch=dict(
            text_tiles=text_tiles, text_sem=text_sem,
            mixed_grad=pltpu.VMEM((lead[1] * lead[2], attention_out.shape[0]), BF16),
            text_send=dma((2, 3)), text_recv=dma((2, 3)), twin_send=dma((2, 4)), twin_recv=dma((2, 4)),
            stay_sem=dma((1,)),
            **ImageSum.scratch(1, projected, width),
            **LineSum.scratch(grad_hidden.shape[3] // WIDE + 2, 3, rows.third_normed),
        ),
    )


def line_kernel(r):
    square = Square()
    spot, beside, above, corner, peers = (
        square.spot, square.beside, square.above, square.corner, square.peers
    )
    pieces = [(0, "grad_projected", c) for c in (0, WIDE, 2 * WIDE)]
    pieces += [(1, "self_mixed", 0)]
    sums = LineSum(r, (r.first_normed, r.self_grad), pieces)
    sums.begin()
    loads = r.loads
    loads.start("grad_projected", "self_mixed", "active", "own_cross")
    shrink = Stream(r.feed_shrink, r.tiles, r.tile_sem, True)
    shrink.start()

    def text_load(j):
        slot = lax.rem(j, 2)
        return (
            pltpu.make_async_copy(r.captions.at[j], r.caption_block.at[slot], r.block_sem.at[0, slot]),
            pltpu.make_async_copy(r.texts.at[j], r.text_block.at[slot], r.block_sem.at[1, slot]),
        )

    for copy in text_load(0):
        copy.start()
    targets = [sums.targets[0]] + square.targets + sums.targets[1:] + [{"mp": corner}]
    rows, columns = r.held.shape[2], r.held.shape[3]
    greet(targets)

    low = rows // 3

    def row_block(owner, j):
        return owner * 3 + j

    def block(job, owner, side, j):
        if job == 0:
            b = row_block(owner, j)
            return r.mixed_part.at[lax.div(b, 4), lax.rem(b, 4), :, pl.ds(side * columns, columns)]
        at = pl.ds(pl.multiple_of(owner * columns, 128), columns)
        return r.caption_part.at[pl.ds(side * rows + j * low, low), at]

    thirds = [pl.ds(j * low, low) for j in range(3)]

    def load(job, slot, owner, side):
        return [
            pltpu.make_async_copy(
                block(job, owner, side, j), r.held.at[job, slot, thirds[j]], r.load_sem.at[job, slot, j]
            )
            for j in range(3)
        ]

    def first_copy(job, side, order):
        owner = corner if order == 0 else peers[side]
        slot = side * 2 + order
        return [
            remote(
                block(job, owner, side, j),
                r.flat_first.at[job, slot, thirds[j]],
                r.flat_send.at[job, slot, j],
                r.flat_recv.at[job, slot, j],
                {"mp": peers[side]},
            )
            for j in range(3)
        ]

    def second_copy(job, side):
        return remote(
            r.flat_out.at[job, side],
            r.flat_second.at[job, side],
            r.flat_send.at[job, 4 + side, 0],
            r.flat_recv.at[job, 4 + side, 0],
            {"mp": peers[1 - side]},
        )

    def flat_start(job):
        for order in range(2):
            for side in range(2):
                for copy in first_copy(job, side, order):
                    copy.start()
        for side in range(2):
            for copy in load(job, side, peers[1 - side], side) + load(job, 2 + side, spot, side):
                copy.start()

    def flat_forward(job):
        for side in range(2):
            for copy in load(job, side, peers[1 - side], side):
                copy.wait()
            for copy in first_copy(job, side, 0):
                copy.wait_recv()
            r.flat_out[job, side] = (
                r.held[job, side].astype(F32) + r.flat_first[job, side * 2].astype(F32)
            ).astype(BF16)
            second_copy(job, side).start()

    def flat_finish(job):
        for side in range(2):
            for copy in load(job, 2 + side, spot, side):
                copy.wait()
            for copy in first_copy(job, side, 1):
                copy.wait_recv()
            second_copy(job, side).wait_recv()
            total = (
                r.held[job, 2 + side].astype(F32)
                + r.flat_first[job, side * 2 + 1].astype(F32)
                + r.flat_second[job, side].astype(F32)
            )
            if job == 0:
                r.mixed_out[:, side * columns : (side + 1) * columns] = total.astype(BF16)
            else:
                r.caption_out[side * rows : (side + 1) * rows, :] = total.astype(BF16)
        for side in range(2):
            for order in range(2):
                for copy in first_copy(job, side, order):
                    copy.wait_send()
            second_copy(job, side).wait_send()

    def move(i):
        b = i * 4 + spot
        keeper, j = lax.div(b, 3), lax.rem(b, 3)
        target = r.tokens_out.at[pl.ds(pl.multiple_of(j * low, low), low)]
        away = remote(
            r.own_out.at[i], target, r.move_send.at[i], r.move_recv.at[j], {"mp": keeper}
        )
        here = pltpu.make_async_copy(r.own_out.at[i], target, r.stay_sem.at[0])
        return keeper, away, here

    def move_start():
        for i in range(3):
            keeper, away, here = move(i)

            @pl.when(keeper != spot)
            def _():
                away.start()

            @pl.when(keeper == spot)
            def _():
                here.start()

    def move_finish():
        for i in range(3):
            keeper, away, here = move(i)

            @pl.when(keeper != spot)
            def _():
                away.wait_send()

            @pl.when(keeper == spot)
            def _():
                here.wait()

        for j in range(3):
            arrival = remote(
                r.own_out.at[0], r.tokens_out.at[thirds[j]], r.move_send.at[0], r.move_recv.at[j], {"mp": corner}
            )

            @pl.when(lax.rem(row_block(spot, j), 4) != spot)
            def _():
                arrival.wait_recv()

    def mixed_tile(j, weight):
        done = product(all_rows(loads.got("active")), weight).astype(BF16)
        at = tile_at(j)
        r.mixed_part[:, :, :, at] = done.reshape(r.mixed_part.shape[:3] + (TILE,))
        for i in range(3):
            own = r.mixed_part[i, spot, :, at].astype(F32) + loads.got("own_cross")[i, :, at]
            r.mixed_part[i, spot, :, at] = own.astype(BF16)

    def text_product(j, carry):
        for copy in text_load(j):
            copy.wait()

        @pl.when(j < 7)
        def _():
            for copy in text_load(j + 1):
                copy.start()

        left = r.caption_block[lax.rem(j, 2)]

        def one(n, inner):
            at = tile_at(n)
            right = r.text_block[lax.rem(j, 2), :, :, at]
            r.text_sum[:, at] += product(left, right.reshape(-1, TILE), TN)
            return inner

        return lax.fori_loop(0, r.text_sum.shape[1] // TILE, one, carry)

    def small_step(slot, device):
        copy = remote(
            r.small_out, r.small_in.at[slot], r.small_send.at[slot], r.small_recv.at[slot], device
        )
        copy.start()
        return copy

    r.small_out[...] = r.small[...]
    r.text_sum[...] = jnp.zeros_like(r.text_sum)

    def small_add(slot, copy):
        copy.wait()
        r.small_out[...] += r.small_in[slot]

    copy = small_step(0, targets[0])
    sums.tick(2)
    small_add(0, copy)
    copy = small_step(1, targets[1])
    sums.tick(1)
    small_add(1, copy)
    copy = small_step(2, targets[2])
    flat_start(1)
    move_start()
    sums.tick(2)
    small_add(2, copy)
    wide = [small_step(3 + j, device) for j, device in enumerate(targets[3:6])]
    loads.got("active")
    loads.got("own_cross")
    shrink.run(0, shrink.count, mixed_tile)
    flat_start(0)
    sums.tick(2)
    flat_forward(1)
    lax.fori_loop(0, 4, text_product, 0)
    sums.tick(2)
    lax.fori_loop(4, 8, text_product, 0)
    sums.tick(2)
    flat_forward(0)
    flat_finish(1)
    sums.tick(2)
    move_finish()
    sums.tick()
    flat_finish(0)
    for copy in wide:
        copy.wait()
    r.small_out[...] += r.small_in[3] + r.small_in[4] + r.small_in[5]
    for g in range(3):
        r.in_sum[:, g * WIDE : (g + 1) * WIDE] = sums.collect(g)
    r.self_sum[...] = sums.collect(3).astype(F32).T.astype(BF16)
    sums.settle()


def line_sums(first_normed, rows, back, entry, small, feed_shrink):
    images, low, full = entry.own_out.shape
    height, columns = images * low, full // 2
    share = full // 8
    dma = pltpu.SemaphoreType.DMA
    block = (height, columns)
    lead = first_normed.shape[:3]
    tiles, tile_sem = Stream.scratch(feed_shrink, True)
    captions, texts = rows.captions, entry.texts
    return launch(
        line_kernel,
        4,
        vmem=dict(small=small),
        loaded=dict(
            grad_projected=entry.grad_projected, self_mixed=rows.self_mixed, active=rows.active,
            own_cross=rows.own_cross,
        ),
        hbm=dict(
            first_normed=first_normed, self_grad=back.self_grad, caption_part=entry.caption_part,
            own_out=entry.own_out, feed_shrink=feed_shrink, captions=captions, texts=texts,
        ),
        outs=dict(
            in_sum=struct((share, 3 * WIDE), BF16),
            self_sum=struct((WIDE, share), BF16),
            text_sum=struct((captions.shape[2], texts.shape[3]), F32),
            small_out=struct(small.shape, F32),
            mixed_out=struct((height, full), BF16),
            caption_out=struct((entry.caption_part.shape[0], columns), BF16),
            tokens_out=struct((height, full), F32),
        ),
        scratch=dict(
            mixed_part=pltpu.VMEM(lead + (full,), BF16),
            tiles=tiles, tile_sem=tile_sem,
            caption_block=pltpu.VMEM((2,) + captions.shape[1:], BF16),
            text_block=pltpu.VMEM((2,) + texts.shape[1:], BF16),
            block_sem=dma((2, 2)),
            small_in=pltpu.VMEM((6,) + small.shape, F32),
            held=pltpu.VMEM((2, 4) + block, BF16),
            flat_first=pltpu.VMEM((2, 4) + block, BF16),
            flat_out=pltpu.VMEM((2, 2) + block, BF16),
            flat_second=pltpu.VMEM((2, 2) + block, BF16),
            small_send=dma((6,)),
            small_recv=dma((6,)),
            load_sem=dma((2, 4, 3)),
            flat_send=dma((2, 6, 3)),
            flat_recv=dma((2, 6, 3)),
            stay_sem=dma((1,)),
            move_send=dma((3,)),
            move_recv=dma((3,)),
            **LineSum.scratch(4, 2, first_normed),
        ),
    )


def plain_step(left, weight, dims, post, gain, rows_in):
    part = product(left, weight, dims).astype(BF16)
    total = lax.psum_scatter(part, "mp", scatter_dimension=0, tiled=True).astype(F32)
    wide, narrow, sums = post(total, rows_in, gain)
    if narrow is None:
        return (wide, *sums)
    return (wide, lax.all_gather(narrow, "mp", axis=0, tiled=True), *sums)


def plain_heads(array, images, parts=1):
    rows, columns = array.shape
    return array.reshape(images, rows // images, parts, -1, HDIM).transpose(2, 0, 3, 1, 4)


def plain_rows(array):
    images, heads, rows, _ = array.shape
    return array.transpose(0, 2, 1, 3).reshape(images * rows, heads * HDIM)


def per_head(function):
    return jax.vmap(jax.vmap(function))


def gelu_exact(values_in):
    return jax.nn.gelu(values_in, approximate=False)


def layer_plain(images, own_rows, gains, own_entry, own_float, first_normed, projected, text_pairs, feed_grad, weights):
    attention_out, cross_query, cross_out, feed_expand, feed_shrink, weight_in, weight_text, caption = weights
    queries, keys_in, values_in = plain_heads(projected, images, 3)
    text_keys, text_values = plain_heads(text_pairs, images, 2)
    self_mixed = plain_rows(per_head(attend)(queries, keys_in, values_in))
    own_self, second_normed = plain_step(
        self_mixed, attention_out, NN, post_forward, gains[1:2], (own_entry,)
    )
    cross_queries = plain_heads(product(second_normed, cross_query).astype(BF16), images)[0]
    cross_mixed = plain_rows(per_head(attend)(cross_queries, text_keys, text_values))
    own_cross, third_normed = plain_step(
        cross_mixed, cross_out, NN, post_forward, gains[2:3], (own_self,)
    )
    hidden = product(third_normed, feed_expand)
    active = gelu_exact(hidden).astype(BF16)
    mixed_sum = lax.psum_scatter(
        product(active, feed_shrink).astype(BF16), "mp", scatter_dimension=0, tiled=True
    )
    mixed_out = (own_cross + mixed_sum.astype(F32)).astype(BF16)
    _, gelu_pull = jax.vjp(gelu_exact, hidden)
    grad_hidden = gelu_pull(product(feed_grad, feed_shrink, NT))[0].astype(BF16)
    own_grad, cross_grad, third_gain = plain_step(
        grad_hidden, feed_expand, NT, post_backward, gains[2:3],
        (own_rows(feed_grad).astype(F32), own_cross),
    )
    grad_mixed = plain_heads(product(cross_grad, cross_out, NT).astype(BF16), images)[0]
    back = per_head(attend_backward_head)(cross_queries, text_keys, text_values, grad_mixed)
    grad_queries, grad_keys, grad_values = (plain_rows(part) for part in back)
    grad_text = jnp.concatenate([grad_keys, grad_values], axis=1)
    own_grad, self_grad, second_gain = plain_step(
        grad_queries, cross_query, NT, post_backward, gains[1:2], (own_grad, own_self)
    )
    grad_mixed = plain_heads(product(self_grad, attention_out, NT).astype(BF16), images)[0]
    back = per_head(attend_backward_head)(queries, keys_in, values_in, grad_mixed)
    grad_projected = jnp.concatenate([plain_rows(part) for part in back], axis=1)
    tokens_grad, first_gain, embed_term = plain_step(
        grad_projected, weight_in, NN, post_entry, gains[0:1], (own_grad, own_entry, own_float)
    )
    caption_grad = lax.psum_scatter(
        product(grad_text, weight_text, NT).astype(BF16), "mp", scatter_dimension=1, tiled=True
    )
    small = jnp.concatenate([first_gain, second_gain, third_gain, embed_term], axis=0)
    return (
        mixed_out,
        tokens_grad,
        caption_grad,
        lax.psum_scatter(small, ("img", "mp"), scatter_dimension=1, tiled=True),
        image_sum(rows_product(first_normed, grad_projected)),
        image_sum(rows_product(self_mixed, self_grad), 1),
        image_sum(rows_product(second_normed, grad_queries)),
        image_sum(rows_product(caption, grad_text)),
        image_sum(rows_product(cross_mixed, cross_grad), 1),
        image_sum(rows_product(third_normed, grad_hidden)),
        image_sum(rows_product(active, feed_grad), 1),
    )


def layer_square(images, own_mask, gains, own_entry, first_normed, projected, text_pairs, feed_grad, weights):
    attention_out, cross_query, cross_out, feed_expand, feed_shrink, weight_in, weight_text, caption = weights
    width = first_normed.shape[1]
    spot = lax.axis_index("mp")

    def four(rows_in):
        return rows_in.reshape(images, 4, -1, rows_in.shape[-1])

    text = text_pairs.reshape(images, -1, text_pairs.shape[1])
    four_grad, four_projected, four_normed = four(feed_grad), four(projected), four(first_normed)
    own_feed = lax.dynamic_index_in_dim(four_grad, spot, 1, False)
    rows = forward_rows(
        gains, four_projected, attention_out, own_entry, cross_query, text, cross_out, four_grad,
        feed_expand, feed_shrink, caption,
    )
    back = middle_rows(gains, four_grad, own_feed, rows, text, cross_out, cross_query, feed_expand)
    entry = entry_rows(
        gains, own_mask, rows, back, four_projected, own_entry, attention_out, weight_in, weight_text,
        rows.grad_hidden[:, :, :, WIDE:],
    )
    terms = [entry.first_gain, back.second_gain, back.third_gain, entry.embed_term]
    small = jnp.concatenate(terms + [jnp.zeros_like(entry.embed_term)] * 4, axis=0)
    late = line_sums(four_normed, rows, back, entry, small, feed_shrink)
    slice_width = width // 32
    at = (lax.axis_index("img") * 4 + spot) * slice_width
    return (
        late.mixed_out,
        late.tokens_out,
        late.caption_out,
        lax.dynamic_slice_in_dim(late.small_out, at, slice_width, 1),
        late.in_sum,
        late.self_sum,
        entry.query_sum,
        late.text_sum,
        entry.cross_sum,
        jnp.concatenate([back.expand_sum, entry.expand_sum], axis=1),
        back.shrink_sum,
    )


def body(
    square,
    tokens,
    caption,
    masked,
    out_grad,
    mask_embed,
    norm_gains,
    attention_in,
    attention_out,
    cross_query,
    cross_text,
    cross_out,
    feed_expand,
    feed_shrink,
):
    images, length = masked.shape
    rows_all = images * length
    count = lax.axis_size("mp")
    spot = lax.axis_index("mp")
    text_width = caption.shape[1]

    def own_rows(rows_in):
        return lax.dynamic_slice_in_dim(rows_in, spot * (rows_all // count), rows_all // count, 0)

    def own_quarters(rows_in):
        parts = rows_in.reshape(images, count, length // count, -1)
        return lax.dynamic_index_in_dim(parts, spot, 1, False)

    def enter(rows_in, mask):
        return jnp.where(mask, mask_embed.astype(F32), rows_in.astype(F32))

    own = own_quarters if square else own_rows
    mask_column = masked.reshape(rows_all, 1) > 0
    own_mask = own(mask_column)
    own_float = own_mask.astype(F32)
    own_entry = enter(own(tokens), own_mask)
    first_unit, _ = norm_parts(enter(tokens, mask_column))
    first_normed = (first_unit * norm_gains[0:1]).astype(BF16)
    weight_in = attention_in.transpose(1, 2, 0).reshape(-1, tokens.shape[1])
    projected = product(first_normed, weight_in, NT).astype(BF16)
    weight_text = cross_text.reshape(text_width, -1)
    text_pairs = product(caption, weight_text).astype(BF16)
    feed_grad = jnp.where(mask_column, out_grad, jnp.zeros_like(out_grad))
    weights = (
        attention_out, cross_query, cross_out, feed_expand, feed_shrink, weight_in, weight_text, caption,
    )
    if square:
        done = layer_square(
            images, own_float, norm_gains, own_entry, first_normed, projected, text_pairs, feed_grad, weights
        )
    else:
        done = layer_plain(
            images, own_rows, norm_gains, own_entry, own_float, first_normed, projected, text_pairs,
            feed_grad, weights,
        )
    mixed_out, tokens_grad, caption_grad, small_sums, self_in, *sums = done
    self_out, cross_query_sum, cross_text_sum, cross_out_sum, expand_sum, shrink_sum = (
        part.astype(F32) for part in sums
    )
    return (
        mixed_out,
        tokens_grad,
        caption_grad.astype(F32),
        small_sums[3],
        small_sums[0:3],
        self_in.astype(F32).reshape(-1, 3, attention_in.shape[2]),
        self_out,
        cross_query_sum,
        cross_text_sum.reshape(-1, 2, cross_text.shape[2]),
        cross_out_sum,
        expand_sum,
        shrink_sum,
    )


def solution(mesh):
    square = mesh.shape["mp"] == 4 and mesh.shape["img"] == 8
    return jax.shard_map(
        functools.partial(body, square),
        mesh=mesh,
        in_specs=(
            P("img", None),
            P("img", None),
            P("img", None),
            P("img", None),
            P(),
            P(),
            P(None, None, "mp"),
            P("mp", None),
            P(None, "mp"),
            P(None, None, "mp"),
            P("mp", None),
            P(None, "mp"),
            P("mp", None),
        ),
        out_specs=(
            P(("img", "mp"), None),
            P(("img", "mp"), None),
            P("img", "mp"),
            P(("img", "mp")),
            P(None, ("img", "mp")),
            P("img", None, "mp"),
            P("mp", "img"),
            P("img", "mp"),
            P("img", None, "mp"),
            P("mp", "img"),
            P("img", "mp"),
            P("mp", "img"),
        ),
        check_vma=False,
    )
```

time: 1740 us -> 564 us (0.32)
  waiting for transfers between devices: 1280 us -> 0 us
  Pallas kernels: 0 us -> 478 us
  matrix products: 222 us -> 16 us
  local copies, waits for them, and re-layouts: 123 us -> 36.4 us
  other arithmetic: 87 us -> 21.5 us
    psum x5 -> x0, waiting for transfers between devices: 695 us -> none  [the longest x3 496 us: reduce_branch(): return lax.psum(partial_rows, 'mp')]
    pallas_call x0 -> x4, Pallas kernels: none -> 478 us  [launch(): pl.pallas_call(run, out_shape=[*outs.values(), *saved.values(), *hbm_outs...]
    reduce_scatter x7 -> x0, waiting for transfers between devices: 311 us -> none  [the longest x1 88.7 us: body(): lax.psum_scatter(shrink_sum.astype(jnp.bfloat16), 'img', scatter_dimensio...]
    unnamed x16 -> x0, waiting for transfers between devices: 276 us -> none
    dot_general x33 -> x2, matrix products: 222 us -> 16 us  [product(): return lax.dot_general(left, right, dims, preferred_element_type=F32)]
    convert_element_type x8 -> x1, local copies, waits for them, and re-layouts: 39.8 us -> 0.75 us  [body(): own_float = own_mask.astype(F32)]
    unnamed x114 -> x39, local copies, waits for them, and re-layouts: 49.2 us -> 13.2 us
    reduce_sum x8 -> x0, other arithmetic: 24.7 us -> none  [the longest x3 15.9 us: norm_back(): middle = jnp.mean(weighted, axis=-1, keepdims=True)]
  transfers between devices with their start and end apart: 14 -> 0, of which waited for: 12 -> 0; matrix products, arithmetic and copies ran while one was open for 14% -> 0% of each run, Pallas kernels for 0% -> 0%
where the time goes in v4:
time: 564 us; the launch traced here: 553 us
  Pallas kernels  478 us (85%)
  local copies, waits for them, and re-layouts  36.4 us (6%)
  other arithmetic  21.5 us (4%)
  matrix products  16 us (3%)
    pallas_call x4, Pallas kernels, launch(): pl.pallas_call(run, out_shape=[*outs.values(), *saved.values(), *hbm_outs...  478 us
    dot_general x2, matrix products, product(): return lax.dot_general(left, right, dims, preferred_element_type=F32)  16 us
    unnamed x39, local copies, waits for them, and re-layouts  13.2 us

profile of v4, /device:TPU:0, one launch (start us, length us, event | category | flops | bytes accessed | tf_op | source)
XLA Modules:
  0.0 552.8 jit_solution(8015744929642908043)
XLA Ops:
  0.6 0.0 copy-start
  0.7 0.8 broadcast_compare_fusion
  1.5 0.1 gt.26
  1.6 0.6 convert_bitcast_fusion
  2.2 0.7 convert_element_type.48
  2.9 2.5 convert_select_fusion.1.refs_3_.refs_8_
  5.3 2.7 fusion.1
  8.0 0.0 copy-done
  8.0 1.6 multiply_reduce_fusion
  9.7 0.0 slice-done
  9.7 2.7 multiply_convert_fusion
  12.4 9.0 %copy.32 = bf16[3,512,2048]{2,1,0:T(8,128)(2,1)} copy(bf16[3,512,2048]{1,2,0:T(8,128)(2,1)} %bitcast.33) | data formatting | bytes 12582912 | tf_op jit(solution)/shard_map/transpose | solution.py:1552
  21.4 0.0 copy-done.2
  21.4 9.2 %convolution_convert_fusion = bf16[768,1536]{1,0:T(8,128)(2,1)} fusion(bf16[768,2048]{1,0:T(8,128)(2,1)S(1)} %copy-done.2, bf16[1536,2048]{1,0:T(8,128)(2,1)} %bitcast.34), kind=kOutput, calls=%fused_computation.5 | convolution fusion | flops 4833017856 | bytes 11796480 | tf_op jit(solution)/shard_map/dot_general | solution.py:30
  30.6 0.0 copy-done.1
  30.6 1.9 broadcast_select_fusion
  32.5 9.5 %copy.39 = bf16[512,8,2,512]{3,1,2,0:T(8,128)(2,1)} copy(bf16[512,8,2,512]{3,2,1,0:T(2,128)(2,1)} %bitcast.30) | data formatting | bytes 16777216
  42.0 0.0 copy-done.16
  42.0 6.8 %convolution_convert_fusion.1 = bf16[384,1024]{1,0:T(8,128)(2,1)} fusion(bf16[384,4096]{1,0:T(8,128)(2,1)S(1)} %copy-done.16, bf16[4096,1024]{1,0:T(8,128)(2,1)} %bitcast.31), kind=kOutput, calls=%fused_computation.8 | convolution fusion | flops 3221618688 | bytes 12320768 | tf_op jit(solution)/shard_map/dot_general | solution.py:30
  48.8 121.0 %shard_map.220 = (bf16[3,4,64,512]{3,2,1,0:T(8,128)(2,1)}, bf16[3,4,64,2048]{3,2,1,0:T(8,128)(2,1)}, bf16[3,4,64,512]{3,2,1,0:T(8,128)(2,1)}, bf16[3,4,64,512]{3...) custom-call(f32[3,2048]{1,0:T(4,128)} %refs_0_.5, ...), custom_call_target="tpu_custom_call" | custom-call | flops 60000002048 | bytes 80000000 | tf_op jit(solution)/shard_map/pallas_call | solution.py:208
  169.8 2.1 dynamic-slice_bitcast_fusion.refs_3_
  171.9 142.4 %shard_map.221 = (f32[1,2048]{1,0:T(1,128)}, f32[1,2048]{1,0:T(1,128)}, bf16[2048,256]{1,0:T(8,128)(2,1)}, bf16[256,512]{1,0:T(8,128)(2,1)}, bf16[3,4,64,2048]{3...) custom-call(f32[3,2048]{1,0:T(4,128)} %refs_0_.5, ...), custom_call_target="tpu_custom_call" | custom-call | flops 60000002048 | bytes 80000000 | tf_op jit(solution)/shard_map/pallas_call | solution.py:208
  314.3 0.0 copy-start.15
  314.3 3.2 slice.13.refs_2_
  317.5 0.0 copy-done.15
  317.5 0.8 copy.34.refs_1_
  318.3 120.8 %shard_map.222 = (f32[1,2048]{1,0:T(1,128)}, f32[1,2048]{1,0:T(1,128)}, bf16[256,1536]{1,0:T(8,128)(2,1)}, bf16[256,512]{1,0:T(8,128)(2,1)}, bf16[512,256]{1,0:T...) custom-call(f32[3,2048]{1,0:T(4,128)} %refs_0_.5, ...), custom_call_target="tpu_custom_call" | custom-call | flops 60000002048 | bytes 80000000 | tf_op jit(solution)/shard_map/pallas_call | solution.py:208
  439.1 2.7 maximum_convert_fusion
  441.8 0.0 copy-done.12
  441.8 0.0 copy-done.13
  441.8 0.0 copy-done.14
  441.8 0.7 concatenate.10.refs_0_
  442.5 93.5 %shard_map.223 = (bf16[256,1536]{1,0:T(8,128)(2,1)}, bf16[512,256]{1,0:T(8,128)(2,1)}, f32[512,1024]{1,0:T(8,128)}, f32[8,2048]{1,0:T(8,128)}, bf16[192,2048]{1,...) custom-call(f32[8,2048]{1,0:T(8,128)} %concatenate.10.refs_0_, ...), custom_call_target="tpu_custom_call" | custom-call | flops 60000002048 | bytes 80000000 | tf_op jit(solution)/shard_map/pallas_call | solution.py:208
  536.0 1.4 copy.35
  537.5 1.6 copy.36
  539.1 4.1 reshape.115
  543.1 1.3 convert_element_type.55
  544.5 0.8 convert_element_type.56
  545.3 0.7 constant_dynamic-slice_fusion
  546.0 0.6 slice.15
  546.6 0.5 slice_bitcast_fusion
  547.1 0.0 copy-done.8
  547.1 0.9 convert_element_type.57
  548.0 0.8 convert_element_type.58
  548.8 1.5 convert_element_type.60
  550.3 0.9 copy.44
  551.2 0.0 copy-done.3
  551.2 1.1 copy.45
  (28 shorter events, 0.1 us)
Async XLA Ops:
  0.6 7.4 %copy-start = (bf16[768,2048]{1,0:T(8,128)(2,1)S(1)}, bf16[768,2048]{1,0:T(8,128)(2,1)}, u32[]{:S(2)}) copy-start(bf16[768,2048]{1,0:T(8,128)(2,1)} %param.13) | copy-start | bytes 9437188
  5.3 4.3 slice-start
  12.4 9.0 %copy-start.2 = (bf16[768,2048]{1,0:T(8,128)(2,1)S(1)}, bf16[768,2048]{1,0:T(8,128)(2,1)}, u32[]{:S(2)}) copy-start(bf16[768,2048]{1,0:T(8,128)(2,1)} %multiply_convert_fusion) | copy-start | bytes 9437188
  21.4 9.2 %copy-start.1 = (bf16[768,2048]{1,0:T(8,128)(2,1)S(1)}, bf16[768,2048]{1,0:T(8,128)(2,1)}, u32[]{:S(2)}) copy-start(bf16[768,2048]{1,0:T(8,128)(2,1)} %param.16) | copy-start | bytes 9437188
  32.5 9.5 %copy-start.16 = (bf16[384,4096]{1,0:T(8,128)(2,1)S(1)}, bf16[384,4096]{1,0:T(8,128)(2,1)}, u32[]{:S(2)}) copy-start(bf16[384,4096]{1,0:T(8,128)(2,1)} %refs_10_.1) | copy-start | bytes 9437188
  314.3 3.2 copy-start.15
  318.2 120.8 %copy-start.9 = (bf16[256,512]{1,0:T(8,128)(2,1)S(1)}, bf16[256,512]{1,0:T(8,128)(2,1)}, u32[]{:S(2)}) copy-start(bf16[256,512]{1,0:T(8,128)(2,1)} %get-tuple-element.79) | copy-start | bytes 786436
  439.0 2.8 copy-start.11
  439.0 2.8 copy-start.12
  439.0 2.8 copy-start.13
  439.0 2.8 copy-start.14
  537.4 5.7 %copy-start.6 = (bf16[384,1024]{1,0:T(8,128)(2,1)S(1)}, bf16[384,1024]{1,0:T(8,128)(2,1)}, u32[]{:S(2)}) copy-start(bf16[384,1024]{1,0:T(8,128)(2,1)} %get-tuple-element.72) | copy-start | bytes 2359300
  539.1 5.4 copy-start.10
  539.1 8.1 %copy-start.8 = (bf16[256,512]{1,0:T(8,128)(2,1)S(1)}, bf16[256,512]{1,0:T(8,128)(2,1)}, u32[]{:S(2)}) copy-start(bf16[256,512]{1,0:T(8,128)(2,1)} %get-tuple-element.76) | copy-start | bytes 786436
  539.1 8.9 %copy-start.7 = (bf16[512,256]{1,0:T(8,128)(2,1)S(1)}, bf16[512,256]{1,0:T(8,128)(2,1)}, u32[]{:S(2)}) copy-start(bf16[512,256]{1,0:T(8,128)(2,1)} %get-tuple-element.78) | copy-start | bytes 786436
  543.1 5.7 %copy-start.4 = (bf16[2048,256]{1,0:T(8,128)(2,1)S(1)}, bf16[2048,256]{1,0:T(8,128)(2,1)}, u32[]{:S(2)}) copy-start(bf16[2048,256]{1,0:T(8,128)(2,1)} %get-tuple-element.81) | copy-start | bytes 3145732
  544.5 5.8 %copy-start.5 = (bf16[192,2048]{1,0:T(8,128)(2,1)S(1)}, bf16[192,2048]{1,0:T(8,128)(2,1)}, u32[]{:S(2)}) copy-start(bf16[192,2048]{1,0:T(8,128)(2,1)} %get-tuple-element.132) | copy-start | bytes 2359300
  547.1 4.1 copy-start.3

commit v5 on v4

--- a/solution.py
+++ b/solution.py
@@ -14,12 +14,15 @@
 HDIM = 128
 EPSILON = 1e-05
 SCALE = 1.0 / math.sqrt(HDIM)
-VMEM_BYTES = 61 * 1024 * 1024
+VMEM_BYTES = 62 * 1024 * 1024
 MESH = pl.DeviceIdType.MESH
 BF16 = jnp.bfloat16
 F32 = jnp.float32
 WIDE = 512
 TILE = 256
+
+MIDDLE_TICKS = (1, 1, 1, 5, 0, 1, 0, 4, 2, 0, 2, 0, 0, 4, 1, 2, 0, 2, 1)
+ENTRY_TICKS = (4, 0, 0, 0, 0, 0, 4, 4, 0, 2, 1, 2, 1, 1, 0, 0, 0, 0, 0, 1)
 
 NN = (((1,), (0,)), ((), ()))
 NT = (((1,), (1,)), ((), ()))
@@ -136,33 +139,35 @@
     def __init__(self, source, tiles, sem, columns=False, passes=1):
         self.source, self.tiles, self.sem, self.columns = source, tiles, sem, columns
         self.count = source.shape[1 if columns else 0] // TILE
-        self.total = passes * self.count
+        self.total, self.depth = passes * self.count, tiles.shape[0]
 
     def copy(self, j):
-        slot, at = lax.rem(j, 2), tile_at(lax.rem(j, self.count))
+        slot, at = lax.rem(j, self.depth), tile_at(lax.rem(j, self.count))
         part = self.source.at[:, at] if self.columns else self.source.at[at, :]
         return pltpu.make_async_copy(part, self.tiles.at[slot], self.sem.at[slot])
 
     def start(self):
-        self.copy(0).start()
+        for j in range(self.depth - 1):
+            self.copy(j).start()
 
     def run(self, first, last, use):
         def one(j, carry):
             self.copy(j).wait()
-
-            @pl.when(j + 1 < self.total)
+            later = j + self.depth - 1
+
+            @pl.when(later < self.total)
             def _():
-                self.copy(j + 1).start()
-
-            use(j, self.tiles[lax.rem(j, 2)])
+                self.copy(later).start()
+
+            use(j, self.tiles[lax.rem(j, self.depth)])
             return carry
 
         lax.fori_loop(first, last, one, 0)
 
     @staticmethod
-    def scratch(source, columns=False):
+    def scratch(source, columns=False, depth=2):
         shape = (source.shape[0], TILE) if columns else (TILE, source.shape[1])
-        return pltpu.VMEM((2,) + shape, source.dtype), pltpu.SemaphoreType.DMA((2,))
+        return pltpu.VMEM((depth,) + shape, source.dtype), pltpu.SemaphoreType.DMA((depth,))
 
 
 class Saves:
@@ -185,9 +190,17 @@
 
 def launch(kernel, ident, vmem=(), loaded=(), hbm=(), outs=(), saved=(), hbm_outs=(), scratch=()):
     vmem, loaded, hbm, outs = dict(vmem), dict(loaded), dict(hbm), dict(outs)
+    starts = {n: a[1] if isinstance(a, tuple) else 0 for n, a in loaded.items()}
+    loaded = {n: a[0] if isinstance(a, tuple) else a for n, a in loaded.items()}
     saved, hbm_outs, scratch = dict(saved), dict(hbm_outs), dict(scratch)
     names = [*vmem, *loaded, *hbm, *outs, *saved, *hbm_outs]
-    buffers = [pltpu.VMEM(a.shape, a.dtype) for a in [*loaded.values(), *saved.values()]]
+    buffers = [
+        pltpu.VMEM(a.shape[:-1] + (a.shape[-1] - starts.get(n, 0),), a.dtype)
+        for n, a in [*loaded.items(), *saved.items()]
+    ]
+
+    def source(ref, start):
+        return ref.at[:, :, :, start:] if start else ref
 
     def run(*refs):
         r = types.SimpleNamespace(**dict(zip(names, refs)))
@@ -195,7 +208,8 @@
         rest, buffer_refs = rest[: len(scratch)], rest[len(scratch) : len(scratch) + len(buffers)]
         for name, ref in zip(scratch, rest):
             setattr(r, name, ref)
-        r.loads = Loads(list(loaded), [getattr(r, n) for n in loaded], buffer_refs[: len(loaded)], refs[-2])
+        sources = [source(getattr(r, n), starts[n]) for n in loaded]
+        r.loads = Loads(list(loaded), sources, buffer_refs[: len(loaded)], refs[-2])
         kept = buffer_refs[len(loaded) :]
         r.saves = Saves(list(saved), kept, [getattr(r, n) for n in saved], refs[-1])
         for name, ref in zip(saved, kept):
@@ -370,6 +384,10 @@
                 self.send_on(g - 1, k)
             self.ticked = at + 1
 
+    def pace(self, counts):
+        counts = iter(counts)
+        return lambda: self.tick(next(counts))
+
     def collect(self, g):
         for way in range(2):
 
@@ -502,21 +520,20 @@
     def scratch(stages, like, width):
         images, _, block = like.shape[:3]
         dma = pltpu.SemaphoreType.DMA
-        lead = (stages, images)
         return dict(
             part=pltpu.VMEM((images, 4, block, width), BF16),
-            first_in=pltpu.VMEM(lead + (2, 2, block, width // 2), BF16),
-            second_out=pltpu.VMEM(lead + (2, block, width // 2), BF16),
-            second_in=pltpu.VMEM(lead + (2, block, width // 2), BF16),
-            sum_send=dma(lead + (12,)),
-            sum_recv=dma(lead + (12,)),
+            first_in=pltpu.VMEM((images, 2, 2, block, width // 2), BF16),
+            second_out=pltpu.VMEM((images, 2, block, width // 2), BF16),
+            second_in=pltpu.VMEM((images, 2, block, width // 2), BF16),
+            sum_send=dma((stages, images, 12)),
+            sum_recv=dma((stages, images, 12)),
         )
 
     @staticmethod
     def stage(r, square, t):
         return [
             ImageSum(
-                square, r.part.at[i], r.first_in.at[t, i], r.second_out.at[t, i], r.second_in.at[t, i],
+                square, r.part.at[i], r.first_in.at[i], r.second_out.at[i], r.second_in.at[i],
                 r.sum_send.at[t, i], r.sum_recv.at[t, i],
             )
             for i in range(r.part.shape[0])
@@ -568,9 +585,11 @@
 def forward_kernel(r):
     loads = r.loads
     images, heads = r.own_self.shape[0], r.self_mixed.shape[3] // HDIM
-    loads.start("projected", "attention_out", "entry", "cross_query", "text", "cross_out", "feed_grad", "feed_expand")
+    loads.start("projected", "attention_out", "entry", "cross_query", "caption", "cross_out", "feed_grad", "feed_expand")
     stream = Stream(r.feed_shrink, r.tiles, r.tile_sem)
     stream.start()
+    text = Stream(r.weight_text, r.text_tiles, r.text_sem, True)
+    text.start()
     square = Square()
     place = lax.axis_index("img")
     peers = [lax.rem(place + j, 8) for j in range(1, 8)]
@@ -626,13 +645,12 @@
         jobs[0][i].sent()
         r.saves.save("second_normed", i)
         r.saves.save("own_self", i)
-        text = loads.got("text")
         queries = product(image_rows(r.second_normed, i), loads.got("cross_query")[...]).astype(BF16)
         put_image(r.queries, i, slice(None), queries)
 
         def one(h, carry):
             own, value = (tile_at(h + n * heads, HDIM) for n in range(2))
-            done = attend(image_rows(r.queries, i, own), text[i, :, own], text[i, :, value])
+            done = attend(image_rows(r.queries, i, own), r.text[i, :, own], r.text[i, :, value])
             put_image(r.cross_mixed, i, own, done)
             return carry
 
@@ -641,6 +659,10 @@
         jobs[1][i].start()
         r.saves.save("queries", i)
         r.saves.save("cross_mixed", i)
+
+    def text_tile(j, weight):
+        done = product(loads.got("caption")[...], weight).astype(BF16)
+        r.text[:, :, tile_at(j)] = done.reshape(r.text.shape[0], -1, TILE)
 
     def shrink_back(j, weight):
         feed_grad = loads.got("feed_grad")
@@ -678,11 +700,14 @@
     self_stage(2)
     first[1].forward()
     first[2].forward()
+    loads.got("caption")
+    text.run(0, text.count, text_tile)
+    r.saves.save("text")
     loads.got("feed_grad")
-    stream.run(0, stream.count // 2, shrink_back)
     gather_stage(0, r.second_normed)
     cross_stage(0)
     first[2].pass_on(r.second_normed.at[2])
+    stream.run(0, stream.count // 2, shrink_back)
     cross_stage(1)
     second[0].forward()
     cross_stage(2)
@@ -704,11 +729,15 @@
         copy.wait()
 
 
-def forward_rows(gains, projected, attention_out, entry, cross_query, text, cross_out, feed_grad, feed_expand, feed_shrink, caption):
+def forward_rows(
+    gains, projected, attention_out, entry, cross_query, weight_text, cross_out, feed_grad, feed_expand,
+    feed_shrink, caption,
+):
     lead = projected.shape[:3]
     width, ff, head_wide = attention_out.shape[1], feed_expand.shape[1], attention_out.shape[0]
     dma = pltpu.SemaphoreType.DMA
     tiles, tile_sem = Stream.scratch(feed_shrink)
+    text_tiles, text_sem = Stream.scratch(weight_text, True)
     own = struct((lead[0], lead[2], width), F32)
     return launch(
         forward_kernel,
@@ -716,9 +745,9 @@
         vmem=dict(gains=gains),
         loaded=dict(
             projected=projected, attention_out=attention_out, entry=entry, cross_query=cross_query,
-            text=text, cross_out=cross_out, feed_grad=feed_grad, feed_expand=feed_expand,
-        ),
-        hbm=dict(feed_shrink=feed_shrink, caption=caption),
+            caption=caption, cross_out=cross_out, feed_grad=feed_grad, feed_expand=feed_expand,
+        ),
+        hbm=dict(feed_shrink=feed_shrink, weight_text=weight_text),
         saved=dict(
             self_mixed=struct(lead + (head_wide,), BF16),
             second_normed=struct(lead + (width,), BF16),
@@ -729,10 +758,11 @@
             grad_hidden=struct(lead + (ff,), BF16),
             own_self=own,
             own_cross=own,
+            text=struct((lead[0], caption.shape[0] // lead[0], weight_text.shape[1]), BF16),
         ),
         hbm_outs=dict(captions=struct((8, caption.shape[0], caption.shape[1] // 8), BF16)),
         scratch=dict(
-            tiles=tiles, tile_sem=tile_sem, move_send=dma((7,)), move_recv=dma((7,)), stay_sem=dma((1,)),
+            tiles=tiles, tile_sem=tile_sem, text_tiles=text_tiles, text_sem=text_sem, move_send=dma((7,)), move_recv=dma((7,)), stay_sem=dma((1,)),
             **ImageSum.scratch(2, projected, width),
         ),
     )
@@ -753,39 +783,46 @@
     loads = r.loads
     images, heads = r.own_grad.shape[0], r.grad_queries.shape[3] // HDIM
     square = Square()
-    pieces = [(0, "active", c) for c in range(0, r.active.shape[3], WIDE)] + [(1, "grad_hidden", 0)]
+    pieces = [(0, "active", c) for c in range(0, r.active.shape[3], WIDE)] + [(1, "grad_hidden", 0), (1, "grad_hidden", WIDE)]
     sums = LineSum(r, (r.feed_grad, r.third_normed), pieces)
     sums.begin()
-    loads.start("grad_hidden", "active", "own_feed", "own_cross", "cross_out", "queries", "text", "cross_query", "own_self")
-    stream = Stream(r.feed_expand, r.tiles, r.tile_sem, passes=images)
+    loads.start("grad_hidden", "active", "own_feed", "own_cross", "cross_out", "queries", "text", "cross_query")
+    stream = Stream(r.feed_expand, r.tiles, r.tile_sem, passes=2)
     stream.start()
     greet(square.targets + sums.targets)
     third, second = [ImageSum.stage(r, square, t) for t in range(2)]
+
+    def text_copy(way):
+        peer = sums.twin if way == 2 else sums.place + (2 if way == 0 else -2)
+        return remote(r.grad_text, r.near.at[way], r.near_send.at[way], r.near_recv.at[way], {"img": peer})
+
     r.third_gain[...] = jnp.zeros_like(r.third_gain)
     r.second_gain[...] = jnp.zeros_like(r.second_gain)
     grad_hidden = loads.got("grad_hidden")
 
-    def expand_back(i):
-        rows = image_rows(grad_hidden, i)
+    def expand_back(turn, members):
+        rows = [image_rows(grad_hidden, i) for i in members]
 
         def one(j, weight):
             at = tile_at(lax.rem(j, stream.count))
-            put_image(r.part, i, at, product(rows, weight, NT).astype(BF16))
+            for i, row in zip(members, rows):
+                put_image(r.part, i, at, product(row, weight, NT).astype(BF16))
 
         for side in range(2):
-            first = i * stream.count + side * stream.count // 2
+            first = turn * stream.count + side * stream.count // 2
             stream.run(first, first + stream.count // 2, one)
-            third[i].start_side(side)
-
-    expand_back(0)
-    expand_back(1)
-    sums.tick(3)
-    third[0].forward()
-    expand_back(2)
-    third[1].forward()
-    sums.tick(2)
-    third[2].forward()
-    sums.tick(1)
+            for i in members:
+                third[i].start_side(side)
+            if turn:
+                tick()
+
+    tick = sums.pace(MIDDLE_TICKS)
+    expand_back(0, range(1))
+    tick()
+    expand_back(1, range(1, images))
+    for job in third:
+        job.forward()
+        tick()
 
     def third_stage(i):
         feed, source = loads.got("own_feed"), loads.got("own_cross")
@@ -823,7 +860,7 @@
 
     def second_stage(i):
         back_norm(
-            r, second[i], i, 1, lambda at: r.own_grad[i, at, :], loads.got("own_self"), r.second_gain,
+            r, second[i], i, 1, lambda at: r.own_grad[i, at, :], loads.targets["own_cross"], r.second_gain,
             r.self_grad, square,
         )
 
@@ -832,40 +869,62 @@
         if i:
             third[i - 1].pass_on(r.cross_grad.at[i - 1])
         third[i].gather(r.cross_grad.at[i])
-    sums.tick(2)
-    cross_stage(0)
-    third[2].pass_on(r.cross_grad.at[2])
-    sums.tick(2)
-    cross_stage(1)
-    second[0].forward()
-    sums.tick(2)
-    cross_stage(2)
-    second[1].forward()
-    sums.tick(1)
-    second[2].forward()
-    sums.tick(1)
+        tick()
+    late = pltpu.make_async_copy(r.own_self, loads.targets["own_cross"], r.late_sem.at[0])
+    late.start()
+    for i in range(images):
+        cross_stage(i)
+        tick()
+        if i == 0:
+            third[-1].pass_on(r.cross_grad.at[images - 1])
+        else:
+            second[i - 1].forward()
+        if i == images - 1:
+            text_copy(2).start()
+            for way in range(2):
+
+                @pl.when(sums.distance(1 - way) >= 1)
+                def _():
+                    text_copy(way).start()
+
+        tick()
+    second[-1].forward()
+    tick()
+    late.wait()
     for i in range(images):
         second_stage(i)
         r.saves.save("own_grad", i)
         if i:
             second[i - 1].pass_on(r.self_grad.at[i - 1])
         second[i].gather(r.self_grad.at[i])
-    sums.tick(3)
-    second[2].pass_on(r.self_grad.at[2])
+        tick()
+    second[-1].pass_on(r.self_grad.at[images - 1])
     sums.tick()
     for i in range(images):
         second[i].gathered()
         r.saves.save("self_grad", i)
     for g in range(sums.count):
         done = sums.collect(g)
-        if g + 1 < sums.count:
+        if g + 2 < sums.count:
             r.shrink_sum[g * WIDE : (g + 1) * WIDE, :] = done.astype(F32).T.astype(BF16)
         else:
-            r.expand_sum[...] = done
+            at = g + 2 - sums.count
+            r.expand_sum[:, at * WIDE : (at + 1) * WIDE] = done
     for job in second:
         job.sent()
     for job in third + second:
         job.spread_sent()
+    text_copy(2).wait()
+    for way in range(2):
+
+        @pl.when(sums.distance(1 - way) >= 1)
+        def _():
+            text_copy(way).wait_send()
+
+        @pl.when(sums.distance(way) >= 1)
+        def _():
+            text_copy(way).wait_recv()
+
     sums.settle()
 
 
@@ -873,7 +932,7 @@
     lead = feed_grad.shape[:3]
     width, head_wide, ff = feed_grad.shape[3], cross_out.shape[0], feed_expand.shape[1]
     share = width // 8
-    tiles, tile_sem = Stream.scratch(feed_expand)
+    tiles, tile_sem = Stream.scratch(feed_expand, depth=3)
     narrow = struct(lead + (width,), BF16)
     gain = struct((1, width), F32)
     return launch(
@@ -883,9 +942,8 @@
         loaded=dict(
             active=rows.active, grad_hidden=rows.grad_hidden, own_feed=own_feed, own_cross=rows.own_cross,
             cross_out=cross_out, queries=rows.queries, text=text, cross_query=cross_query,
-            own_self=rows.own_self,
-        ),
-        hbm=dict(feed_grad=feed_grad, third_normed=rows.third_normed, feed_expand=feed_expand),
+        ),
+        hbm=dict(own_self=rows.own_self, feed_grad=feed_grad, third_normed=rows.third_normed, feed_expand=feed_expand),
         saved=dict(
             cross_grad=narrow,
             self_grad=narrow,
@@ -897,11 +955,14 @@
             third_gain=gain,
             second_gain=gain,
             shrink_sum=struct((ff, share), BF16),
-            expand_sum=struct((share, WIDE), BF16),
-        ),
+            expand_sum=struct((share, 2 * WIDE), BF16),
+        ),
+        hbm_outs=dict(near=struct((3,) + text.shape, BF16)),
         scratch=dict(
+            late_sem=pltpu.SemaphoreType.DMA((1,)),
+            near_send=pltpu.SemaphoreType.DMA((3,)), near_recv=pltpu.SemaphoreType.DMA((3,)),
             tiles=tiles, tile_sem=tile_sem, mixed_grad=pltpu.VMEM((lead[1] * lead[2], head_wide), BF16),
-            **ImageSum.scratch(2, feed_grad, width), **LineSum.scratch(ff // WIDE + 1, 2, feed_grad),
+            **ImageSum.scratch(2, feed_grad, width), **LineSum.scratch(ff // WIDE + 2, 2, feed_grad),
         ),
     )
 
@@ -910,7 +971,7 @@
     loads = r.loads
     images, heads = r.own_out.shape[0], r.grad_projected.shape[3] // (3 * HDIM)
     square = Square()
-    pieces = [(0, "grad_hidden", c) for c in range(0, r.grad_hidden.shape[3], WIDE)]
+    pieces = [(0, "grad_hidden", c) for c in range(0, r.loads.targets["grad_hidden"].shape[3], WIDE)]
     pieces += [(1, "grad_queries", 0), (2, "cross_mixed", 0)]
     sums = LineSum(r, (r.third_normed, r.second_normed, r.cross_grad), pieces)
     sums.begin()
@@ -926,35 +987,44 @@
     def text_at(line):
         return r.texts.at[line * 2 + sums.core]
 
+    def behind(way, hop):
+        return sums.line - (hop if way == 0 else -hop)
+
     def text_along(way, hop):
-        ahead = 1 if way == 0 else -1
-        source = text_at(sums.line - ahead * hop) if hop else r.grad_text
+        source = r.near.at[way] if hop == 1 else text_at(behind(way, hop))
         return remote(
-            source, text_at(sums.line - ahead * hop), r.text_send.at[way, hop], r.text_recv.at[way, hop],
-            {"img": sums.place + 2 * ahead},
+            source, text_at(behind(way, hop)), r.text_send.at[way, hop], r.text_recv.at[way, hop],
+            {"img": sums.place + (2 if way == 0 else -2)},
         )
 
     def text_across(way, hop):
-        line = sums.line - (hop + 1) * (1 if way == 0 else -1)
+        line = behind(way, hop + 1)
+        source = r.near.at[way] if hop == 0 else text_at(line)
         return remote(
-            text_at(line), text_at(line), r.twin_send.at[way, hop], r.twin_recv.at[way, hop],
-            {"img": sums.twin},
+            source, text_at(line), r.twin_send.at[way, hop], r.twin_recv.at[way, hop], {"img": sums.twin}
         )
 
-    stay = pltpu.make_async_copy(r.grad_text, text_at(sums.line), r.stay_sem.at[0])
-    over = remote(r.grad_text, text_at(sums.line), r.twin_send.at[0, 3], r.twin_recv.at[0, 3], {"img": sums.twin})
+    def text_here(way):
+        return pltpu.make_async_copy(r.near.at[way], text_at(behind(way, 1)), r.stay_sem.at[way])
+
+    stay = [
+        pltpu.make_async_copy(r.text_own, text_at(sums.line), r.stay_sem.at[2]),
+        pltpu.make_async_copy(r.near.at[2], r.texts.at[sums.twin], r.stay_sem.at[3]),
+    ]
 
     def text_sends(way, hop):
         return (sums.distance(way) >= hop) & (sums.distance(1 - way) >= 1)
 
     def text_step(hop):
         for way in range(2):
-            if hop:
-
-                @pl.when(sums.distance(way) >= hop)
-                def _():
+
+            @pl.when(sums.distance(way) >= hop)
+            def _():
+                if hop > 1:
                     text_along(way, hop - 1).wait_recv()
-                    text_across(way, hop - 1).start()
+                else:
+                    text_here(way).start()
+                text_across(way, hop - 1).start()
 
             if hop < 3:
 
@@ -963,17 +1033,20 @@
                     text_along(way, hop).start()
 
     def text_settle():
-        stay.wait()
-        over.wait()
+        for copy in stay:
+            copy.wait()
         for way in range(2):
             for hop in range(3):
-
-                @pl.when(text_sends(way, hop))
-                def _():
-                    text_along(way, hop).wait_send()
+                if hop:
+
+                    @pl.when(text_sends(way, hop))
+                    def _():
+                        text_along(way, hop).wait_send()
 
                 @pl.when(sums.distance(way) >= hop + 1)
                 def _():
+                    if hop == 0:
+                        text_here(way).wait()
                     text_across(way, hop).wait()
 
     def self_stage(i):
@@ -981,6 +1054,7 @@
         r.mixed_grad[...] = product(
             image_rows(loads.got("self_grad"), i), loads.got("attention_out")[...], NT
         ).astype(BF16)
+        tick()
 
         def read(n, h):
             if n == 3:
@@ -991,9 +1065,11 @@
             put_image(r.grad_projected, i, tile_at(h + n * heads, HDIM), done)
 
         backward_heads(heads, read, write)
+        tick()
         project(r, i, image_rows(r.grad_projected, i), loads.got("weight_in"))
         jobs[i].start()
         r.saves.save("grad_projected", i)
+        tick()
 
     def entry_stage(i):
         job = jobs[i]
@@ -1014,34 +1090,30 @@
         done = product(grad.reshape(-1, grad.shape[2]), weight, NT)
         r.caption_part[:, tile_at(j)] = done.astype(BF16)
 
-    stay.start()
-    over.start()
-    sums.tick(3)
-    text_step(0)
-    sums.tick(1)
-    self_stage(0)
-    sums.tick(2)
-    self_stage(1)
-    jobs[0].forward()
-    sums.tick(3)
-    self_stage(2)
-    jobs[1].forward()
-    sums.tick(2)
-    jobs[2].forward()
+    for copy in stay:
+        copy.start()
+    tick = sums.pace(ENTRY_TICKS)
+    tick()
     text_step(1)
+    tick()
+    for i in range(images):
+        self_stage(i)
+        if i:
+            jobs[i - 1].forward()
+    text_step(2)
+    tick()
+    jobs[-1].forward()
+    tick()
     loads.got("grad_text")
-    text.run(0, text.count // 2, caption_tile)
-    sums.tick(3)
-    text.run(text.count // 2, text.count, caption_tile)
+    for quarter in range(4):
+        text.run(quarter * text.count // 4, (quarter + 1) * text.count // 4, caption_tile)
+        tick()
     r.saves.save("caption_part")
-    sums.tick(2)
-    entry_stage(0)
-    entry_stage(1)
-    sums.tick(2)
-    text_step(2)
-    entry_stage(2)
+    text_step(3)
+    for i in range(images):
+        entry_stage(i)
+        tick()
     sums.tick()
-    text_step(3)
     for g in range(sums.count - 2):
         r.expand_sum[:, g * WIDE : (g + 1) * WIDE] = sums.collect(g)
     r.query_sum[...] = sums.collect(sums.count - 2)
@@ -1052,12 +1124,13 @@
     sums.settle()
 
 
-def entry_rows(gains, mask, rows, back, projected, entry, attention_out, weight_in, weight_text, grad_hidden):
+def entry_rows(gains, mask, rows, back, projected, entry, attention_out, weight_in, weight_text):
     lead = projected.shape[:3]
     width = attention_out.shape[1]
     share = width // 8
     dma = pltpu.SemaphoreType.DMA
-    text_tiles, text_sem = Stream.scratch(weight_text)
+    text_tiles, text_sem = Stream.scratch(weight_text, depth=4)
+    left = rows.grad_hidden.shape[3] - 2 * WIDE
     text_rows = back.grad_text.shape[0] * back.grad_text.shape[1]
     gain = struct((1, width), F32)
     return launch(
@@ -1065,13 +1138,13 @@
         3,
         vmem=dict(gains=gains, mask=mask),
         loaded=dict(
-            grad_hidden=grad_hidden, self_grad=back.self_grad, attention_out=attention_out,
+            grad_hidden=(rows.grad_hidden, 2 * WIDE), self_grad=back.self_grad, attention_out=attention_out,
             projected=projected, weight_in=weight_in, own_grad=back.own_grad, entry=entry,
             grad_text=back.grad_text, grad_queries=back.grad_queries, cross_mixed=rows.cross_mixed,
         ),
         hbm=dict(
             third_normed=rows.third_normed, second_normed=rows.second_normed, cross_grad=back.cross_grad,
-            weight_text=weight_text,
+            weight_text=weight_text, near=back.near, text_own=back.grad_text,
         ),
         saved=dict(
             grad_projected=struct(projected.shape, BF16),
@@ -1081,7 +1154,7 @@
         outs=dict(
             first_gain=gain,
             embed_term=gain,
-            expand_sum=struct((share, grad_hidden.shape[3]), BF16),
+            expand_sum=struct((share, left), BF16),
             query_sum=struct((share, WIDE), BF16),
             cross_sum=struct((WIDE, share), BF16),
         ),
@@ -1090,9 +1163,9 @@
             text_tiles=text_tiles, text_sem=text_sem,
             mixed_grad=pltpu.VMEM((lead[1] * lead[2], attention_out.shape[0]), BF16),
             text_send=dma((2, 3)), text_recv=dma((2, 3)), twin_send=dma((2, 4)), twin_recv=dma((2, 4)),
-            stay_sem=dma((1,)),
+            stay_sem=dma((4,)),
             **ImageSum.scratch(1, projected, width),
-            **LineSum.scratch(grad_hidden.shape[3] // WIDE + 2, 3, rows.third_normed),
+            **LineSum.scratch(left // WIDE + 2, 3, rows.third_normed),
         ),
     )
 
@@ -1309,19 +1382,26 @@
     wide = [small_step(3 + j, device) for j, device in enumerate(targets[3:6])]
     loads.got("active")
     loads.got("own_cross")
-    shrink.run(0, shrink.count, mixed_tile)
+    shrink.run(0, shrink.count // 2, mixed_tile)
+    sums.tick(2)
+    shrink.run(shrink.count // 2, shrink.count, mixed_tile)
     flat_start(0)
     sums.tick(2)
     flat_forward(1)
-    lax.fori_loop(0, 4, text_product, 0)
+    lax.fori_loop(0, 2, text_product, 0)
     sums.tick(2)
-    lax.fori_loop(4, 8, text_product, 0)
-    sums.tick(2)
+    lax.fori_loop(2, 4, text_product, 0)
+    sums.tick(1)
+    lax.fori_loop(4, 5, text_product, 0)
+    sums.tick(1)
     flat_forward(0)
+    lax.fori_loop(5, 6, text_product, 0)
+    sums.tick(1)
+    lax.fori_loop(6, 8, text_product, 0)
+    sums.tick(1)
     flat_finish(1)
-    sums.tick(2)
+    sums.tick()
     move_finish()
-    sums.tick()
     flat_finish(0)
     for copy in wide:
         copy.wait()
@@ -1339,7 +1419,7 @@
     dma = pltpu.SemaphoreType.DMA
     block = (height, columns)
     lead = first_normed.shape[:3]
-    tiles, tile_sem = Stream.scratch(feed_shrink, True)
+    tiles, tile_sem = Stream.scratch(feed_shrink, True, 3)
     captions, texts = rows.captions, entry.texts
     return launch(
         line_kernel,
@@ -1413,9 +1493,10 @@
     return jax.nn.gelu(values_in, approximate=False)
 
 
-def layer_plain(images, own_rows, gains, own_entry, own_float, first_normed, projected, text_pairs, feed_grad, weights):
+def layer_plain(images, own_rows, gains, own_entry, own_float, first_normed, projected, feed_grad, weights):
     attention_out, cross_query, cross_out, feed_expand, feed_shrink, weight_in, weight_text, caption = weights
     queries, keys_in, values_in = plain_heads(projected, images, 3)
+    text_pairs = product(caption, weight_text).astype(BF16)
     text_keys, text_values = plain_heads(text_pairs, images, 2)
     self_mixed = plain_rows(per_head(attend)(queries, keys_in, values_in))
     own_self, second_normed = plain_step(
@@ -1470,7 +1551,7 @@
     )
 
 
-def layer_square(images, own_mask, gains, own_entry, first_normed, projected, text_pairs, feed_grad, weights):
+def layer_square(images, own_mask, gains, own_entry, first_normed, projected, feed_grad, weights):
     attention_out, cross_query, cross_out, feed_expand, feed_shrink, weight_in, weight_text, caption = weights
     width = first_normed.shape[1]
     spot = lax.axis_index("mp")
@@ -1478,17 +1559,15 @@
     def four(rows_in):
         return rows_in.reshape(images, 4, -1, rows_in.shape[-1])
 
-    text = text_pairs.reshape(images, -1, text_pairs.shape[1])
     four_grad, four_projected, four_normed = four(feed_grad), four(projected), four(first_normed)
     own_feed = lax.dynamic_index_in_dim(four_grad, spot, 1, False)
     rows = forward_rows(
-        gains, four_projected, attention_out, own_entry, cross_query, text, cross_out, four_grad,
+        gains, four_projected, attention_out, own_entry, cross_query, weight_text, cross_out, four_grad,
         feed_expand, feed_shrink, caption,
     )
-    back = middle_rows(gains, four_grad, own_feed, rows, text, cross_out, cross_query, feed_expand)
+    back = middle_rows(gains, four_grad, own_feed, rows, rows.text, cross_out, cross_query, feed_expand)
     entry = entry_rows(
         gains, own_mask, rows, back, four_projected, own_entry, attention_out, weight_in, weight_text,
-        rows.grad_hidden[:, :, :, WIDE:],
     )
     terms = [entry.first_gain, back.second_gain, back.third_gain, entry.embed_term]
     small = jnp.concatenate(terms + [jnp.zeros_like(entry.embed_term)] * 4, axis=0)
@@ -1552,18 +1631,17 @@
     weight_in = attention_in.transpose(1, 2, 0).reshape(-1, tokens.shape[1])
     projected = product(first_normed, weight_in, NT).astype(BF16)
     weight_text = cross_text.reshape(text_width, -1)
-    text_pairs = product(caption, weight_text).astype(BF16)
     feed_grad = jnp.where(mask_column, out_grad, jnp.zeros_like(out_grad))
     weights = (
         attention_out, cross_query, cross_out, feed_expand, feed_shrink, weight_in, weight_text, caption,
     )
     if square:
         done = layer_square(
-            images, own_float, norm_gains, own_entry, first_normed, projected, text_pairs, feed_grad, weights
+            images, own_float, norm_gains, own_entry, first_normed, projected, feed_grad, weights
         )
     else:
         done = layer_plain(
-            images, own_rows, norm_gains, own_entry, own_float, first_normed, projected, text_pairs,
+            images, own_rows, norm_gains, own_entry, own_float, first_normed, projected,
             feed_grad, weights,
         )
     mixed_out, tokens_grad, caption_grad, small_sums, self_in, *sums = done

time: 564 us -> 517 us (0.917)
  Pallas kernels: 478 us -> 442 us
  matrix products: 16 us -> 9.25 us
    pallas_call x4, Pallas kernels: 478 us -> 442 us  [launch(): pl.pallas_call(run, out_shape=[*outs.values(), *saved.values(), *hbm_outs...]
    dot_general x2 -> x1, matrix products: 16 us -> 9.25 us  [product(): return lax.dot_general(left, right, dims, preferred_element_type=F32)]
    unnamed x39 -> x37, local copies, waits for them, and re-layouts: 13.2 us -> 13 us
where the time goes in v5:
time: 517 us; the launch traced here: 507 us
  Pallas kernels  442 us (85%)
  local copies, waits for them, and re-layouts  33 us (6%)
  other arithmetic  21.4 us (4%)
  matrix products  9.25 us (2%)
    pallas_call x4, Pallas kernels, launch(): pl.pallas_call(run, out_shape=[*outs.values(), *saved.values(), *hbm_outs...  442 us
    unnamed x37, local copies, waits for them, and re-layouts  13 us

profile of v5, /device:TPU:0, one launch (start us, length us, event | category | flops | bytes accessed | tf_op | source)
XLA Modules:
  0.0 507.3 jit_solution(7041287294606513925)
XLA Ops:
  0.6 0.0 copy-start
  0.7 0.8 broadcast_compare_fusion
  1.5 0.1 gt.26
  1.6 0.6 convert_bitcast_fusion
  2.2 0.7 convert_element_type.45
  2.9 2.5 convert_select_fusion.1.refs_3_.refs_8_
  5.3 2.7 fusion.1
  8.0 0.0 copy-done
  8.0 1.6 multiply_reduce_fusion
  9.7 0.0 slice-done
  9.7 2.7 multiply_convert_fusion
  12.4 9.0 %copy.32 = bf16[3,512,2048]{2,1,0:T(8,128)(2,1)} copy(bf16[3,512,2048]{1,2,0:T(8,128)(2,1)} %bitcast.30) | data formatting | bytes 12582912 | tf_op jit(solution)/shard_map/transpose | solution.py:1631
  21.4 0.0 copy-done.2
  21.4 9.3 %convolution_convert_fusion = bf16[768,1536]{1,0:T(8,128)(2,1)} fusion(bf16[768,2048]{1,0:T(8,128)(2,1)S(1)} %copy-done.2, bf16[1536,2048]{1,0:T(8,128)(2,1)} %bitcast.31), kind=kOutput, calls=%fused_computation.5 | convolution fusion | flops 4833017856 | bytes 11796480 | tf_op jit(solution)/shard_map/dot_general | solution.py:33
  30.6 0.0 copy-done.1
  30.6 1.9 broadcast_select_fusion
  32.5 9.3 %copy.39 = bf16[512,8,2,512]{3,1,2,0:T(8,128)(2,1)} copy(bf16[512,8,2,512]{3,2,1,0:T(2,128)(2,1)} %bitcast.27) | data formatting | bytes 16777216
  41.9 121.8 %shard_map.220 = (bf16[3,4,64,512]{3,2,1,0:T(8,128)(2,1)}, bf16[3,4,64,2048]{3,2,1,0:T(8,128)(2,1)}, bf16[3,4,64,512]{3,2,1,0:T(8,128)(2,1)}, bf16[3,4,64,512]{3...) custom-call(f32[3,2048]{1,0:T(4,128)} %refs_0_.5, ...), custom_call_target="tpu_custom_call" | custom-call | flops 60000002048 | bytes 80000000 | tf_op jit(solution)/shard_map/pallas_call | solution.py:222
  163.7 2.1 dynamic-slice_bitcast_fusion.refs_3_
  165.8 136.7 %shard_map.221 = (f32[1,2048]{1,0:T(1,128)}, f32[1,2048]{1,0:T(1,128)}, bf16[2048,256]{1,0:T(8,128)(2,1)}, bf16[256,1024]{1,0:T(8,128)(2,1)}, bf16[3,4,64,2048]{...) custom-call(f32[3,2048]{1,0:T(4,128)} %refs_0_.5, ...), custom_call_target="tpu_custom_call" | custom-call | flops 60000002048 | bytes 80000000 | tf_op jit(solution)/shard_map/pallas_call | solution.py:222
  302.5 0.0 copy-done.15
  302.5 0.8 copy.34.refs_1_
  303.3 87.5 %shard_map.222 = (f32[1,2048]{1,0:T(1,128)}, f32[1,2048]{1,0:T(1,128)}, bf16[256,1024]{1,0:T(8,128)(2,1)}, bf16[256,512]{1,0:T(8,128)(2,1)}, bf16[512,256]{1,0:T...) custom-call(f32[3,2048]{1,0:T(4,128)} %refs_0_.5, ...), custom_call_target="tpu_custom_call" | custom-call | flops 60000002048 | bytes 80000000 | tf_op jit(solution)/shard_map/pallas_call | solution.py:222
  390.8 0.0 copy-start.11
  390.8 0.0 copy-start.12
  390.8 0.0 copy-start.13
  390.8 0.0 copy-start.14
  390.8 0.0 copy-done.7
  390.8 2.6 maximum_convert_fusion
  393.4 0.0 copy-done.11
  393.4 0.0 copy-done.12
  393.4 0.0 copy-done.13
  393.4 0.0 copy-done.14
  393.5 0.7 concatenate.10.refs_0_
  394.2 96.4 %shard_map.223 = (bf16[256,1536]{1,0:T(8,128)(2,1)}, bf16[512,256]{1,0:T(8,128)(2,1)}, f32[512,1024]{1,0:T(8,128)}, f32[8,2048]{1,0:T(8,128)}, bf16[192,2048]{1,...) custom-call(f32[8,2048]{1,0:T(8,128)} %concatenate.10.refs_0_, ...), custom_call_target="tpu_custom_call" | custom-call | flops 60000002048 | bytes 80000000 | tf_op jit(solution)/shard_map/pallas_call | solution.py:222
  490.6 1.4 copy.35
  492.0 1.6 copy.36
  493.6 4.1 reshape.111
  497.7 1.3 convert_element_type.51
  499.0 0.8 convert_element_type.52
  499.8 0.8 constant_dynamic-slice_fusion
  500.6 0.6 slice.11
  501.2 0.5 slice_bitcast_fusion
  501.7 0.9 convert_element_type.53
  502.5 0.8 convert_element_type.54
  503.4 1.5 convert_element_type.56
  504.8 0.9 copy.44
  505.7 1.1 copy.45
  (24 shorter events, 0.1 us)
Async XLA Ops:
  0.6 7.4 %copy-start = (bf16[768,2048]{1,0:T(8,128)(2,1)S(1)}, bf16[768,2048]{1,0:T(8,128)(2,1)}, u32[]{:S(2)}) copy-start(bf16[768,2048]{1,0:T(8,128)(2,1)} %param.13) | copy-start | bytes 9437188
  5.3 4.3 slice-start
  12.4 9.0 %copy-start.2 = (bf16[768,2048]{1,0:T(8,128)(2,1)S(1)}, bf16[768,2048]{1,0:T(8,128)(2,1)}, u32[]{:S(2)}) copy-start(bf16[768,2048]{1,0:T(8,128)(2,1)} %multiply_convert_fusion) | copy-start | bytes 9437188
  21.4 9.3 %copy-start.1 = (bf16[768,2048]{1,0:T(8,128)(2,1)S(1)}, bf16[768,2048]{1,0:T(8,128)(2,1)}, u32[]{:S(2)}) copy-start(bf16[768,2048]{1,0:T(8,128)(2,1)} %param.16) | copy-start | bytes 9437188
  165.8 136.7 %copy-start.15 = (f32[3,64,1]{1,2,0:T(1,128)S(1)}, f32[3,64,1]{1,2,0:T(1,128)}, u32[]{:S(2)}) copy-start(f32[3,64,1]{1,2,0:T(1,128)} %get-tuple-element.122) | copy-start | bytes 2308
  303.3 87.5 %copy-start.7 = (bf16[256,1024]{1,0:T(8,128)(2,1)S(1)}, bf16[256,1024]{1,0:T(8,128)(2,1)}, u32[]{:S(2)}) copy-start(bf16[256,1024]{1,0:T(8,128)(2,1)} %get-tuple-element.83) | copy-start | bytes 1572868
  390.8 2.7 copy-start.11
  390.8 2.7 copy-start.12
  390.8 2.7 copy-start.13
  390.8 2.7 copy-start.14
  492.0 5.7 %copy-start.6 = (bf16[384,1024]{1,0:T(8,128)(2,1)S(1)}, bf16[384,1024]{1,0:T(8,128)(2,1)}, u32[]{:S(2)}) copy-start(bf16[384,1024]{1,0:T(8,128)(2,1)} %get-tuple-element.76) | copy-start | bytes 2359300
  493.6 5.4 %copy-start.10 = (bf16[512,256]{1,0:T(8,128)(2,1)S(1)}, bf16[512,256]{1,0:T(8,128)(2,1)}, u32[]{:S(2)}) copy-start(bf16[512,256]{1,0:T(8,128)(2,1)} %get-tuple-element.79) | copy-start | bytes 786436
  493.6 8.1 %copy-start.9 = (bf16[256,512]{1,0:T(8,128)(2,1)S(1)}, bf16[256,512]{1,0:T(8,128)(2,1)}, u32[]{:S(2)}) copy-start(bf16[256,512]{1,0:T(8,128)(2,1)} %get-tuple-element.80) | copy-start | bytes 786436
  493.6 8.9 %copy-start.8 = (bf16[512,256]{1,0:T(8,128)(2,1)S(1)}, bf16[512,256]{1,0:T(8,128)(2,1)}, u32[]{:S(2)}) copy-start(bf16[512,256]{1,0:T(8,128)(2,1)} %get-tuple-element.82) | copy-start | bytes 786436
  497.7 5.7 %copy-start.4 = (bf16[2048,256]{1,0:T(8,128)(2,1)S(1)}, bf16[2048,256]{1,0:T(8,128)(2,1)}, u32[]{:S(2)}) copy-start(bf16[2048,256]{1,0:T(8,128)(2,1)} %get-tuple-element.85) | copy-start | bytes 3145732
  499.0 5.9 %copy-start.5 = (bf16[192,2048]{1,0:T(8,128)(2,1)S(1)}, bf16[192,2048]{1,0:T(8,128)(2,1)}, u32[]{:S(2)}) copy-start(bf16[192,2048]{1,0:T(8,128)(2,1)} %get-tuple-element.136) | copy-start | bytes 2359300
  501.7 4.1 copy-start.3

commit v6 on v5

--- a/solution.py
+++ b/solution.py
@@ -22,7 +22,7 @@
 TILE = 256
 
 MIDDLE_TICKS = (1, 1, 1, 5, 0, 1, 0, 4, 2, 0, 2, 0, 0, 4, 1, 2, 0, 2, 1)
-ENTRY_TICKS = (4, 0, 0, 0, 0, 0, 4, 4, 0, 2, 1, 2, 1, 1, 0, 0, 0, 0, 0, 1)
+ENTRY_TICKS = (3, 0, 0, 0, 1, 0, 3, 4, 0, 1, 0, 2, 0, 1, 0, 0, 2, 1, 0, 1)
 
 NN = (((1,), (0,)), ((), ()))
 NT = (((1,), (1,)), ((), ()))
@@ -701,19 +701,23 @@
     first[1].forward()
     first[2].forward()
     loads.got("caption")
-    text.run(0, text.count, text_tile)
-    r.saves.save("text")
+    text.run(0, text.count // 2, text_tile)
     loads.got("feed_grad")
     gather_stage(0, r.second_normed)
+    text.run(text.count // 2, text.count, text_tile)
+    r.saves.save("text")
+    quarter = stream.count // 4
     cross_stage(0)
     first[2].pass_on(r.second_normed.at[2])
-    stream.run(0, stream.count // 2, shrink_back)
+    stream.run(0, quarter, shrink_back)
     cross_stage(1)
+    stream.run(quarter, 2 * quarter, shrink_back)
     second[0].forward()
     cross_stage(2)
     second[1].forward()
+    stream.run(2 * quarter, 3 * quarter, shrink_back)
     second[2].forward()
-    stream.run(stream.count // 2, stream.count, shrink_back)
+    stream.run(3 * quarter, stream.count, shrink_back)
     gather_stage(1, r.third_normed)
     feed_stage(0)
     second[2].pass_on(r.third_normed.at[2])
@@ -786,7 +790,9 @@
     pieces = [(0, "active", c) for c in range(0, r.active.shape[3], WIDE)] + [(1, "grad_hidden", 0), (1, "grad_hidden", WIDE)]
     sums = LineSum(r, (r.feed_grad, r.third_normed), pieces)
     sums.begin()
-    loads.start("grad_hidden", "active", "own_feed", "own_cross", "cross_out", "queries", "text", "cross_query")
+    own_feed = pltpu.make_async_copy(r.feed_grad.at[:, square.spot], r.own_feed, r.late_sem.at[1])
+    own_feed.start()
+    loads.start("grad_hidden", "active", "own_cross", "cross_out", "queries", "text", "cross_query")
     stream = Stream(r.feed_expand, r.tiles, r.tile_sem, passes=2)
     stream.start()
     greet(square.targets + sums.targets)
@@ -825,9 +831,9 @@
         tick()
 
     def third_stage(i):
-        feed, source = loads.got("own_feed"), loads.got("own_cross")
+        source = loads.got("own_cross")
         back_norm(
-            r, third[i], i, 2, lambda at: feed[i, at, :].astype(F32), source, r.third_gain, r.cross_grad, square
+            r, third[i], i, 2, lambda at: r.own_feed[i, at, :].astype(F32), source, r.third_gain, r.cross_grad, square
         )
 
     def cross_stage(i):
@@ -864,6 +870,7 @@
             r.self_grad, square,
         )
 
+    own_feed.wait()
     for i in range(images):
         third_stage(i)
         if i:
@@ -928,7 +935,7 @@
     sums.settle()
 
 
-def middle_rows(gains, feed_grad, own_feed, rows, text, cross_out, cross_query, feed_expand):
+def middle_rows(gains, feed_grad, rows, text, cross_out, cross_query, feed_expand):
     lead = feed_grad.shape[:3]
     width, head_wide, ff = feed_grad.shape[3], cross_out.shape[0], feed_expand.shape[1]
     share = width // 8
@@ -940,7 +947,7 @@
         2,
         vmem=dict(gains=gains),
         loaded=dict(
-            active=rows.active, grad_hidden=rows.grad_hidden, own_feed=own_feed, own_cross=rows.own_cross,
+            active=rows.active, grad_hidden=rows.grad_hidden, own_cross=rows.own_cross,
             cross_out=cross_out, queries=rows.queries, text=text, cross_query=cross_query,
         ),
         hbm=dict(own_self=rows.own_self, feed_grad=feed_grad, third_normed=rows.third_normed, feed_expand=feed_expand),
@@ -959,7 +966,7 @@
         ),
         hbm_outs=dict(near=struct((3,) + text.shape, BF16)),
         scratch=dict(
-            late_sem=pltpu.SemaphoreType.DMA((1,)),
+            late_sem=pltpu.SemaphoreType.DMA((2,)), own_feed=pltpu.VMEM((lead[0], lead[2], width), BF16),
             near_send=pltpu.SemaphoreType.DMA((3,)), near_recv=pltpu.SemaphoreType.DMA((3,)),
             tiles=tiles, tile_sem=tile_sem, mixed_grad=pltpu.VMEM((lead[1] * lead[2], head_wide), BF16),
             **ImageSum.scratch(2, feed_grad, width), **LineSum.scratch(ff // WIDE + 2, 2, feed_grad),
@@ -1004,13 +1011,15 @@
             source, text_at(line), r.twin_send.at[way, hop], r.twin_recv.at[way, hop], {"img": sums.twin}
         )
 
-    def text_here(way):
-        return pltpu.make_async_copy(r.near.at[way], text_at(behind(way, 1)), r.stay_sem.at[way])
-
-    stay = [
-        pltpu.make_async_copy(r.text_own, text_at(sums.line), r.stay_sem.at[2]),
-        pltpu.make_async_copy(r.near.at[2], r.texts.at[sums.twin], r.stay_sem.at[3]),
-    ]
+    def text_in(way):
+        return pltpu.make_async_copy(r.near.at[way], r.bounce.at[way], r.in_sem.at[way])
+
+    def text_out(way):
+        target = r.texts.at[sums.twin] if way == 2 else text_at(behind(way, 1))
+        return pltpu.make_async_copy(r.bounce.at[way], target, r.stay_sem.at[way])
+
+    def text_own():
+        return pltpu.make_async_copy(loads.targets["grad_text"], text_at(sums.line), r.stay_sem.at[3])
 
     def text_sends(way, hop):
         return (sums.distance(way) >= hop) & (sums.distance(1 - way) >= 1)
@@ -1023,7 +1032,7 @@
                 if hop > 1:
                     text_along(way, hop - 1).wait_recv()
                 else:
-                    text_here(way).start()
+                    text_in(way).start()
                 text_across(way, hop - 1).start()
 
             if hop < 3:
@@ -1033,8 +1042,8 @@
                     text_along(way, hop).start()
 
     def text_settle():
-        for copy in stay:
-            copy.wait()
+        text_out(2).wait()
+        text_own().wait()
         for way in range(2):
             for hop in range(3):
                 if hop:
@@ -1046,7 +1055,7 @@
                 @pl.when(sums.distance(way) >= hop + 1)
                 def _():
                     if hop == 0:
-                        text_here(way).wait()
+                        text_out(way).wait()
                     text_across(way, hop).wait()
 
     def self_stage(i):
@@ -1090,26 +1099,38 @@
         done = product(grad.reshape(-1, grad.shape[2]), weight, NT)
         r.caption_part[:, tile_at(j)] = done.astype(BF16)
 
-    for copy in stay:
-        copy.start()
+    text_in(2).start()
     tick = sums.pace(ENTRY_TICKS)
+    text_step(1)
     tick()
-    text_step(1)
     tick()
     for i in range(images):
         self_stage(i)
         if i:
             jobs[i - 1].forward()
-    text_step(2)
+        if i == 0:
+            text_in(2).wait()
+            text_out(2).start()
+            for way in range(2):
+
+                @pl.when(sums.distance(way) >= 1)
+                def _():
+                    text_in(way).wait()
+                    text_out(way).start()
+
+        if i == 1:
+            text_step(2)
     tick()
     jobs[-1].forward()
     tick()
     loads.got("grad_text")
+    text_own().start()
     for quarter in range(4):
         text.run(quarter * text.count // 4, (quarter + 1) * text.count // 4, caption_tile)
         tick()
+        if quarter == 1:
+            text_step(3)
     r.saves.save("caption_part")
-    text_step(3)
     for i in range(images):
         entry_stage(i)
         tick()
@@ -1144,7 +1165,7 @@
         ),
         hbm=dict(
             third_normed=rows.third_normed, second_normed=rows.second_normed, cross_grad=back.cross_grad,
-            weight_text=weight_text, near=back.near, text_own=back.grad_text,
+            weight_text=weight_text, near=back.near,
         ),
         saved=dict(
             grad_projected=struct(projected.shape, BF16),
@@ -1163,7 +1184,7 @@
             text_tiles=text_tiles, text_sem=text_sem,
             mixed_grad=pltpu.VMEM((lead[1] * lead[2], attention_out.shape[0]), BF16),
             text_send=dma((2, 3)), text_recv=dma((2, 3)), twin_send=dma((2, 4)), twin_recv=dma((2, 4)),
-            stay_sem=dma((4,)),
+            stay_sem=dma((4,)), in_sem=dma((3,)), bounce=pltpu.VMEM(back.near.shape, BF16),
             **ImageSum.scratch(1, projected, width),
             **LineSum.scratch(left // WIDE + 2, 3, rows.third_normed),
         ),
@@ -1560,12 +1581,11 @@
         return rows_in.reshape(images, 4, -1, rows_in.shape[-1])
 
     four_grad, four_projected, four_normed = four(feed_grad), four(projected), four(first_normed)
-    own_feed = lax.dynamic_index_in_dim(four_grad, spot, 1, False)
     rows = forward_rows(
         gains, four_projected, attention_out, own_entry, cross_query, weight_text, cross_out, four_grad,
         feed_expand, feed_shrink, caption,
     )
-    back = middle_rows(gains, four_grad, own_feed, rows, rows.text, cross_out, cross_query, feed_expand)
+    back = middle_rows(gains, four_grad, rows, rows.text, cross_out, cross_query, feed_expand)
     entry = entry_rows(
         gains, own_mask, rows, back, four_projected, own_entry, attention_out, weight_in, weight_text,
     )

time: 517 us -> 496 us (0.959)
  the two profiles are of different devices: /device:TPU:0 before, /device:TPU:11 now
where the time goes in v6:
time: 496 us; the launch traced here: 486 us
  Pallas kernels  423 us (85%)
  local copies, waits for them, and re-layouts  30.7 us (6%)
  other arithmetic  21.7 us (4%)
  matrix products  9.19 us (2%)
    pallas_call x4, Pallas kernels, launch(): pl.pallas_call(run, out_shape=[*outs.values(), *saved.values(), *hbm_outs...  423 us
    unnamed x31, local copies, waits for them, and re-layouts  13 us

profile of v6, /device:TPU:11, one launch (start us, length us, event | category | flops | bytes accessed | tf_op | source)
XLA Modules:
  0.0 486.2 jit_solution(11527405099729476030)
XLA Ops:
  0.6 0.0 copy-start
  0.7 0.8 broadcast_compare_fusion
  1.5 0.8 convert_element_type.45
  2.3 2.7 fusion.1
  5.0 0.0 copy-done
  5.0 1.6 multiply_reduce_fusion
  6.6 0.0 slice-done
  6.6 2.7 multiply_convert_fusion
  9.3 8.8 %copy.32 = bf16[3,512,2048]{2,1,0:T(8,128)(2,1)} copy(bf16[3,512,2048]{1,2,0:T(8,128)(2,1)} %bitcast.28) | data formatting | bytes 12582912 | tf_op jit(solution)/shard_map/transpose | solution.py:1651
  18.2 9.2 %convolution_convert_fusion = bf16[768,1536]{1,0:T(8,128)(2,1)} fusion(bf16[768,2048]{1,0:T(8,128)(2,1)} %multiply_convert_fusion, bf16[1536,2048]{1,0:T(8,128)(2,1)} %bitcast.29), kind=kOutput, calls=%fused_computation.5 | convolution fusion | flops 4833017856 | bytes 11796480 | tf_op jit(solution)/shard_map/dot_general | solution.py:33
  27.4 0.1 gt.26
  27.5 1.3 convert_select_fusion.1.refs_3_.refs_8_
  28.8 3.8 broadcast_select_fusion
  32.6 9.3 %copy.39 = bf16[512,8,2,512]{3,1,2,0:T(8,128)(2,1)} copy(bf16[512,8,2,512]{3,2,1,0:T(2,128)(2,1)} %bitcast.25) | data formatting | bytes 16777216
  41.9 118.4 %shard_map.220 = (bf16[3,4,64,512]{3,2,1,0:T(8,128)(2,1)}, bf16[3,4,64,2048]{3,2,1,0:T(8,128)(2,1)}, bf16[3,4,64,512]{3,2,1,0:T(8,128)(2,1)}, bf16[3,4,64,512]{3...) custom-call(f32[3,2048]{1,0:T(4,128)} %refs_0_.5, ...), custom_call_target="tpu_custom_call" | custom-call | flops 60000002048 | bytes 80000000 | tf_op jit(solution)/shard_map/pallas_call | solution.py:222
  160.3 140.0 %shard_map.221 = (f32[1,2048]{1,0:T(1,128)}, f32[1,2048]{1,0:T(1,128)}, bf16[2048,256]{1,0:T(8,128)(2,1)}, bf16[256,1024]{1,0:T(8,128)(2,1)}, bf16[3,4,64,2048]{...) custom-call(f32[3,2048]{1,0:T(4,128)} %refs_0_.5, ...), custom_call_target="tpu_custom_call" | custom-call | flops 60000002048 | bytes 80000000 | tf_op jit(solution)/shard_map/pallas_call | solution.py:222
  300.2 0.8 copy.34.refs_1_
  301.0 82.2 %shard_map.222 = (f32[1,2048]{1,0:T(1,128)}, f32[1,2048]{1,0:T(1,128)}, bf16[256,1024]{1,0:T(8,128)(2,1)}, bf16[256,512]{1,0:T(8,128)(2,1)}, bf16[512,256]{1,0:T...) custom-call(f32[3,2048]{1,0:T(4,128)} %refs_0_.5, ...), custom_call_target="tpu_custom_call" | custom-call | flops 60000002048 | bytes 80000000 | tf_op jit(solution)/shard_map/pallas_call | solution.py:222
  383.2 0.0 copy-start.9
  383.2 0.0 copy-start.10
  383.2 0.0 copy-start.11
  383.2 0.0 copy-start.12
  383.2 0.0 copy-done.5
  383.2 2.6 maximum_convert_fusion
  385.8 0.0 copy-done.9
  385.8 0.0 copy-done.10
  385.8 0.0 copy-done.11
  385.8 0.0 copy-done.12
  385.9 0.7 concatenate.10.refs_0_
  386.5 82.9 %shard_map.223 = (bf16[256,1536]{1,0:T(8,128)(2,1)}, bf16[512,256]{1,0:T(8,128)(2,1)}, f32[512,1024]{1,0:T(8,128)}, f32[8,2048]{1,0:T(8,128)}, bf16[192,2048]{1,...) custom-call(f32[8,2048]{1,0:T(8,128)} %concatenate.10.refs_0_, ...), custom_call_target="tpu_custom_call" | custom-call | flops 60000002048 | bytes 80000000 | tf_op jit(solution)/shard_map/pallas_call | solution.py:222
  469.4 1.4 copy.35
  470.8 0.0 copy-start.4
  470.8 1.6 copy.36
  472.4 4.1 reshape.111
  476.5 0.0 copy-done.4
  476.5 1.3 convert_element_type.51
  477.8 0.0 copy-done.8
  477.8 0.8 convert_element_type.52
  478.7 0.8 constant_dynamic-slice_fusion
  479.4 0.6 slice.11
  480.0 0.5 slice_bitcast_fusion
  480.5 0.0 copy-done.7
  480.5 0.9 convert_element_type.53
  481.4 0.8 convert_element_type.54
  482.2 1.5 convert_element_type.56
  483.7 0.9 copy.44
  484.6 0.0 copy-done.1
  484.6 1.1 copy.45
  (17 shorter events, 0.1 us)
Async XLA Ops:
  0.6 4.3 copy-start
  2.3 4.3 slice-start
  301.0 82.2 %copy-start.5 = (bf16[256,1024]{1,0:T(8,128)(2,1)S(1)}, bf16[256,1024]{1,0:T(8,128)(2,1)}, u32[]{:S(2)}) copy-start(bf16[256,1024]{1,0:T(8,128)(2,1)} %get-tuple-element.83) | copy-start | bytes 1572868
  383.2 2.7 copy-start.9
  383.2 2.7 copy-start.10
  383.2 2.7 copy-start.11
  383.2 2.7 copy-start.12
  470.8 5.7 %copy-start.4 = (bf16[384,1024]{1,0:T(8,128)(2,1)S(1)}, bf16[384,1024]{1,0:T(8,128)(2,1)}, u32[]{:S(2)}) copy-start(bf16[384,1024]{1,0:T(8,128)(2,1)} %get-tuple-element.76) | copy-start | bytes 2359300
  472.4 5.4 %copy-start.8 = (bf16[512,256]{1,0:T(8,128)(2,1)S(1)}, bf16[512,256]{1,0:T(8,128)(2,1)}, u32[]{:S(2)}) copy-start(bf16[512,256]{1,0:T(8,128)(2,1)} %get-tuple-element.79) | copy-start | bytes 786436
  472.4 8.1 %copy-start.7 = (bf16[256,512]{1,0:T(8,128)(2,1)S(1)}, bf16[256,512]{1,0:T(8,128)(2,1)}, u32[]{:S(2)}) copy-start(bf16[256,512]{1,0:T(8,128)(2,1)} %get-tuple-element.80) | copy-start | bytes 786436
  472.4 8.9 %copy-start.6 = (bf16[512,256]{1,0:T(8,128)(2,1)S(1)}, bf16[512,256]{1,0:T(8,128)(2,1)}, u32[]{:S(2)}) copy-start(bf16[512,256]{1,0:T(8,128)(2,1)} %get-tuple-element.82) | copy-start | bytes 786436
  476.5 5.7 %copy-start.2 = (bf16[2048,256]{1,0:T(8,128)(2,1)S(1)}, bf16[2048,256]{1,0:T(8,128)(2,1)}, u32[]{:S(2)}) copy-start(bf16[2048,256]{1,0:T(8,128)(2,1)} %get-tuple-element.85) | copy-start | bytes 3145732
  477.8 5.9 %copy-start.3 = (bf16[192,2048]{1,0:T(8,128)(2,1)S(1)}, bf16[192,2048]{1,0:T(8,128)(2,1)}, u32[]{:S(2)}) copy-start(bf16[192,2048]{1,0:T(8,128)(2,1)} %get-tuple-element.136) | copy-start | bytes 2359300
  480.5 4.1 copy-start.1
